TPU v7x, 32 devices: a whole 2x2x4 slice. The times are simulated.
32 devices in a mesh: seq: 16 (over z, y, x), mp: 2 (over core).
Axes of the slice: x: 2, y: 2, z: 4, core: 2. Of those that a mesh axis runs over, the one named last changes fastest.
Arguments:
- queries: bfloat16 [4096, 2048], P('seq', 'mp'), may hold values from -6 to 6
- keys: bfloat16 [4096, 2048], P('seq', 'mp'), may hold values from -6 to 6
- values: bfloat16 [4096, 2048], P('seq', 'mp'), may hold values from -20 to 20
- norm_gain: float32 [2048], P('mp'), may hold values from 0.1 to 1.9
- w_out: bfloat16 [2048, 4096], P('seq', 'mp'), may hold values from -0.125 to 0.125
Outputs:
- projected: bfloat16 [4096, 4096], P('seq', 'mp')
All inputs are finite; a program needn't handle non-finite values.
Results may differ from a plain program's by a relative error of at most 0.0057.
Values may be sent and summed in bfloat16 or wider, within the bound.
No kernel may reach another device: no remote copies, remote signals or barrier semaphores. Data moves between devices by JAX's collectives and lax.ppermute only.
A program may use at most 192 MiB of HBM per device.

v0:
```python
import jax
import jax.numpy as jnp
from jax import lax
from jax.sharding import PartitionSpec as P

HD = 128


def entering(x, axis, combine, identity):
    count, index = (lax.axis_size(axis), lax.axis_index(axis))
    everything = lax.all_gather(x, axis)
    start = jnp.broadcast_to(jnp.asarray(identity, x.dtype), x.shape)

    def lap(k, before):
        reached = k < index
        new = combine(before, everything[k])
        return jnp.where(reached, new, before)

    return lax.fori_loop(0, count, lap, start)


def add_states(earlier, later):
    return earlier + later


def per_device(queries, keys, values, norm_gain, w_out):
    rows = queries.shape[0]
    heads_here = queries.shape[1] // HD
    q_three = queries.reshape(rows, heads_here, HD)
    k_three = keys.reshape(rows, heads_here, HD)
    v_three = values.reshape(rows, heads_here, HD)
    feat_q = jax.nn.silu(q_three.astype(jnp.float32)).astype(jnp.bfloat16)
    feat_k = jax.nn.silu(k_three.astype(jnp.float32)).astype(jnp.bfloat16)
    own_state = jnp.einsum("thd,the->hde", feat_k, v_three, preferred_element_type=jnp.float32)
    prefix = entering(own_state, "seq", add_states, jnp.zeros_like(own_state))
    causal = jnp.arange(rows)[:, None] >= jnp.arange(rows)[None, :]

    def one_head(operands):
        head_q, head_k, head_v = operands
        head_scores = jnp.dot(head_q, head_k.T, preferred_element_type=jnp.float32)
        head_scores = jnp.where(causal, head_scores, 0.0).astype(jnp.bfloat16)
        return jnp.dot(head_scores, head_v, preferred_element_type=jnp.float32)

    per_head = lax.map(
        one_head, (feat_q.transpose(1, 0, 2), feat_k.transpose(1, 0, 2), v_three.transpose(1, 0, 2))
    )
    intra = per_head.transpose(1, 0, 2)
    inter = jnp.einsum(
        "thd,hde->the", feat_q.astype(jnp.float32), prefix, precision=lax.Precision.HIGHEST
    )
    mixed = intra + inter
    scale = lax.rsqrt(jnp.mean(mixed * mixed, axis=-1, keepdims=True) + 1e-06)
    gain = norm_gain.reshape(heads_here, HD)
    normed = (mixed * scale * gain[None]).astype(jnp.bfloat16).reshape(rows, heads_here * HD)
    all_heads = lax.all_gather(normed, "mp", axis=1, tiled=True)
    late_weight = lax.all_gather(w_out, "seq", axis=0, tiled=True)
    result = jnp.dot(all_heads, late_weight, preferred_element_type=jnp.float32)
    return result.astype(jnp.bfloat16)


def solution(mesh):
    in_specs = (P("seq", "mp"), P("seq", "mp"), P("seq", "mp"), P("mp"), P("seq", "mp"))
    out_specs = P("seq", "mp")
    return jax.shard_map(
        per_device, mesh=mesh, in_specs=in_specs, out_specs=out_specs, check_vma=False
    )
```

profile of v0, /device:TPU:0, one launch (start us, length us, event | category | flops | bytes accessed | tf_op | source)
XLA Modules:
  0.0 262.2 jit_solution(13440799125488620299)
XLA Ops:
  6.5 1.3 copy.21
  7.8 1.2 copy.20
  9.1 1.2 fusion.31
  12.0 8.3 %while.25 = (s32[]{:T(128)}, f32[8,256,128]{1,2,0:T(8,128)}, bf16[8,256,128]{1,2,0:T(8,128)(2,1)S(1)}, bf16[8,256,128]{1,2,0:T(8,128)(2,1)S(1)}, bf16[8,256,128]{1,2,0:T(8,128)(2,1)S(1)}, /*index=5*/s32[]{:T(128)}) while((s32[]{:T(128)}, f32[8,256,128]{1,2,0:T(8,128)}, bf16[8,256,128]{1,2,0:T(8,128)(2,1)S(1)}, ...), condition=%wide.region_1.2_spmd.clone, body=%wide.region_0.1_spmd.clone.sunk | while | flops 33751040 | bytes 329805 | solution.py:44
  20.4 105.7 %all-gather.9.cloned.1.call-done = f32[128,128,128]{2,1,0:T(8,128)} async-done(((f32[8,128,128]{2,1,0:T(8,128)}), f32[128,128,128]{2,1,0:T(8,128)}) %all-gather.9.cloned.1.call-update) | async-done | bytes 8388624 | tf_op jit(solution)/shard_map/all_gather | solution.py:11
  126.0 20.1 %while.26 = (s32[]{:T(128)}, f32[8,128,128]{2,1,0:T(8,128)S(1)}, s32[]{:T(128)}, f32[16,8,128,128]{3,2,1,0:T(8,128)}, s32[]{:T(128)}, /*index=5*/s32[]{:T(128)}) while((s32[]{:T(128)}, f32[8,128,128]{2,1,0:T(8,128)S(1)}, s32[]{:T(128)}, f32[16,8,128,128]{3,2,1,0:T(8,128)}, s32[]{:T(128)}, /*index=5*/s32[]{:T(128)}) %tuple.63), condition=%wide.region_3.4_spmd.clone, body=%wide.region_2.3_spmd.clone.sunk | while | flops 393220 | bytes 1572965 | solution.py:19
  127.3 1.2 add_select_fusion.2
  128.5 1.2 add_select_fusion.2
  129.8 1.2 add_select_fusion.2
  131.0 1.2 add_select_fusion.2
  132.3 1.2 add_select_fusion.2
  133.5 1.2 add_select_fusion.2
  134.8 1.3 add_select_fusion.2
  136.1 1.3 add_select_fusion.2
  137.4 1.2 add_select_fusion.2
  138.7 1.2 add_select_fusion.2
  139.9 1.2 add_select_fusion.2
  141.2 1.2 add_select_fusion.2
  142.4 1.2 add_select_fusion.2
  143.7 1.2 add_select_fusion.2
  146.2 2.1 multiply_reduce_fusion
  149.3 90.5 %all-gather.7.cloned.1.call-done = bf16[2048,2048]{1,0:T(8,128)(2,1)} async-done(((bf16[128,2048]{1,0:T(8,128)(2,1)}), bf16[2048,2048]{1,0:T(8,128)(2,1)}) %all-gather.7.cloned.1.call-update) | async-done | bytes 8388624 | tf_op jit(solution)/shard_map/all_gather | solution.py:56
  239.9 8.8 %all-gather.5.cloned.1.call-done = bf16[256,2048]{0,1:T(8,128)(2,1)} async-done(((bf16[256,1024]{0,1:T(8,128)(2,1)}), bf16[256,2048]{0,1:T(8,128)(2,1)}) %all-gather.5.cloned.1.call-update) | async-done | bytes 1048592 | tf_op jit(solution)/shard_map/all_gather | solution.py:55
  248.7 7.0 %convolution_convert_fusion = bf16[256,2048]{1,0:T(8,128)(2,1)} fusion(bf16[256,2048]{0,1:T(8,128)(2,1)} %all-gather.5.cloned.1.call-done, bf16[2048,2048]{1,0:T(8,128)(2,1)} %all-gather.7.cloned.1.call-done), kind=kOutput, calls=%fused_computation.17 | convolution fusion | flops 2148007936 | bytes 10485760 | tf_op jit(solution)/shard_map/dot_general | solution.py:57
  (27 shorter events, 13.4 us)
Async XLA Ops:
  6.5 4.6 %copy-start = (bf16[256,1024]{1,0:T(8,128)(2,1)S(1)}, bf16[256,1024]{1,0:T(8,128)(2,1)}, u32[]{:S(2)}) copy-start(bf16[256,1024]{1,0:T(8,128)(2,1)} %param.9) | copy-start | bytes 1572868
  6.5 119.5 %all-gather.9.cloned.1.call-start = ((), (), s32[]{:S(2)}) async-start(), calls=%async_computation.2 | async-start | bytes 8912896 | tf_op jit(solution)/shard_map/all_gather | solution.py:11
  10.3 229.5 %all-gather.7.cloned.1.call-start = ((), (), s32[]{:S(2)}) async-start(), calls=%async_computation.1 | async-start | bytes 8912896 | tf_op jit(solution)/shard_map/all_gather | solution.py:56
  11.1 237.6 %all-gather.5.cloned.1.call-start = ((), (), s32[]{:S(2)}) async-start(), calls=%async_computation | async-start | bytes 1572864 | tf_op jit(solution)/shard_map/all_gather | solution.py:55
  11.7 136.6 %copy-start.1 = (f32[1024]{0:T(1024)S(1)}, f32[1024]{0:T(1024)}, u32[]{:S(2)}) copy-start(f32[1024]{0:T(1024)} %param.12) | copy-start | bytes 12292
Sparse Core Ops, SparseCore 0:
  10.5 115.5 all-gather.8
  128.8 111.0 all-gather.6
  241.4 7.2 all-gather.4
where the time goes:
time: 263 us; the launch traced here: 262 us
  waiting for transfers between devices  206 us (78%)
  other arithmetic  21.4 us (8%)
  matrix products  18.7 us (7%)
  between operations  13.2 us (5%)
  local copies, waits for them, and re-layouts  2.76 us (1%)
    all_gather x1, waiting for transfers between devices, entering(): everything = lax.all_gather(x, axis)  106 us
    all_gather x1, waiting for transfers between devices, per_device(): late_weight = lax.all_gather(w_out, 'seq', axis=0, tiled=True)  90.5 us
    select_n x16, other arithmetic, lap(): return jnp.where(reached, new, before)  19.7 us
    all_gather x1, waiting for transfers between devices, per_device(): all_heads = lax.all_gather(normed, 'mp', axis=1, tiled=True)  8.81 us
    dot_general x8, matrix products, one_head(): return jnp.dot(head_scores, head_v, preferred_element_type=jnp.float32)  8.33 us
    dot_general x1, matrix products, per_device(): result = jnp.dot(all_heads, late_weight, preferred_element_type=jnp.float32)  7.04 us
  transfers between devices with their start and end apart: 3, of which 3 were waited for; matrix products, arithmetic and copies ran while one was open for 12% of the time, Pallas kernels for 0%

commit v1 on v0

v1 whole, which is shorter than its diff:
```python
import functools

import jax
import jax.numpy as jnp
from jax import lax
from jax.experimental import pallas as pl
from jax.experimental.pallas import tpu as pltpu
from jax.sharding import PartitionSpec as P

HD = 128
PLANE = 4
F32, BF16 = jnp.float32, jnp.bfloat16
VMEM_LIMIT = 40 * 1024 * 1024

ANY = pl.BlockSpec(memory_space=pl.ANY)
VMEM = pl.BlockSpec(memory_space=pltpu.VMEM)
SMEM = pl.BlockSpec(memory_space=pltpu.SMEM)


def call(body, outs, ins, scratch=(), flops=0, moved=0):
    return pl.pallas_call(
        body,
        out_shape=outs,
        in_specs=ins,
        out_specs=[VMEM] * len(outs),
        scratch_shapes=list(scratch),
        compiler_params=pltpu.CompilerParams(vmem_limit_bytes=VMEM_LIMIT),
        cost_estimate=pl.CostEstimate(flops=flops, bytes_accessed=moved, transcendentals=0),
    )


def shape(dims, dtype):
    return jax.ShapeDtypeStruct(dims, dtype)


def silu(block):
    wide = block.astype(F32)
    return (wide / (1.0 + jnp.exp(-wide))).astype(BF16)


def head_cols(head):
    return pl.ds(pl.multiple_of(head * HD, HD), HD)


def states_kernel(place, k_ref, v_ref, *outs):
    per = outs[0].shape[0]
    for j, out in enumerate(outs):
        quarter = place[0] ^ j
        for i in range(per):
            cols = head_cols(quarter * per + i)
            out[i] = lax.dot_general(
                silu(k_ref[:, cols]), v_ref[:, cols], (((0,), (0,)), ((), ())), preferred_element_type=F32
            ).astype(BF16)


def intra_kernel(q_ref, k_ref, v_ref, intra, feat):
    rows = q_ref.shape[0]
    causal = lax.broadcasted_iota(jnp.int32, (rows, rows), 0) >= lax.broadcasted_iota(jnp.int32, (rows, rows), 1)
    for h in range(q_ref.shape[1] // HD):
        cols = slice(h * HD, (h + 1) * HD)
        fq = silu(q_ref[:, cols])
        feat[:, cols] = fq
        scores = lax.dot_general(
            fq, silu(k_ref[:, cols]), (((1,), (1,)), ((), ())), preferred_element_type=F32
        )
        scores = jnp.where(causal, scores, 0.0).astype(BF16)
        intra[:, cols] = jnp.dot(scores, v_ref[:, cols], preferred_element_type=F32)


def total_kernel(a0, a1, a2, a3, out):
    out[...] = ((a0[...].astype(F32) + a1[...].astype(F32)) + (a2[...].astype(F32) + a3[...].astype(F32))).astype(BF16)


def prefixes_kernel(steps, place, *refs):
    own, shifts, outs = refs[:PLANE], refs[PLANE:PLANE + steps], refs[PLANE + steps:]
    before = sum(ref[...].astype(F32) for ref in shifts)
    for j, out in enumerate(outs):
        total = before
        for i, ref in enumerate(own):
            total = total + jnp.where((place[0] ^ i) < (place[0] ^ j), ref[...].astype(F32), 0.0)
        out[...] = total.astype(BF16)


def norm_kernel(place, intra, feat, c0, c1, c2, c3, gain, normed):
    for j, state in enumerate((c0, c1, c2, c3)):
        per = state.shape[0]
        for i in range(per):
            cols = head_cols((place[0] ^ j) * per + i)
            mixed = intra[:, cols] + jnp.dot(feat[:, cols], state[i], preferred_element_type=F32)
            scale = lax.rsqrt(jnp.mean(mixed * mixed, axis=-1, keepdims=True) + 1e-06)
            normed[:, cols] = (mixed * scale * gain[:, cols]).astype(BF16)


def norm_send_kernel(place, intra, feat, c0, c1, c2, c3, gain, normed, to_x, to_y):
    norm_kernel(place, intra, feat, c0, c1, c2, c3, gain, normed)
    x, y = place[0] & 1, place[0] >> 1
    for t in range(4):
        slot = slice(t * HD, (t + 1) * HD)
        to_x[:, slot] = normed[:, head_cols(2 * t + (1 - x))]
        to_y[:, slot] = normed[:, head_cols(4 * (t // 2) + 2 * (1 - y) + t % 2)]


def load_weights(pieces, held, sems):
    copies = []
    for at, piece in enumerate(pieces):
        copies.append(pltpu.make_async_copy(piece, held.at[pl.ds(at * HD, HD)], sems.at[at]))
        copies[-1].start()
    return copies


def partner_kernel(place, *refs):
    wa, wb = refs[0:8], refs[8:16]
    x_own, x_other, y_own, y_other, out_a, out_b, held_a, held_b, left, got, sems = refs[16:]
    copies_a = load_weights(wa, held_a, sems.at[0])
    copies_b = load_weights(wb, held_b, sems.at[1])
    x, y, z, core = place[0] & 1, place[0] >> 1, place[1], place[2]
    for own, other, along, out, held, copies in (
        (x_own, x_other, y, out_a, held_a, copies_a),
        (y_own, y_other, x, out_b, held_b, copies_b),
    ):
        got[core] = own[...]
        got[1 - core] = other[...]
        for r in range(4):
            from_z = (z - r) & 3
            for t in range(2):
                at = 2 * (from_z & 1) + (along ^ t)
                left[:, (2 * r + t) * HD:(2 * r + t + 1) * HD] = got[from_z >> 1, :, head_cols(at)]
        for copy in copies:
            copy.wait()
        out[...] = jnp.dot(left[...], held[...], preferred_element_type=F32).astype(BF16)


def own_kernel(place, *refs):
    wa, wb = refs[0:8], refs[8:16]
    own, other, out, held_a, held_b, left, got, sems = refs[16:]
    copies_a = load_weights(wa, held_a, sems.at[0])
    copies_b = load_weights(wb, held_b, sems.at[1])
    x, y, z, core = place[0] & 1, place[0] >> 1, place[1], place[2]
    got[core] = own[...]
    got[1 - core] = other[...]
    half = held_a.shape[1]
    for first, held, copies in ((0, held_a, copies_a), (1, held_b, copies_b)):
        for r in range(4):
            from_z = (z - r) & 3
            for t in range(2):
                flip = (t << 1) if first == 0 else t
                at = 4 * (from_z & 1) + ((2 * y + x) ^ flip)
                left[:, (2 * r + t) * HD:(2 * r + t + 1) * HD] = got[from_z >> 1, :, head_cols(at)]
        for copy in copies:
            copy.wait()
        out[:, first * half:(first + 1) * half] = jnp.dot(left[...], held[...], preferred_element_type=F32)


def per_device(queries, keys, values, norm_gain, w_out):
    rows, feats = queries.shape
    heads = feats // HD
    blocks = lax.axis_size("seq")
    me, core = lax.axis_index("seq"), lax.axis_index("mp")
    position, level = me % PLANE, me // PLANE
    place = jnp.stack([position, level, core]).astype(jnp.int32)

    def partner(value, flip):
        return lax.ppermute(value, "seq", [(i, i ^ flip) for i in range(blocks)])

    def ring(value):
        return lax.ppermute(value, "seq", [(i, (i + PLANE) % blocks) for i in range(blocks)])

    def up(value, by):
        return lax.ppermute(value, "seq", [(i, i + by * PLANE) for i in range(blocks - by * PLANE)])

    def swap(value):
        return lax.ppermute(value, "mp", [(0, 1), (1, 0)])

    per = heads // PLANE
    quarter = shape((per, HD, HD), BF16)
    own = call(states_kernel, [quarter] * PLANE, [SMEM, VMEM, VMEM], flops=2 * rows * feats * HD)(place, keys, values)
    intra, feat = call(
        intra_kernel, [shape((rows, feats), F32), shape((rows, feats), BF16)], [VMEM] * 3, flops=4 * rows * rows * feats
    )(queries, keys, values)
    mine = [own[0]] + [partner(own[j], j) for j in range(1, PLANE)]
    (running,) = call(total_kernel, [quarter], [VMEM] * PLANE)(*mine)
    shifts, by = [], 1
    while by * PLANE < blocks:
        shifts.append(up(running, by))
        running = (running.astype(F32) + shifts[-1].astype(F32)).astype(BF16)
        by *= 2
    prefixes = call(
        functools.partial(prefixes_kernel, len(shifts)), [quarter] * PLANE, [SMEM] + [VMEM] * (PLANE + len(shifts))
    )(place, *mine, *shifts)
    states = [prefixes[0]] + [partner(prefixes[j], j) for j in range(1, PLANE)]
    gain = norm_gain.reshape(1, feats)
    normed_args = (place, intra, feat, *states, gain)

    if w_out.shape[0] != HD or blocks != 4 * PLANE:
        (normed,) = call(norm_kernel, [shape((rows, feats), BF16)], [SMEM] + [VMEM] * 7)(*normed_args)
        all_heads = lax.all_gather(normed, "mp", axis=1, tiled=True)
        weight = lax.all_gather(w_out, "seq", axis=0, tiled=True)
        return jnp.dot(all_heads, weight, preferred_element_type=F32).astype(BF16)

    cols = w_out.shape[1]
    half = cols // 2
    wa, wb = [], []
    a, b = w_out[:, :half], w_out[:, half:]
    for r in range(4):
        wa += [a, partner(a, 2)]
        wb += [b, partner(b, 1)]
        if r < 3:
            a, b = ring(a), ring(b)

    normed, to_x, to_y = call(
        norm_send_kernel,
        [shape((rows, feats), BF16)] + [shape((rows, feats // 2), BF16)] * 2,
        [SMEM] + [VMEM] * 7,
        flops=2 * rows * feats * HD,
    )(*normed_args)
    got_x, got_y = partner(to_x, 1), partner(to_y, 2)
    other = swap(normed)
    weights = [ANY] * 16
    flops = 2 * rows * cols * (feats)
    room = [pltpu.VMEM((8 * HD, half), BF16)] * 2 + [pltpu.VMEM((rows, feats), BF16)]
    sems = pltpu.SemaphoreType.DMA((2, 8))
    part_a, part_b = call(
        partner_kernel,
        [shape((rows, half), BF16)] * 2,
        [SMEM] + weights + [VMEM] * 4,
        room + [pltpu.VMEM((2, rows, feats // 2), BF16), sems],
        flops=flops,
    )(place, *wa, *wb, got_x, swap(got_x), got_y, swap(got_y))
    (mine_all,) = call(
        own_kernel,
        [shape((rows, cols), F32)],
        [SMEM] + weights + [VMEM] * 2,
        room + [pltpu.VMEM((2, rows, feats), BF16), sems],
        flops=flops,
    )(place, *wa, *wb, normed, other)
    theirs = jnp.concatenate([partner(part_a, 1), partner(part_b, 2)], axis=1)
    return (mine_all + theirs.astype(F32)).astype(BF16)


def solution(mesh):
    in_specs = (P("seq", "mp"), P("seq", "mp"), P("seq", "mp"), P("mp"), P("seq", "mp"))
    out_specs = P("seq", "mp")
    return jax.shard_map(
        per_device, mesh=mesh, in_specs=in_specs, out_specs=out_specs, check_vma=False
    )
```

time: 263 us -> 87.1 us (0.33)
  waiting for transfers between devices: 206 us -> 36.7 us
  starting transfers between devices: 0.08 us -> 36 us
  other arithmetic: 21.4 us -> 1.38 us
  matrix products: 18.7 us -> 0 us
  between operations: 13.2 us -> 0.14 us
  Pallas kernels: 0 us -> 9.51 us
    all_gather x3 -> x0, waiting for transfers between devices: 205 us -> none  [the longest x1 106 us: entering(): everything = lax.all_gather(x, axis)]
    ppermute x0 -> x29, waiting for transfers between devices: none -> 36.7 us  [the longest x18 25.2 us: partner(): return lax.ppermute(value, 'seq', [(i, i ^ flip) for i in range(blocks)])]
    ppermute x0 -> x29, starting transfers between devices: none -> 36 us  [the longest x18 18.4 us: partner(): return lax.ppermute(value, 'seq', [(i, i ^ flip) for i in range(blocks)])]
    select_n x16 -> x0, other arithmetic: 19.7 us -> none  [lap(): return jnp.where(reached, new, before)]
    dot_general x11 -> x0, matrix products: 18.7 us -> none  [the longest x8 8.33 us: one_head(): return jnp.dot(head_scores, head_v, preferred_element_type=jnp.float32)]
    pallas_call x0 -> x7, Pallas kernels: none -> 9.51 us  [the longest x1 2.68 us: per_device(): call(partner_kernel, [shape((rows, half), BF16)] * 2, [SMEM] + weights +...]
  transfers between devices with their start and end apart: 3 -> 29, of which waited for: 3 -> 16; matrix products, arithmetic and copies ran while one was open for 12% -> 1% of each run, Pallas kernels for 0% -> 10%
where the time goes in v1:
time: 87.1 us; the launch traced here: 86.8 us
  waiting for transfers between devices  36.7 us (42%)
  starting transfers between devices  36 us (41%)
  Pallas kernels  9.51 us (11%)
  local copies, waits for them, and re-layouts  3.17 us (4%)
  other arithmetic  1.38 us (2%)
    ppermute x18, waiting for transfers between devices, partner(): return lax.ppermute(value, 'seq', [(i, i ^ flip) for i in range(blocks)])  25.2 us
    ppermute x18, starting transfers between devices, partner(): return lax.ppermute(value, 'seq', [(i, i ^ flip) for i in range(blocks)])  18.4 us
    ppermute x6, starting transfers between devices, ring(): lax.ppermute(value, 'seq', [(i, (i + PLANE) % blocks) for i in range(bloc...  10.9 us
    ppermute x2, starting transfers between devices, up(): lax.ppermute(value, 'seq', [(i, i + by * PLANE) for i in range(blocks - b...  6.62 us
    ppermute x2, waiting for transfers between devices, up(): lax.ppermute(value, 'seq', [(i, i + by * PLANE) for i in range(blocks - b...  6.01 us
    ppermute x6, waiting for transfers between devices, ring(): lax.ppermute(value, 'seq', [(i, (i + PLANE) % blocks) for i in range(bloc...  5.51 us
    pallas_call x1, Pallas kernels, per_device(): call(partner_kernel, [shape((rows, half), BF16)] * 2, [SMEM] + weights +...  2.68 us
    pallas_call x1, Pallas kernels, per_device(): call(own_kernel, [shape((rows, cols), F32)], [SMEM] + weights + [VMEM] *...  2.67 us
  transfers between devices with their start and end apart: 29, of which 16 were waited for; matrix products, arithmetic and copies ran while one was open for 1% of the time, Pallas kernels for 10%

profile of v1, /device:TPU:0, one launch (start us, length us, event | category | flops | bytes accessed | tf_op | source)
XLA Modules:
  0.0 86.8 jit_solution(4256479776764584678)
XLA Ops:
  3.3 3.0 %collective-permute-start.14 = (bf16[2,128,128]{2,1,0:T(8,128)(2,1)S(1)}, bf16[2,128,128]{2,1,0:T(8,128)(2,1)S(1)}, u32[]{:S(2)}, u32[]{:S(2)}) collective-permute-start(bf16[2,128,128]{2,1,0:T(8,128)(2,1)S(1)} %get-tuple-element.23), channel_id=1, source_target_pairs={{0,2},{2,0},{4,6},{6,4},{8,10},{10,8},{12,14},{14,12},{16,18},{18,... | collective-permute-start | bytes 196616 | tf_op jit(solution)/shard_map/ppermute | solution.py:163
  6.3 1.5 %collective-permute-start.15 = (bf16[2,128,128]{2,1,0:T(8,128)(2,1)S(1)}, bf16[2,128,128]{2,1,0:T(8,128)(2,1)S(1)}, u32[]{:S(2)}, u32[]{:S(2)}) collective-permute-start(bf16[2,128,128]{2,1,0:T(8,128)(2,1)S(1)} %get-tuple-element.24), channel_id=1, source_target_pairs={{0,4},{2,6},{4,0},{6,2},{8,12},{10,14},{12,8},{14,10},{16,20},{18,... | collective-permute-start | bytes 196616 | tf_op jit(solution)/shard_map/ppermute | solution.py:163
  8.7 1.9 %collective-permute-done.15.a2.refs_2_ = bf16[2,128,128]{2,1,0:T(8,128)(2,1)S(1)} collective-permute-done((bf16[2,128,128]{2,1,0:T(8,128)(2,1)S(1)}, bf16[2,128,128]{2,1,0:T(8,128)(2,1)S(1)}, u32[]{:S(2)}, u32[]{:S(2)}) %collective-permute-start.15) | collective-permute-done | bytes 65568 | tf_op jit(solution)/shard_map/ppermute | solution.py:163
  10.6 2.4 %collective-permute-done.16.a3.refs_3_ = bf16[2,128,128]{2,1,0:T(8,128)(2,1)S(1)} collective-permute-done((bf16[2,128,128]{2,1,0:T(8,128)(2,1)S(1)}, bf16[2,128,128]{2,1,0:T(8,128)(2,1)S(1)}, u32[]{:S(2)}, u32[]{:S(2)}) %collective-permute-start.16) | collective-permute-done | bytes 65568 | tf_op jit(solution)/shard_map/ppermute | solution.py:163
  13.0 3.5 %collective-permute-start.17 = (bf16[2,128,128]{2,1,0:T(8,128)(2,1)S(1)}, bf16[2,128,128]{2,1,0:T(8,128)(2,1)S(1)}, u32[]{:S(2)}, u32[]{:S(2)}) collective-permute-start(bf16[2,128,128]{2,1,0:T(8,128)(2,1)S(1)} %shard_map.57), channel_id=1, source_target_pairs={{0,8},{2,10},{4,12},{6,14},{8,16},{10,18},{12,20},{14,22},{16,24},... | collective-permute-start | bytes 196616 | tf_op jit(solution)/shard_map/ppermute | solution.py:169
  17.6 1.6 %collective-permute-start.8 = (bf16[128,1024]{1,0:T(8,128)(2,1)S(1)}, bf16[128,1024]{1,0:T(8,128)(2,1)S(1)}, u32[]{:S(2)}, u32[]{:S(2)}) collective-permute-start(bf16[128,1024]{1,0:T(8,128)(2,1)S(1)} %get-tuple-element.35.refs_8_), channel_id=1, source_target_pairs={{0,8},{2,10},{4,12},{6,14},{8,16},{10,18},{12,20},{14,22},{16,24},... | collective-permute-start | bytes 786440 | tf_op jit(solution)/shard_map/ppermute | solution.py:166
  19.8 1.6 %collective-permute-start.1 = (bf16[128,1024]{1,0:T(8,128)(2,1)S(1)}, bf16[128,1024]{1,0:T(8,128)(2,1)S(1)}, u32[]{:S(2)}, u32[]{:S(2)}) collective-permute-start(bf16[128,1024]{1,0:T(8,128)(2,1)S(1)} %get-tuple-element.36.refs_0_), channel_id=1, source_target_pairs={{0,8},{2,10},{4,12},{6,14},{8,16},{10,18},{12,20},{14,22},{16,24},... | collective-permute-start | bytes 786440 | tf_op jit(solution)/shard_map/ppermute | solution.py:166
  21.4 3.1 %collective-permute-start.18 = (bf16[2,128,128]{2,1,0:T(8,128)(2,1)S(1)}, bf16[2,128,128]{2,1,0:T(8,128)(2,1)S(1)}, u32[]{:S(2)}, u32[]{:S(2)}) collective-permute-start(bf16[2,128,128]{2,1,0:T(8,128)(2,1)S(1)} %add_convert_fusion.1), channel_id=1, source_target_pairs={{0,16},{2,18},{4,20},{6,22},{8,24},{10,26},{12,28},{14,30},{1,17},... | collective-permute-start | bytes 196616 | tf_op jit(solution)/shard_map/ppermute | solution.py:169
  24.5 6.0 %collective-permute-done.18.refs_5_ = bf16[2,128,128]{2,1,0:T(8,128)(2,1)S(1)} collective-permute-done((bf16[2,128,128]{2,1,0:T(8,128)(2,1)S(1)}, bf16[2,128,128]{2,1,0:T(8,128)(2,1)S(1)}, u32[]{:S(2)}, u32[]{:S(2)}) %collective-permute-start.18) | collective-permute-done | bytes 65568 | tf_op jit(solution)/shard_map/ppermute | solution.py:169
  32.8 3.3 %collective-permute-done.19.c1 = bf16[2,128,128]{2,1,0:T(8,128)(2,1)S(1)} collective-permute-done((bf16[2,128,128]{2,1,0:T(8,128)(2,1)S(1)}, bf16[2,128,128]{2,1,0:T(8,128)(2,1)S(1)}, u32[]{:S(2)}, u32[]{:S(2)}) %collective-permute-start.19) | collective-permute-done | bytes 65568 | tf_op jit(solution)/shard_map/ppermute | solution.py:163
  38.6 2.5 %collective-permute-start.10 = (bf16[128,1024]{1,0:T(8,128)(2,1)S(1)}, bf16[128,1024]{1,0:T(8,128)(2,1)S(1)}, u32[]{:S(2)}, u32[]{:S(2)}) collective-permute-start(bf16[128,1024]{1,0:T(8,128)(2,1)S(1)} %collective-permute-done.8.refs_10_), channel_id=1, source_target_pairs={{0,8},{2,10},{4,12},{6,14},{8,16},{10,18},{12,20},{14,22},{16,24},... | collective-permute-start | bytes 786440 | tf_op jit(solution)/shard_map/ppermute | solution.py:166
  43.0 2.6 %collective-permute-start.3 = (bf16[128,1024]{1,0:T(8,128)(2,1)S(1)}, bf16[128,1024]{1,0:T(8,128)(2,1)S(1)}, u32[]{:S(2)}, u32[]{:S(2)}) collective-permute-start(bf16[128,1024]{1,0:T(8,128)(2,1)S(1)} %collective-permute-done.1.refs_2_), channel_id=1, source_target_pairs={{0,8},{2,10},{4,12},{6,14},{8,16},{10,18},{12,20},{14,22},{16,24},... | collective-permute-start | bytes 786440 | tf_op jit(solution)/shard_map/ppermute | solution.py:166
  48.6 1.5 %collective-permute-start.23 = (bf16[256,512]{1,0:T(8,128)(2,1)S(1)}, bf16[256,512]{1,0:T(8,128)(2,1)S(1)}, u32[]{:S(2)}, u32[]{:S(2)}) collective-permute-start(bf16[256,512]{1,0:T(8,128)(2,1)S(1)} %get-tuple-element.31), channel_id=1, source_target_pairs={{0,2},{2,0},{4,6},{6,4},{8,10},{10,8},{12,14},{14,12},{16,18},{18,... | collective-permute-start | bytes 786440 | tf_op jit(solution)/shard_map/ppermute | solution.py:163
  50.9 2.7 %collective-permute-start.12 = (bf16[128,1024]{1,0:T(8,128)(2,1)S(1)}, bf16[128,1024]{1,0:T(8,128)(2,1)S(1)}, u32[]{:S(2)}, u32[]{:S(2)}) collective-permute-start(bf16[128,1024]{1,0:T(8,128)(2,1)S(1)} %collective-permute-done.10.refs_12_), channel_id=1, source_target_pairs={{0,8},{2,10},{4,12},{6,14},{8,16},{10,18},{12,20},{14,22},{16,24},... | collective-permute-start | bytes 786440 | tf_op jit(solution)/shard_map/ppermute | solution.py:166
  53.6 1.9 %collective-permute-done.3.refs_4_ = bf16[128,1024]{1,0:T(8,128)(2,1)S(1)} collective-permute-done((bf16[128,1024]{1,0:T(8,128)(2,1)S(1)}, bf16[128,1024]{1,0:T(8,128)(2,1)S(1)}, u32[]{:S(2)}, u32[]{:S(2)}) %collective-permute-start.3) | collective-permute-done | bytes 262176 | tf_op jit(solution)/shard_map/ppermute | solution.py:166
  58.5 1.8 %collective-permute-done.12.refs_14_ = bf16[128,1024]{1,0:T(8,128)(2,1)S(1)} collective-permute-done((bf16[128,1024]{1,0:T(8,128)(2,1)S(1)}, bf16[128,1024]{1,0:T(8,128)(2,1)S(1)}, u32[]{:S(2)}, u32[]{:S(2)}) %collective-permute-start.12) | collective-permute-done | bytes 262176 | tf_op jit(solution)/shard_map/ppermute | solution.py:166
  60.3 1.5 %collective-permute-done.11.refs_13_ = bf16[128,1024]{1,0:T(8,128)(2,1)S(1)} collective-permute-done((bf16[128,1024]{1,0:T(8,128)(2,1)S(1)}, bf16[128,1024]{1,0:T(8,128)(2,1)S(1)}, u32[]{:S(2)}, u32[]{:S(2)}) %collective-permute-start.11) | collective-permute-done | bytes 262176 | tf_op jit(solution)/shard_map/ppermute | solution.py:163
  62.6 1.8 %collective-permute-done.5.refs_6_ = bf16[128,1024]{1,0:T(8,128)(2,1)S(1)} collective-permute-done((bf16[128,1024]{1,0:T(8,128)(2,1)S(1)}, bf16[128,1024]{1,0:T(8,128)(2,1)S(1)}, u32[]{:S(2)}, u32[]{:S(2)}) %collective-permute-start.5) | collective-permute-done | bytes 262176 | tf_op jit(solution)/shard_map/ppermute | solution.py:166
  65.7 3.3 %collective-permute-done.13.refs_15_ = bf16[128,1024]{1,0:T(8,128)(2,1)S(1)} collective-permute-done((bf16[128,1024]{1,0:T(8,128)(2,1)S(1)}, bf16[128,1024]{1,0:T(8,128)(2,1)S(1)}, u32[]{:S(2)}, u32[]{:S(2)}) %collective-permute-start.13) | collective-permute-done | bytes 262176 | tf_op jit(solution)/shard_map/ppermute | solution.py:163
  69.0 1.8 %collective-permute-done.6.refs_7_ = bf16[128,1024]{1,0:T(8,128)(2,1)S(1)} collective-permute-done((bf16[128,1024]{1,0:T(8,128)(2,1)S(1)}, bf16[128,1024]{1,0:T(8,128)(2,1)S(1)}, u32[]{:S(2)}, u32[]{:S(2)}) %collective-permute-start.6) | collective-permute-done | bytes 262176 | tf_op jit(solution)/shard_map/ppermute | solution.py:163
  70.8 2.7 %shard_map.61 = (bf16[256,1024]{1,0:T(8,128)(2,1)S(1)}, bf16[256,1024]{1,0:T(8,128)(2,1)S(1)}) custom-call(s32[3]{0:T(128)S(1)} %pad_add_fusion.place, bf16[128,1024]{1,0:T(8,128)(2,1)S(1)} %get-tuple-element.36.refs_0_, bf16[128,1024]{1,0:T(8,128)(2,1)S(1)} %collective-permute-done.refs_1_, bf16[128,1024]{1,0:T(8,128)(2,1)S(1)} %collective-permute-done.1.refs_2_, ...), custom_call_target="tpu_custom_call" | custom-call | flops 1073741824 | tf_op jit(solution)/shard_map/pallas_call | solution.py:222
  75.8 2.7 %shard_map.60 = f32[256,2048]{1,0:T(8,128)S(1)} custom-call(s32[3]{0:T(128)S(1)} %pad_add_fusion.place, bf16[128,1024]{1,0:T(8,128)(2,1)S(1)} %get-tuple-element.36.refs_0_, bf16[128,1024]{1,0:T(8,128)(2,1)S(1)} %collective-permute-done.refs_1_, bf16[128,1024]{1,0:T(8,128)(2,1)S(1)} %collective-permute-done.1.refs_2_, ...), custom_call_target="tpu_custom_call" | custom-call | flops 1073741824 | tf_op jit(solution)/shard_map/pallas_call | solution.py:229
  78.5 5.6 %collective-permute-done.27 = bf16[256,1024]{1,0:T(8,128)(2,1)S(1)} collective-permute-done((bf16[256,1024]{1,0:T(8,128)(2,1)S(1)}, bf16[256,1024]{1,0:T(8,128)(2,1)S(1)}, u32[]{:S(2)}, u32[]{:S(2)}) %collective-permute-start.27) | collective-permute-done | bytes 524320 | tf_op jit(solution)/shard_map/ppermute | solution.py:163
  84.1 1.4 %collective-permute-done.28 = bf16[256,1024]{1,0:T(8,128)(2,1)S(1)} collective-permute-done((bf16[256,1024]{1,0:T(8,128)(2,1)S(1)}, bf16[256,1024]{1,0:T(8,128)(2,1)S(1)}, u32[]{:S(2)}, u32[]{:S(2)}) %collective-permute-start.28) | collective-permute-done | bytes 524320 | tf_op jit(solution)/shard_map/ppermute | solution.py:163
  (57 shorter events, 24.9 us)
Async XLA Ops:
  13.0 8.3 %collective-permute-start.17 = (bf16[2,128,128]{2,1,0:T(8,128)(2,1)S(1)}, bf16[2,128,128]{2,1,0:T(8,128)(2,1)S(1)}, u32[]{:S(2)}, u32[]{:S(2)}) collective-permute-start(bf16[2,128,128]{2,1,0:T(8,128)(2,1)S(1)} %shard_map.57), channel_id=1, source_target_pairs={{0,8},{2,10},{4,12},{6,14},{8,16},{10,18},{12,20},{14,22},{16,24},... | collective-permute-start | bytes 196616 | tf_op jit(solution)/shard_map/ppermute | solution.py:169
  17.6 21.0 %collective-permute-start.8 = (bf16[128,1024]{1,0:T(8,128)(2,1)S(1)}, bf16[128,1024]{1,0:T(8,128)(2,1)S(1)}, u32[]{:S(2)}, u32[]{:S(2)}) collective-permute-start(bf16[128,1024]{1,0:T(8,128)(2,1)S(1)} %get-tuple-element.35.refs_8_), channel_id=1, source_target_pairs={{0,8},{2,10},{4,12},{6,14},{8,16},{10,18},{12,20},{14,22},{16,24},... | collective-permute-start | bytes 786440 | tf_op jit(solution)/shard_map/ppermute | solution.py:166
  19.2 26.3 %collective-permute-start.7 = (bf16[128,1024]{1,0:T(8,128)(2,1)S(1)}, bf16[128,1024]{1,0:T(8,128)(2,1)S(1)}, u32[]{:S(2)}, u32[]{:S(2)}) collective-permute-start(bf16[128,1024]{1,0:T(8,128)(2,1)S(1)} %get-tuple-element.35.refs_8_), channel_id=1, source_target_pairs={{0,2},{2,0},{4,6},{6,4},{8,10},{10,8},{12,14},{14,12},{16,18},{18,... | collective-permute-start | bytes 786440 | tf_op jit(solution)/shard_map/ppermute | solution.py:163
  19.8 23.2 %collective-permute-start.1 = (bf16[128,1024]{1,0:T(8,128)(2,1)S(1)}, bf16[128,1024]{1,0:T(8,128)(2,1)S(1)}, u32[]{:S(2)}, u32[]{:S(2)}) collective-permute-start(bf16[128,1024]{1,0:T(8,128)(2,1)S(1)} %get-tuple-element.36.refs_0_), channel_id=1, source_target_pairs={{0,8},{2,10},{4,12},{6,14},{8,16},{10,18},{12,20},{14,22},{16,24},... | collective-permute-start | bytes 786440 | tf_op jit(solution)/shard_map/ppermute | solution.py:166
  21.4 9.2 %collective-permute-start.18 = (bf16[2,128,128]{2,1,0:T(8,128)(2,1)S(1)}, bf16[2,128,128]{2,1,0:T(8,128)(2,1)S(1)}, u32[]{:S(2)}, u32[]{:S(2)}) collective-permute-start(bf16[2,128,128]{2,1,0:T(8,128)(2,1)S(1)} %add_convert_fusion.1), channel_id=1, source_target_pairs={{0,16},{2,18},{4,20},{6,22},{8,24},{10,26},{12,28},{14,30},{1,17},... | collective-permute-start | bytes 196616 | tf_op jit(solution)/shard_map/ppermute | solution.py:169
  32.2 5.4 %collective-permute-start.20 = (bf16[2,128,128]{2,1,0:T(8,128)(2,1)S(1)}, bf16[2,128,128]{2,1,0:T(8,128)(2,1)S(1)}, u32[]{:S(2)}, u32[]{:S(2)}) collective-permute-start(bf16[2,128,128]{2,1,0:T(8,128)(2,1)S(1)} %get-tuple-element.28), channel_id=1, source_target_pairs={{0,4},{2,6},{4,0},{6,2},{8,12},{10,14},{12,8},{14,10},{16,20},{18,... | collective-permute-start | bytes 196616 | tf_op jit(solution)/shard_map/ppermute | solution.py:163
  36.1 5.9 %collective-permute-start.21 = (bf16[2,128,128]{2,1,0:T(8,128)(2,1)S(1)}, bf16[2,128,128]{2,1,0:T(8,128)(2,1)S(1)}, u32[]{:S(2)}, u32[]{:S(2)}) collective-permute-start(bf16[2,128,128]{2,1,0:T(8,128)(2,1)S(1)} %get-tuple-element.29), channel_id=1, source_target_pairs={{0,6},{2,4},{4,2},{6,0},{8,14},{10,12},{12,10},{14,8},{16,22},{18,... | collective-permute-start | bytes 196616 | tf_op jit(solution)/shard_map/ppermute | solution.py:163
  37.7 10.9 %collective-permute-start = (bf16[128,1024]{1,0:T(8,128)(2,1)S(1)}, bf16[128,1024]{1,0:T(8,128)(2,1)S(1)}, u32[]{:S(2)}, u32[]{:S(2)}) collective-permute-start(bf16[128,1024]{1,0:T(8,128)(2,1)S(1)} %get-tuple-element.36.refs_0_), channel_id=1, source_target_pairs={{0,4},{2,6},{4,0},{6,2},{8,12},{10,14},{12,8},{14,10},{16,20},{18,... | collective-permute-start | bytes 786440 | tf_op jit(solution)/shard_map/ppermute | solution.py:163
  38.6 11.5 %collective-permute-start.10 = (bf16[128,1024]{1,0:T(8,128)(2,1)S(1)}, bf16[128,1024]{1,0:T(8,128)(2,1)S(1)}, u32[]{:S(2)}, u32[]{:S(2)}) collective-permute-start(bf16[128,1024]{1,0:T(8,128)(2,1)S(1)} %collective-permute-done.8.refs_10_), channel_id=1, source_target_pairs={{0,8},{2,10},{4,12},{6,14},{8,16},{10,18},{12,20},{14,22},{16,24},... | collective-permute-start | bytes 786440 | tf_op jit(solution)/shard_map/ppermute | solution.py:166
  42.0 8.9 %collective-permute-start.9 = (bf16[128,1024]{1,0:T(8,128)(2,1)S(1)}, bf16[128,1024]{1,0:T(8,128)(2,1)S(1)}, u32[]{:S(2)}, u32[]{:S(2)}) collective-permute-start(bf16[128,1024]{1,0:T(8,128)(2,1)S(1)} %collective-permute-done.8.refs_10_), channel_id=1, source_target_pairs={{0,2},{2,0},{4,6},{6,4},{8,10},{10,8},{12,14},{14,12},{16,18},{18,... | collective-permute-start | bytes 786440 | tf_op jit(solution)/shard_map/ppermute | solution.py:163
  43.0 12.5 %collective-permute-start.3 = (bf16[128,1024]{1,0:T(8,128)(2,1)S(1)}, bf16[128,1024]{1,0:T(8,128)(2,1)S(1)}, u32[]{:S(2)}, u32[]{:S(2)}) collective-permute-start(bf16[128,1024]{1,0:T(8,128)(2,1)S(1)} %collective-permute-done.1.refs_2_), channel_id=1, source_target_pairs={{0,8},{2,10},{4,12},{6,14},{8,16},{10,18},{12,20},{14,22},{16,24},... | collective-permute-start | bytes 786440 | tf_op jit(solution)/shard_map/ppermute | solution.py:166
  45.6 10.7 %collective-permute-start.2 = (bf16[128,1024]{1,0:T(8,128)(2,1)S(1)}, bf16[128,1024]{1,0:T(8,128)(2,1)S(1)}, u32[]{:S(2)}, u32[]{:S(2)}) collective-permute-start(bf16[128,1024]{1,0:T(8,128)(2,1)S(1)} %collective-permute-done.1.refs_2_), channel_id=1, source_target_pairs={{0,4},{2,6},{4,0},{6,2},{8,12},{10,14},{12,8},{14,10},{16,20},{18,... | collective-permute-start | bytes 786440 | tf_op jit(solution)/shard_map/ppermute | solution.py:163
  48.6 7.7 %collective-permute-start.23 = (bf16[256,512]{1,0:T(8,128)(2,1)S(1)}, bf16[256,512]{1,0:T(8,128)(2,1)S(1)}, u32[]{:S(2)}, u32[]{:S(2)}) collective-permute-start(bf16[256,512]{1,0:T(8,128)(2,1)S(1)} %get-tuple-element.31), channel_id=1, source_target_pairs={{0,2},{2,0},{4,6},{6,4},{8,10},{10,8},{12,14},{14,12},{16,18},{18,... | collective-permute-start | bytes 786440 | tf_op jit(solution)/shard_map/ppermute | solution.py:163
  50.1 8.4 %collective-permute-start.25 = (bf16[256,512]{1,0:T(8,128)(2,1)S(1)}, bf16[256,512]{1,0:T(8,128)(2,1)S(1)}, u32[]{:S(2)}, u32[]{:S(2)}) collective-permute-start(bf16[256,512]{1,0:T(8,128)(2,1)S(1)} %get-tuple-element.32), channel_id=1, source_target_pairs={{0,4},{2,6},{4,0},{6,2},{8,12},{10,14},{12,8},{14,10},{16,20},{18,... | collective-permute-start | bytes 786440 | tf_op jit(solution)/shard_map/ppermute | solution.py:163
  50.9 9.4 %collective-permute-start.12 = (bf16[128,1024]{1,0:T(8,128)(2,1)S(1)}, bf16[128,1024]{1,0:T(8,128)(2,1)S(1)}, u32[]{:S(2)}, u32[]{:S(2)}) collective-permute-start(bf16[128,1024]{1,0:T(8,128)(2,1)S(1)} %collective-permute-done.10.refs_12_), channel_id=1, source_target_pairs={{0,8},{2,10},{4,12},{6,14},{8,16},{10,18},{12,20},{14,22},{16,24},... | collective-permute-start | bytes 786440 | tf_op jit(solution)/shard_map/ppermute | solution.py:166
  55.5 6.4 %collective-permute-start.11 = (bf16[128,1024]{1,0:T(8,128)(2,1)S(1)}, bf16[128,1024]{1,0:T(8,128)(2,1)S(1)}, u32[]{:S(2)}, u32[]{:S(2)}) collective-permute-start(bf16[128,1024]{1,0:T(8,128)(2,1)S(1)} %collective-permute-done.10.refs_12_), channel_id=1, source_target_pairs={{0,2},{2,0},{4,6},{6,4},{8,10},{10,8},{12,14},{14,12},{16,18},{18,... | collective-permute-start | bytes 786440 | tf_op jit(solution)/shard_map/ppermute | solution.py:163
  56.3 8.2 %collective-permute-start.5 = (bf16[128,1024]{1,0:T(8,128)(2,1)S(1)}, bf16[128,1024]{1,0:T(8,128)(2,1)S(1)}, u32[]{:S(2)}, u32[]{:S(2)}) collective-permute-start(bf16[128,1024]{1,0:T(8,128)(2,1)S(1)} %collective-permute-done.3.refs_4_), channel_id=1, source_target_pairs={{0,8},{2,10},{4,12},{6,14},{8,16},{10,18},{12,20},{14,22},{16,24},... | collective-permute-start | bytes 786440 | tf_op jit(solution)/shard_map/ppermute | solution.py:166
  56.3 9.4 %collective-permute-start.4 = (bf16[128,1024]{1,0:T(8,128)(2,1)S(1)}, bf16[128,1024]{1,0:T(8,128)(2,1)S(1)}, u32[]{:S(2)}, u32[]{:S(2)}) collective-permute-start(bf16[128,1024]{1,0:T(8,128)(2,1)S(1)} %collective-permute-done.3.refs_4_), channel_id=1, source_target_pairs={{0,4},{2,6},{4,0},{6,2},{8,12},{10,14},{12,8},{14,10},{16,20},{18,... | collective-permute-start | bytes 786440 | tf_op jit(solution)/shard_map/ppermute | solution.py:163
  58.5 7.2 %collective-permute-start.24 = (bf16[256,512]{1,0:T(8,128)(2,1)S(1)}, bf16[256,512]{1,0:T(8,128)(2,1)S(1)}, u32[]{:S(2)}, u32[]{:S(2)}) collective-permute-start(bf16[256,512]{1,0:T(8,128)(2,1)S(1)} %collective-permute-done.23.refs_16_), channel_id=1, source_target_pairs={{0,1},{1,0},{2,3},{3,2},{4,5},{5,4},{6,7},{7,6},{8,9},{9,8},{10,11... | collective-permute-start | bytes 786440 | tf_op jit(solution)/shard_map/ppermute | solution.py:172
  61.8 7.2 %collective-permute-start.13 = (bf16[128,1024]{1,0:T(8,128)(2,1)S(1)}, bf16[128,1024]{1,0:T(8,128)(2,1)S(1)}, u32[]{:S(2)}, u32[]{:S(2)}) collective-permute-start(bf16[128,1024]{1,0:T(8,128)(2,1)S(1)} %collective-permute-done.12.refs_14_), channel_id=1, source_target_pairs={{0,2},{2,0},{4,6},{6,4},{8,10},{10,8},{12,14},{14,12},{16,18},{18,... | collective-permute-start | bytes 786440 | tf_op jit(solution)/shard_map/ppermute | solution.py:163
  64.4 6.4 %collective-permute-start.6 = (bf16[128,1024]{1,0:T(8,128)(2,1)S(1)}, bf16[128,1024]{1,0:T(8,128)(2,1)S(1)}, u32[]{:S(2)}, u32[]{:S(2)}) collective-permute-start(bf16[128,1024]{1,0:T(8,128)(2,1)S(1)} %collective-permute-done.5.refs_6_), channel_id=1, source_target_pairs={{0,4},{2,6},{4,0},{6,2},{8,12},{10,14},{12,8},{14,10},{16,20},{18,... | collective-permute-start | bytes 786440 | tf_op jit(solution)/shard_map/ppermute | solution.py:163
  65.7 10.1 %collective-permute-start.22 = (bf16[256,1024]{1,0:T(8,128)(2,1)S(1)}, bf16[256,1024]{1,0:T(8,128)(2,1)S(1)}, u32[]{:S(2)}, u32[]{:S(2)}) collective-permute-start(bf16[256,1024]{1,0:T(8,128)(2,1)S(1)} %get-tuple-element.30.refs_16_), channel_id=1, source_target_pairs={{0,1},{1,0},{2,3},{3,2},{4,5},{5,4},{6,7},{7,6},{8,9},{9,8},{10,11... | collective-permute-start | bytes 1572872 | tf_op jit(solution)/shard_map/ppermute | solution.py:172
  73.5 10.6 %collective-permute-start.27 = (bf16[256,1024]{1,0:T(8,128)(2,1)S(1)}, bf16[256,1024]{1,0:T(8,128)(2,1)S(1)}, u32[]{:S(2)}, u32[]{:S(2)}) collective-permute-start(bf16[256,1024]{1,0:T(8,128)(2,1)S(1)} %get-tuple-element.33), channel_id=1, source_target_pairs={{0,2},{2,0},{4,6},{6,4},{8,10},{10,8},{12,14},{14,12},{16,18},{18,... | collective-permute-start | bytes 1572872 | tf_op jit(solution)/shard_map/ppermute | solution.py:163
  74.8 10.8 %collective-permute-start.28 = (bf16[256,1024]{1,0:T(8,128)(2,1)S(1)}, bf16[256,1024]{1,0:T(8,128)(2,1)S(1)}, u32[]{:S(2)}, u32[]{:S(2)}) collective-permute-start(bf16[256,1024]{1,0:T(8,128)(2,1)S(1)} %get-tuple-element.34), channel_id=1, source_target_pairs={{0,4},{2,6},{4,0},{6,2},{8,12},{10,14},{12,8},{14,10},{16,20},{18,... | collective-permute-start | bytes 1572872 | tf_op jit(solution)/shard_map/ppermute | solution.py:163
  (11 other events, 204.4 us)

commit v2 on v1

--- a/solution.py
+++ b/solution.py
@@ -100,55 +100,45 @@
         to_y[:, slot] = normed[:, head_cols(4 * (t // 2) + 2 * (1 - y) + t % 2)]
 
 
-def load_weights(pieces, held, sems):
-    copies = []
-    for at, piece in enumerate(pieces):
-        copies.append(pltpu.make_async_copy(piece, held.at[pl.ds(at * HD, HD)], sems.at[at]))
-        copies[-1].start()
-    return copies
-
-
-def partner_kernel(place, *refs):
-    wa, wb = refs[0:8], refs[8:16]
-    x_own, x_other, y_own, y_other, out_a, out_b, held_a, held_b, left, got, sems = refs[16:]
-    copies_a = load_weights(wa, held_a, sems.at[0])
-    copies_b = load_weights(wb, held_b, sems.at[1])
-    x, y, z, core = place[0] & 1, place[0] >> 1, place[1], place[2]
-    for own, other, along, out, held, copies in (
-        (x_own, x_other, y, out_a, held_a, copies_a),
-        (y_own, y_other, x, out_b, held_b, copies_b),
-    ):
-        got[core] = own[...]
-        got[1 - core] = other[...]
-        for r in range(4):
-            from_z = (z - r) & 3
-            for t in range(2):
-                at = 2 * (from_z & 1) + (along ^ t)
-                left[:, (2 * r + t) * HD:(2 * r + t + 1) * HD] = got[from_z >> 1, :, head_cols(at)]
-        for copy in copies:
-            copy.wait()
-        out[...] = jnp.dot(left[...], held[...], preferred_element_type=F32).astype(BF16)
-
-
-def own_kernel(place, *refs):
-    wa, wb = refs[0:8], refs[8:16]
-    own, other, out, held_a, held_b, left, got, sems = refs[16:]
-    copies_a = load_weights(wa, held_a, sems.at[0])
-    copies_b = load_weights(wb, held_b, sems.at[1])
-    x, y, z, core = place[0] & 1, place[0] >> 1, place[1], place[2]
-    got[core] = own[...]
-    got[1 - core] = other[...]
-    half = held_a.shape[1]
-    for first, held, copies in ((0, held_a, copies_a), (1, held_b, copies_b)):
-        for r in range(4):
-            from_z = (z - r) & 3
-            for t in range(2):
-                flip = (t << 1) if first == 0 else t
-                at = 4 * (from_z & 1) + ((2 * y + x) ^ flip)
-                left[:, (2 * r + t) * HD:(2 * r + t + 1) * HD] = got[from_z >> 1, :, head_cols(at)]
-        for copy in copies:
-            copy.wait()
-        out[:, first * half:(first + 1) * half] = jnp.dot(left[...], held[...], preferred_element_type=F32)
+def head_at(place, r, t, way, flip):
+    from_z = (place[1] + way * r) & 3
+    return from_z >> 1, 4 * (from_z & 1) + (place[0] ^ (t * flip))
+
+
+def sums(place, pieces, own, other, way, flip, thin):
+    left = []
+    for r in range(4):
+        for t in range(2):
+            core, head = head_at(place, r, t, way, flip)
+            if thin:
+                head = (head >> 1) if flip == 2 else 2 * (head >> 2) + (head & 1)
+            cols = head_cols(head)
+            left.append(jnp.where(core == place[2], own[:, cols], other[:, cols]))
+    return jnp.dot(
+        jnp.concatenate(left, axis=1), jnp.concatenate([p[...] for p in pieces], axis=0), preferred_element_type=F32
+    )
+
+
+def partner_kernel(way, flip, place, *refs):
+    own, other, out = refs[8:]
+    out[...] = sums(place, refs[:8], own, other, way, flip, True).astype(BF16)
+
+
+def own_kernel(ways, place, *refs):
+    own, other, out = refs[16:]
+    cut = refs[0].shape[1]
+    out[:, :cut] = sums(place, refs[:8], own, other, ways[0], 2, False)
+    out[:, cut:] = sums(place, refs[8:16], own, other, ways[1], 1, False)
+
+
+CUT = 8
+ZD = 0
+BD = 0
+TIES = {'tot': '', 'z1': 'b1', 'z2': '', 'add': 'x0 y0', 'back': 'a2 y1', 'norm': 'b2', 'act': 'a3', 'act2': 'y2', 'act3': 'b3 x2'}
+
+
+def tie(value, *others):
+    return lax.optimization_barrier((value, *others))
 
 
 def per_device(queries, keys, values, norm_gain, w_out):
@@ -158,18 +148,39 @@
     me, core = lax.axis_index("seq"), lax.axis_index("mp")
     position, level = me % PLANE, me // PLANE
     place = jnp.stack([position, level, core]).astype(jnp.int32)
+    split = w_out.shape[0] == HD and blocks == 4 * PLANE
 
     def partner(value, flip):
         return lax.ppermute(value, "seq", [(i, i ^ flip) for i in range(blocks)])
 
-    def ring(value):
-        return lax.ppermute(value, "seq", [(i, (i + PLANE) % blocks) for i in range(blocks)])
+    def ring(value, way=1):
+        return lax.ppermute(value, "seq", [(i, (i + way * PLANE) % blocks) for i in range(blocks)])
 
     def up(value, by):
         return lax.ppermute(value, "seq", [(i, i + by * PLANE) for i in range(blocks - by * PLANE)])
 
     def swap(value):
         return lax.ppermute(value, "mp", [(0, 1), (1, 0)])
+
+    cols = w_out.shape[1]
+    half = cols * CUT // 16
+    held = {"a0": w_out[:, :half], "b0": w_out[:, half:]}
+
+    def piece(n):
+        if n not in held:
+            if n[0] in "ab":
+                held[n] = ring(piece(n[0] + str(int(n[1]) - 1)), -1 if BD and n[0] == "b" else 1)
+            else:
+                held[n] = partner(piece({"x": "b", "y": "a"}[n[0]] + n[1]), {"x": 1, "y": 2}[n[0]])
+        return held[n]
+
+    def tied(value, name):
+        names = TIES[name].split() if split else []
+        if not names:
+            return value
+        value, *rest = tie(value, *[piece(n) for n in names])
+        held.update(zip(names, rest))
+        return value
 
     per = heads // PLANE
     quarter = shape((per, HD, HD), BF16)
@@ -178,34 +189,35 @@
         intra_kernel, [shape((rows, feats), F32), shape((rows, feats), BF16)], [VMEM] * 3, flops=4 * rows * rows * feats
     )(queries, keys, values)
     mine = [own[0]] + [partner(own[j], j) for j in range(1, PLANE)]
+    mine[3] = tied(mine[3], "tot")
     (running,) = call(total_kernel, [quarter], [VMEM] * PLANE)(*mine)
-    shifts, by = [], 1
-    while by * PLANE < blocks:
-        shifts.append(up(running, by))
-        running = (running.astype(F32) + shifts[-1].astype(F32)).astype(BF16)
-        by *= 2
+    running = tied(running, "z1")
+    if split and ZD:
+        shifts = [up(running, by) for by in range(1, blocks // PLANE)]
+    else:
+        shifts, by = [], 1
+        while by * PLANE < blocks:
+            if by == 2:
+                running = tied(running, "z2")
+            shifts.append(up(running, by))
+            running = (running.astype(F32) + shifts[-1].astype(F32)).astype(BF16)
+            by *= 2
+    shifts[-1] = tied(shifts[-1], "add")
     prefixes = call(
         functools.partial(prefixes_kernel, len(shifts)), [quarter] * PLANE, [SMEM] + [VMEM] * (PLANE + len(shifts))
     )(place, *mine, *shifts)
+    prefixes = list(prefixes)
+    prefixes[1] = tied(prefixes[1], "back")
     states = [prefixes[0]] + [partner(prefixes[j], j) for j in range(1, PLANE)]
+    states[3] = tied(states[3], "norm")
     gain = norm_gain.reshape(1, feats)
     normed_args = (place, intra, feat, *states, gain)
 
-    if w_out.shape[0] != HD or blocks != 4 * PLANE:
+    if not split:
         (normed,) = call(norm_kernel, [shape((rows, feats), BF16)], [SMEM] + [VMEM] * 7)(*normed_args)
         all_heads = lax.all_gather(normed, "mp", axis=1, tiled=True)
         weight = lax.all_gather(w_out, "seq", axis=0, tiled=True)
         return jnp.dot(all_heads, weight, preferred_element_type=F32).astype(BF16)
-
-    cols = w_out.shape[1]
-    half = cols // 2
-    wa, wb = [], []
-    a, b = w_out[:, :half], w_out[:, half:]
-    for r in range(4):
-        wa += [a, partner(a, 2)]
-        wb += [b, partner(b, 1)]
-        if r < 3:
-            a, b = ring(a), ring(b)
 
     normed, to_x, to_y = call(
         norm_send_kernel,
@@ -213,27 +225,35 @@
         [SMEM] + [VMEM] * 7,
         flops=2 * rows * feats * HD,
     )(*normed_args)
+    if TIES["act"]:
+        to_x, to_y = tie(to_x, to_y)
+    to_x = tied(to_x, "act")
     got_x, got_y = partner(to_x, 1), partner(to_y, 2)
+    got_x = tied(got_x, "act2")
+    got_y = tied(got_y, "act3")
+    wa, wb = [], []
+    for r in range(4):
+        wa += [piece("a%d" % r), piece("y%d" % r)]
+        wb += [piece("b%d" % r), piece("x%d" % r)]
     other = swap(normed)
-    weights = [ANY] * 16
-    flops = 2 * rows * cols * (feats)
-    room = [pltpu.VMEM((8 * HD, half), BF16)] * 2 + [pltpu.VMEM((rows, feats), BF16)]
-    sems = pltpu.SemaphoreType.DMA((2, 8))
-    part_a, part_b = call(
-        partner_kernel,
-        [shape((rows, half), BF16)] * 2,
-        [SMEM] + weights + [VMEM] * 4,
-        room + [pltpu.VMEM((2, rows, feats // 2), BF16), sems],
-        flops=flops,
-    )(place, *wa, *wb, got_x, swap(got_x), got_y, swap(got_y))
+    ways = (-1, 1 if BD else -1)
+    parts = []
+    for way, flip, pieces, got in ((ways[0], 2, wa, got_x), (ways[1], 1, wb, got_y)):
+        width = pieces[0].shape[1]
+        (part,) = call(
+            functools.partial(partner_kernel, way, flip),
+            [shape((rows, width), BF16)],
+            [SMEM] + [VMEM] * 10,
+            flops=rows * feats * width * 2,
+        )(place, *pieces, got, swap(got))
+        parts.append(partner(part, 3 - flip))
     (mine_all,) = call(
-        own_kernel,
+        functools.partial(own_kernel, ways),
         [shape((rows, cols), F32)],
-        [SMEM] + weights + [VMEM] * 2,
-        room + [pltpu.VMEM((2, rows, feats), BF16), sems],
-        flops=flops,
+        [SMEM] + [VMEM] * 18,
+        flops=rows * feats * cols * 2,
     )(place, *wa, *wb, normed, other)
-    theirs = jnp.concatenate([partner(part_a, 1), partner(part_b, 2)], axis=1)
+    theirs = jnp.concatenate(parts, axis=1)
     return (mine_all + theirs.astype(F32)).astype(BF16)
 
 

time: 87.1 us -> 78 us (0.90)
  waiting for transfers between devices: 36.7 us -> 29.3 us
  starting transfers between devices: 36 us -> 34.6 us
    ppermute x2, waiting for transfers between devices: 6.01 us -> 0.01 us  [up(): lax.ppermute(value, 'seq', [(i, i + by * PLANE) for i in range(blocks - b...]
    ppermute x6, starting transfers between devices: 10.9 us -> 8.58 us  [ring(): lax.ppermute(value, 'seq', [(i, (i + way * PLANE) % blocks) for i in rang...]
    ppermute x6, waiting for transfers between devices: 5.51 us -> 3.43 us  [ring(): lax.ppermute(value, 'seq', [(i, (i + way * PLANE) % blocks) for i in rang...]
    pallas_call x2 -> x3, Pallas kernels: 5.35 us -> 4.51 us  [the longest x2 2.56 us: per_device(): call(functools.partial(partner_kernel, way, flip), [shape((rows, width),...]
  transfers between devices with their start and end apart: 29 -> 29, of which waited for: 16 -> 15; matrix products, arithmetic and copies ran while one was open for 1% -> 0% of each run, Pallas kernels for 10% -> 11%
where the time goes in v2:
time: 78 us; the launch traced here: 77.3 us
  starting transfers between devices  34.6 us (44%)
  waiting for transfers between devices  29.3 us (38%)
  Pallas kernels  8.67 us (11%)
  local copies, waits for them, and re-layouts  3.25 us (4%)
  other arithmetic  1.36 us (2%)
    ppermute x18, waiting for transfers between devices, partner(): return lax.ppermute(value, 'seq', [(i, i ^ flip) for i in range(blocks)])  25.8 us
    ppermute x18, starting transfers between devices, partner(): return lax.ppermute(value, 'seq', [(i, i ^ flip) for i in range(blocks)])  18.9 us
    ppermute x6, starting transfers between devices, ring(): lax.ppermute(value, 'seq', [(i, (i + way * PLANE) % blocks) for i in rang...  8.58 us
    ppermute x2, starting transfers between devices, up(): lax.ppermute(value, 'seq', [(i, i + by * PLANE) for i in range(blocks - b...  7.14 us
    ppermute x6, waiting for transfers between devices, ring(): lax.ppermute(value, 'seq', [(i, (i + way * PLANE) % blocks) for i in rang...  3.43 us
    pallas_call x2, Pallas kernels, per_device(): call(functools.partial(partner_kernel, way, flip), [shape((rows, width),...  2.56 us
    unnamed x12, local copies, waits for them, and re-layouts  2.1 us
    pallas_call x1, Pallas kernels, per_device(): call(functools.partial(own_kernel, ways), [shape((rows, cols), F32)], [SM...  1.95 us
  transfers between devices with their start and end apart: 29, of which 15 were waited for; matrix products, arithmetic and copies ran while one was open for 0% of the time, Pallas kernels for 11%

profile of v2, /device:TPU:0, one launch (start us, length us, event | category | flops | bytes accessed | tf_op | source)
XLA Modules:
  0.0 77.3 jit_solution(15464547295973983751)
XLA Ops:
  1.2 3.1 %collective-permute-start.3 = (bf16[128,1024]{1,0:T(8,128)(2,1)S(1)}, bf16[128,1024]{1,0:T(8,128)(2,1)S(1)}, u32[]{:S(2)}, u32[]{:S(2)}) collective-permute-start(bf16[128,1024]{1,0:T(8,128)(2,1)S(1)} %get-tuple-element.69.refs_8_.refs_0_), channel_id=1, source_target_pairs={{0,8},{2,10},{4,12},{6,14},{8,16},{10,18},{12,20},{14,22},{16,24},... | collective-permute-start | bytes 786440 | tf_op jit(solution)/shard_map/ppermute | solution.py:157
  4.2 1.6 %collective-permute-start.8 = (bf16[128,1024]{1,0:T(8,128)(2,1)S(1)}, bf16[128,1024]{1,0:T(8,128)(2,1)S(1)}, u32[]{:S(2)}, u32[]{:S(2)}) collective-permute-start(bf16[128,1024]{1,0:T(8,128)(2,1)S(1)} %get-tuple-element.70.refs_0_), channel_id=1, source_target_pairs={{0,8},{2,10},{4,12},{6,14},{8,16},{10,18},{12,20},{14,22},{16,24},... | collective-permute-start | bytes 786440 | tf_op jit(solution)/shard_map/ppermute | solution.py:157
  9.1 1.6 %collective-permute-start = (bf16[2,128,128]{2,1,0:T(8,128)(2,1)S(1)}, bf16[2,128,128]{2,1,0:T(8,128)(2,1)S(1)}, u32[]{:S(2)}, u32[]{:S(2)}) collective-permute-start(bf16[2,128,128]{2,1,0:T(8,128)(2,1)S(1)} %get-tuple-element.38), channel_id=1, source_target_pairs={{0,2},{2,0},{4,6},{6,4},{8,10},{10,8},{12,14},{14,12},{16,18},{18,... | collective-permute-start | bytes 196616 | tf_op jit(solution)/shard_map/ppermute | solution.py:154
  10.7 1.5 %collective-permute-start.1 = (bf16[2,128,128]{2,1,0:T(8,128)(2,1)S(1)}, bf16[2,128,128]{2,1,0:T(8,128)(2,1)S(1)}, u32[]{:S(2)}, u32[]{:S(2)}) collective-permute-start(bf16[2,128,128]{2,1,0:T(8,128)(2,1)S(1)} %get-tuple-element.39), channel_id=1, source_target_pairs={{0,4},{2,6},{4,0},{6,2},{8,12},{10,14},{12,8},{14,10},{16,20},{18,... | collective-permute-start | bytes 196616 | tf_op jit(solution)/shard_map/ppermute | solution.py:154
  13.5 2.1 %collective-permute-done.1.a2.refs_2_ = bf16[2,128,128]{2,1,0:T(8,128)(2,1)S(1)} collective-permute-done((bf16[2,128,128]{2,1,0:T(8,128)(2,1)S(1)}, bf16[2,128,128]{2,1,0:T(8,128)(2,1)S(1)}, u32[]{:S(2)}, u32[]{:S(2)}) %collective-permute-start.1) | collective-permute-done | bytes 65568 | tf_op jit(solution)/shard_map/ppermute | solution.py:154
  15.6 1.7 %collective-permute-done.2.a3.refs_3_ = bf16[2,128,128]{2,1,0:T(8,128)(2,1)S(1)} collective-permute-done((bf16[2,128,128]{2,1,0:T(8,128)(2,1)S(1)}, bf16[2,128,128]{2,1,0:T(8,128)(2,1)S(1)}, u32[]{:S(2)}, u32[]{:S(2)}) %collective-permute-start.2) | collective-permute-done | bytes 65568 | tf_op jit(solution)/shard_map/ppermute | solution.py:154
  17.4 3.5 %collective-permute-start.4 = (bf16[2,128,128]{2,1,0:T(8,128)(2,1)S(1)}, bf16[2,128,128]{2,1,0:T(8,128)(2,1)S(1)}, u32[]{:S(2)}, u32[]{:S(2)}) collective-permute-start(bf16[2,128,128]{2,1,0:T(8,128)(2,1)S(1)} %shard_map.56), channel_id=1, source_target_pairs={{0,8},{2,10},{4,12},{6,14},{8,16},{10,18},{12,20},{14,22},{16,24},... | collective-permute-start | bytes 196616 | tf_op jit(solution)/shard_map/ppermute | solution.py:160
  22.1 1.7 %collective-permute-start.10 = (bf16[128,1024]{1,0:T(8,128)(2,1)S(1)}, bf16[128,1024]{1,0:T(8,128)(2,1)S(1)}, u32[]{:S(2)}, u32[]{:S(2)}) collective-permute-start(bf16[128,1024]{1,0:T(8,128)(2,1)S(1)} %collective-permute-done.8.refs_2_), channel_id=1, source_target_pairs={{0,4},{2,6},{4,0},{6,2},{8,12},{10,14},{12,8},{14,10},{16,20},{18,... | collective-permute-start | bytes 786440 | tf_op jit(solution)/shard_map/ppermute | solution.py:154
  23.8 3.7 %collective-permute-start.5 = (bf16[2,128,128]{2,1,0:T(8,128)(2,1)S(1)}, bf16[2,128,128]{2,1,0:T(8,128)(2,1)S(1)}, u32[]{:S(2)}, u32[]{:S(2)}) collective-permute-start(bf16[2,128,128]{2,1,0:T(8,128)(2,1)S(1)} %add_convert_fusion.1), channel_id=1, source_target_pairs={{0,16},{2,18},{4,20},{6,22},{8,24},{10,26},{12,28},{14,30},{1,17},... | collective-permute-start | bytes 196616 | tf_op jit(solution)/shard_map/ppermute | solution.py:160
  27.5 2.5 %collective-permute-start.14 = (bf16[128,1024]{1,0:T(8,128)(2,1)S(1)}, bf16[128,1024]{1,0:T(8,128)(2,1)S(1)}, u32[]{:S(2)}, u32[]{:S(2)}) collective-permute-start(bf16[128,1024]{1,0:T(8,128)(2,1)S(1)} %collective-permute-done.3.refs_10_.refs_2_), channel_id=1, source_target_pairs={{0,8},{2,10},{4,12},{6,14},{8,16},{10,18},{12,20},{14,22},{16,24},... | collective-permute-start | bytes 786440 | tf_op jit(solution)/shard_map/ppermute | solution.py:157
  30.7 1.8 %collective-permute-done.9.refs_4_ = bf16[128,1024]{1,0:T(8,128)(2,1)S(1)} collective-permute-done((bf16[128,1024]{1,0:T(8,128)(2,1)S(1)}, bf16[128,1024]{1,0:T(8,128)(2,1)S(1)}, u32[]{:S(2)}, u32[]{:S(2)}) %collective-permute-start.9) | collective-permute-done | bytes 262176 | tf_op jit(solution)/shard_map/ppermute | solution.py:157
  33.4 2.4 %collective-permute-start.13 = (bf16[2,128,128]{2,1,0:T(8,128)(2,1)S(1)}, bf16[2,128,128]{2,1,0:T(8,128)(2,1)S(1)}, u32[]{:S(2)}, u32[]{:S(2)}) collective-permute-start(bf16[2,128,128]{2,1,0:T(8,128)(2,1)S(1)} %get-tuple-element.52), channel_id=1, source_target_pairs={{0,6},{2,4},{4,2},{6,0},{8,14},{10,12},{12,10},{14,8},{16,22},{18,... | collective-permute-start | bytes 196616 | tf_op jit(solution)/shard_map/ppermute | solution.py:154
  38.0 1.3 %collective-permute-done.13.c3 = bf16[2,128,128]{2,1,0:T(8,128)(2,1)S(1)} collective-permute-done((bf16[2,128,128]{2,1,0:T(8,128)(2,1)S(1)}, bf16[2,128,128]{2,1,0:T(8,128)(2,1)S(1)}, u32[]{:S(2)}, u32[]{:S(2)}) %collective-permute-start.13) | collective-permute-done | bytes 65568 | tf_op jit(solution)/shard_map/ppermute | solution.py:154
  43.7 1.3 %collective-permute-start.17 = (bf16[128,1024]{1,0:T(8,128)(2,1)S(1)}, bf16[128,1024]{1,0:T(8,128)(2,1)S(1)}, u32[]{:S(2)}, u32[]{:S(2)}) collective-permute-start(bf16[128,1024]{1,0:T(8,128)(2,1)S(1)} %collective-permute-done.9.refs_4_), channel_id=1, source_target_pairs={{0,4},{2,6},{4,0},{6,2},{8,12},{10,14},{12,8},{14,10},{16,20},{18,... | collective-permute-start | bytes 786440 | tf_op jit(solution)/shard_map/ppermute | solution.py:154
  45.8 1.7 %collective-permute-done.21.refs_14_.refs_6_ = bf16[128,1024]{1,0:T(8,128)(2,1)S(1)} collective-permute-done((bf16[128,1024]{1,0:T(8,128)(2,1)S(1)}, bf16[128,1024]{1,0:T(8,128)(2,1)S(1)}, u32[]{:S(2)}, u32[]{:S(2)}) %collective-permute-start.21) | collective-permute-done | bytes 262176 | tf_op jit(solution)/shard_map/ppermute | solution.py:157
  47.5 1.5 %collective-permute-start.19 = (bf16[128,1024]{1,0:T(8,128)(2,1)S(1)}, bf16[128,1024]{1,0:T(8,128)(2,1)S(1)}, u32[]{:S(2)}, u32[]{:S(2)}) collective-permute-start(bf16[128,1024]{1,0:T(8,128)(2,1)S(1)} %collective-permute-done.3.refs_10_.refs_2_), channel_id=1, source_target_pairs={{0,2},{2,0},{4,6},{6,4},{8,10},{10,8},{12,14},{14,12},{16,18},{18,... | collective-permute-start | bytes 786440 | tf_op jit(solution)/shard_map/ppermute | solution.py:154
  50.1 2.0 %collective-permute-done.17.refs_5_ = bf16[128,1024]{1,0:T(8,128)(2,1)S(1)} collective-permute-done((bf16[128,1024]{1,0:T(8,128)(2,1)S(1)}, bf16[128,1024]{1,0:T(8,128)(2,1)S(1)}, u32[]{:S(2)}, u32[]{:S(2)}) %collective-permute-start.17) | collective-permute-done | bytes 262176 | tf_op jit(solution)/shard_map/ppermute | solution.py:154
  52.9 1.4 %collective-permute-done.16.refs_8_ = bf16[256,512]{1,0:T(8,128)(2,1)S(1)} collective-permute-done((bf16[256,512]{1,0:T(8,128)(2,1)S(1)}, bf16[256,512]{1,0:T(8,128)(2,1)S(1)}, u32[]{:S(2)}, u32[]{:S(2)}) %collective-permute-start.16) | collective-permute-done | bytes 262176 | tf_op jit(solution)/shard_map/ppermute | solution.py:154
  54.2 4.1 %collective-permute-done.19.refs_11_.refs_3_ = bf16[128,1024]{1,0:T(8,128)(2,1)S(1)} collective-permute-done((bf16[128,1024]{1,0:T(8,128)(2,1)S(1)}, bf16[128,1024]{1,0:T(8,128)(2,1)S(1)}, u32[]{:S(2)}, u32[]{:S(2)}) %collective-permute-start.19) | collective-permute-done | bytes 262176 | tf_op jit(solution)/shard_map/ppermute | solution.py:154
  58.3 2.8 %collective-permute-done.23.refs_15_.refs_7_ = bf16[128,1024]{1,0:T(8,128)(2,1)S(1)} collective-permute-done((bf16[128,1024]{1,0:T(8,128)(2,1)S(1)}, bf16[128,1024]{1,0:T(8,128)(2,1)S(1)}, u32[]{:S(2)}, u32[]{:S(2)}) %collective-permute-start.23) | collective-permute-done | bytes 262176 | tf_op jit(solution)/shard_map/ppermute | solution.py:154
  63.5 1.3 %shard_map.61 = bf16[256,1024]{1,0:T(8,128)(2,1)S(1)} custom-call(s32[3]{0:T(128)S(1)} %pad_add_fusion.place, bf16[128,1024]{1,0:T(8,128)(2,1)S(1)} %get-tuple-element.70.refs_0_, bf16[128,1024]{1,0:T(8,128)(2,1)S(1)} %collective-permute-done.7.refs_1_, bf16[128,1024]{1,0:T(8,128)(2,1)S(1)} %collective-permute-done.8.refs_2_, ...), custom_call_target="tpu_custom_call" | custom-call | flops 536870912 | tf_op jit(solution)/shard_map/pallas_call | solution.py:243
  65.6 2.0 %shard_map.60 = f32[256,2048]{1,0:T(8,128)S(1)} custom-call(s32[3]{0:T(128)S(1)} %pad_add_fusion.place, bf16[128,1024]{1,0:T(8,128)(2,1)S(1)} %get-tuple-element.70.refs_0_, bf16[128,1024]{1,0:T(8,128)(2,1)S(1)} %collective-permute-done.7.refs_1_, bf16[128,1024]{1,0:T(8,128)(2,1)S(1)} %collective-permute-done.8.refs_2_, ...), custom_call_target="tpu_custom_call" | custom-call | flops 1073741824 | tf_op jit(solution)/shard_map/pallas_call | solution.py:250
  67.6 6.4 %collective-permute-done.28 = bf16[256,1024]{1,0:T(8,128)(2,1)S(1)} collective-permute-done((bf16[256,1024]{1,0:T(8,128)(2,1)S(1)}, bf16[256,1024]{1,0:T(8,128)(2,1)S(1)}, u32[]{:S(2)}, u32[]{:S(2)}) %collective-permute-start.28) | collective-permute-done | bytes 524320 | tf_op jit(solution)/shard_map/ppermute | solution.py:154
  74.0 2.1 %collective-permute-done.26 = bf16[256,1024]{1,0:T(8,128)(2,1)S(1)} collective-permute-done((bf16[256,1024]{1,0:T(8,128)(2,1)S(1)}, bf16[256,1024]{1,0:T(8,128)(2,1)S(1)}, u32[]{:S(2)}, u32[]{:S(2)}) %collective-permute-start.26) | collective-permute-done | bytes 524320 | tf_op jit(solution)/shard_map/ppermute | solution.py:154
  (58 shorter events, 22.4 us)
Async XLA Ops:
  1.2 16.2 %collective-permute-start.3 = (bf16[128,1024]{1,0:T(8,128)(2,1)S(1)}, bf16[128,1024]{1,0:T(8,128)(2,1)S(1)}, u32[]{:S(2)}, u32[]{:S(2)}) collective-permute-start(bf16[128,1024]{1,0:T(8,128)(2,1)S(1)} %get-tuple-element.69.refs_8_.refs_0_), channel_id=1, source_target_pairs={{0,8},{2,10},{4,12},{6,14},{8,16},{10,18},{12,20},{14,22},{16,24},... | collective-permute-start | bytes 786440 | tf_op jit(solution)/shard_map/ppermute | solution.py:157
  4.2 17.8 %collective-permute-start.8 = (bf16[128,1024]{1,0:T(8,128)(2,1)S(1)}, bf16[128,1024]{1,0:T(8,128)(2,1)S(1)}, u32[]{:S(2)}, u32[]{:S(2)}) collective-permute-start(bf16[128,1024]{1,0:T(8,128)(2,1)S(1)} %get-tuple-element.70.refs_0_), channel_id=1, source_target_pairs={{0,8},{2,10},{4,12},{6,14},{8,16},{10,18},{12,20},{14,22},{16,24},... | collective-permute-start | bytes 786440 | tf_op jit(solution)/shard_map/ppermute | solution.py:157
  17.4 6.4 %collective-permute-start.4 = (bf16[2,128,128]{2,1,0:T(8,128)(2,1)S(1)}, bf16[2,128,128]{2,1,0:T(8,128)(2,1)S(1)}, u32[]{:S(2)}, u32[]{:S(2)}) collective-permute-start(bf16[2,128,128]{2,1,0:T(8,128)(2,1)S(1)} %shard_map.56), channel_id=1, source_target_pairs={{0,8},{2,10},{4,12},{6,14},{8,16},{10,18},{12,20},{14,22},{16,24},... | collective-permute-start | bytes 196616 | tf_op jit(solution)/shard_map/ppermute | solution.py:160
  20.9 6.6 %collective-permute-start.6 = (bf16[128,1024]{1,0:T(8,128)(2,1)S(1)}, bf16[128,1024]{1,0:T(8,128)(2,1)S(1)}, u32[]{:S(2)}, u32[]{:S(2)}) collective-permute-start(bf16[128,1024]{1,0:T(8,128)(2,1)S(1)} %get-tuple-element.69.refs_8_.refs_0_), channel_id=1, source_target_pairs={{0,2},{2,0},{4,6},{6,4},{8,10},{10,8},{12,14},{14,12},{16,18},{18,... | collective-permute-start | bytes 786440 | tf_op jit(solution)/shard_map/ppermute | solution.py:154
  21.5 8.5 %collective-permute-start.7 = (bf16[128,1024]{1,0:T(8,128)(2,1)S(1)}, bf16[128,1024]{1,0:T(8,128)(2,1)S(1)}, u32[]{:S(2)}, u32[]{:S(2)}) collective-permute-start(bf16[128,1024]{1,0:T(8,128)(2,1)S(1)} %get-tuple-element.70.refs_0_), channel_id=1, source_target_pairs={{0,4},{2,6},{4,0},{6,2},{8,12},{10,14},{12,8},{14,10},{16,20},{18,... | collective-permute-start | bytes 786440 | tf_op jit(solution)/shard_map/ppermute | solution.py:154
  22.0 10.4 %collective-permute-start.9 = (bf16[128,1024]{1,0:T(8,128)(2,1)S(1)}, bf16[128,1024]{1,0:T(8,128)(2,1)S(1)}, u32[]{:S(2)}, u32[]{:S(2)}) collective-permute-start(bf16[128,1024]{1,0:T(8,128)(2,1)S(1)} %collective-permute-done.8.refs_2_), channel_id=1, source_target_pairs={{0,8},{2,10},{4,12},{6,14},{8,16},{10,18},{12,20},{14,22},{16,24},... | collective-permute-start | bytes 786440 | tf_op jit(solution)/shard_map/ppermute | solution.py:157
  22.1 11.1 %collective-permute-start.10 = (bf16[128,1024]{1,0:T(8,128)(2,1)S(1)}, bf16[128,1024]{1,0:T(8,128)(2,1)S(1)}, u32[]{:S(2)}, u32[]{:S(2)}) collective-permute-start(bf16[128,1024]{1,0:T(8,128)(2,1)S(1)} %collective-permute-done.8.refs_2_), channel_id=1, source_target_pairs={{0,4},{2,6},{4,0},{6,2},{8,12},{10,14},{12,8},{14,10},{16,20},{18,... | collective-permute-start | bytes 786440 | tf_op jit(solution)/shard_map/ppermute | solution.py:154
  23.8 6.2 %collective-permute-start.5 = (bf16[2,128,128]{2,1,0:T(8,128)(2,1)S(1)}, bf16[2,128,128]{2,1,0:T(8,128)(2,1)S(1)}, u32[]{:S(2)}, u32[]{:S(2)}) collective-permute-start(bf16[2,128,128]{2,1,0:T(8,128)(2,1)S(1)} %add_convert_fusion.1), channel_id=1, source_target_pairs={{0,16},{2,18},{4,20},{6,22},{8,24},{10,26},{12,28},{14,30},{1,17},... | collective-permute-start | bytes 196616 | tf_op jit(solution)/shard_map/ppermute | solution.py:160
  27.5 11.8 %collective-permute-start.14 = (bf16[128,1024]{1,0:T(8,128)(2,1)S(1)}, bf16[128,1024]{1,0:T(8,128)(2,1)S(1)}, u32[]{:S(2)}, u32[]{:S(2)}) collective-permute-start(bf16[128,1024]{1,0:T(8,128)(2,1)S(1)} %collective-permute-done.3.refs_10_.refs_2_), channel_id=1, source_target_pairs={{0,8},{2,10},{4,12},{6,14},{8,16},{10,18},{12,20},{14,22},{16,24},... | collective-permute-start | bytes 786440 | tf_op jit(solution)/shard_map/ppermute | solution.py:157
  33.2 11.8 %collective-permute-start.15 = (bf16[128,1024]{1,0:T(8,128)(2,1)S(1)}, bf16[128,1024]{1,0:T(8,128)(2,1)S(1)}, u32[]{:S(2)}, u32[]{:S(2)}) collective-permute-start(bf16[128,1024]{1,0:T(8,128)(2,1)S(1)} %collective-permute-done.9.refs_4_), channel_id=1, source_target_pairs={{0,8},{2,10},{4,12},{6,14},{8,16},{10,18},{12,20},{14,22},{16,24},... | collective-permute-start | bytes 786440 | tf_op jit(solution)/shard_map/ppermute | solution.py:157
  33.4 5.8 %collective-permute-start.13 = (bf16[2,128,128]{2,1,0:T(8,128)(2,1)S(1)}, bf16[2,128,128]{2,1,0:T(8,128)(2,1)S(1)}, u32[]{:S(2)}, u32[]{:S(2)}) collective-permute-start(bf16[2,128,128]{2,1,0:T(8,128)(2,1)S(1)} %get-tuple-element.52), channel_id=1, source_target_pairs={{0,6},{2,4},{4,2},{6,0},{8,14},{10,12},{12,10},{14,8},{16,22},{18,... | collective-permute-start | bytes 196616 | tf_op jit(solution)/shard_map/ppermute | solution.py:154
  39.3 8.2 %collective-permute-start.21 = (bf16[128,1024]{1,0:T(8,128)(2,1)S(1)}, bf16[128,1024]{1,0:T(8,128)(2,1)S(1)}, u32[]{:S(2)}, u32[]{:S(2)}) collective-permute-start(bf16[128,1024]{1,0:T(8,128)(2,1)S(1)} %collective-permute-done.14.refs_12_.refs_4_), channel_id=1, source_target_pairs={{0,8},{2,10},{4,12},{6,14},{8,16},{10,18},{12,20},{14,22},{16,24},... | collective-permute-start | bytes 786440 | tf_op jit(solution)/shard_map/ppermute | solution.py:157
  40.4 8.6 %collective-permute-start.22 = (bf16[128,1024]{1,0:T(8,128)(2,1)S(1)}, bf16[128,1024]{1,0:T(8,128)(2,1)S(1)}, u32[]{:S(2)}, u32[]{:S(2)}) collective-permute-start(bf16[128,1024]{1,0:T(8,128)(2,1)S(1)} %collective-permute-done.14.refs_12_.refs_4_), channel_id=1, source_target_pairs={{0,2},{2,0},{4,6},{6,4},{8,10},{10,8},{12,14},{14,12},{16,18},{18,... | collective-permute-start | bytes 786440 | tf_op jit(solution)/shard_map/ppermute | solution.py:154
  42.9 6.4 %collective-permute-start.20 = (bf16[256,512]{1,0:T(8,128)(2,1)S(1)}, bf16[256,512]{1,0:T(8,128)(2,1)S(1)}, u32[]{:S(2)}, u32[]{:S(2)}) collective-permute-start(bf16[256,512]{1,0:T(8,128)(2,1)S(1)} %get-tuple-element.63), channel_id=1, source_target_pairs={{0,4},{2,6},{4,0},{6,2},{8,12},{10,14},{12,8},{14,10},{16,20},{18,... | collective-permute-start | bytes 786440 | tf_op jit(solution)/shard_map/ppermute | solution.py:154
  43.7 8.4 %collective-permute-start.17 = (bf16[128,1024]{1,0:T(8,128)(2,1)S(1)}, bf16[128,1024]{1,0:T(8,128)(2,1)S(1)}, u32[]{:S(2)}, u32[]{:S(2)}) collective-permute-start(bf16[128,1024]{1,0:T(8,128)(2,1)S(1)} %collective-permute-done.9.refs_4_), channel_id=1, source_target_pairs={{0,4},{2,6},{4,0},{6,2},{8,12},{10,14},{12,8},{14,10},{16,20},{18,... | collective-permute-start | bytes 786440 | tf_op jit(solution)/shard_map/ppermute | solution.py:154
  45.0 9.2 %collective-permute-start.16 = (bf16[256,512]{1,0:T(8,128)(2,1)S(1)}, bf16[256,512]{1,0:T(8,128)(2,1)S(1)}, u32[]{:S(2)}, u32[]{:S(2)}) collective-permute-start(bf16[256,512]{1,0:T(8,128)(2,1)S(1)} %get-tuple-element.58), channel_id=1, source_target_pairs={{0,2},{2,0},{4,6},{6,4},{8,10},{10,8},{12,14},{14,12},{16,18},{18,... | collective-permute-start | bytes 786440 | tf_op jit(solution)/shard_map/ppermute | solution.py:154
  47.5 10.8 %collective-permute-start.19 = (bf16[128,1024]{1,0:T(8,128)(2,1)S(1)}, bf16[128,1024]{1,0:T(8,128)(2,1)S(1)}, u32[]{:S(2)}, u32[]{:S(2)}) collective-permute-start(bf16[128,1024]{1,0:T(8,128)(2,1)S(1)} %collective-permute-done.3.refs_10_.refs_2_), channel_id=1, source_target_pairs={{0,2},{2,0},{4,6},{6,4},{8,10},{10,8},{12,14},{14,12},{16,18},{18,... | collective-permute-start | bytes 786440 | tf_op jit(solution)/shard_map/ppermute | solution.py:154
  49.3 11.8 %collective-permute-start.23 = (bf16[128,1024]{1,0:T(8,128)(2,1)S(1)}, bf16[128,1024]{1,0:T(8,128)(2,1)S(1)}, u32[]{:S(2)}, u32[]{:S(2)}) collective-permute-start(bf16[128,1024]{1,0:T(8,128)(2,1)S(1)} %collective-permute-done.21.refs_14_.refs_6_), channel_id=1, source_target_pairs={{0,2},{2,0},{4,6},{6,4},{8,10},{10,8},{12,14},{14,12},{16,18},{18,... | collective-permute-start | bytes 786440 | tf_op jit(solution)/shard_map/ppermute | solution.py:154
  50.1 11.0 %collective-permute-start.27 = (bf16[256,512]{1,0:T(8,128)(2,1)S(1)}, bf16[256,512]{1,0:T(8,128)(2,1)S(1)}, u32[]{:S(2)}, u32[]{:S(2)}) collective-permute-start(bf16[256,512]{1,0:T(8,128)(2,1)S(1)} %collective-permute-done.20.refs_8_), channel_id=1, source_target_pairs={{0,1},{1,0},{2,3},{3,2},{4,5},{5,4},{6,7},{7,6},{8,9},{9,8},{10,11... | collective-permute-start | bytes 786440 | tf_op jit(solution)/shard_map/ppermute | solution.py:163
  52.1 11.3 %collective-permute-start.18 = (bf16[128,1024]{1,0:T(8,128)(2,1)S(1)}, bf16[128,1024]{1,0:T(8,128)(2,1)S(1)}, u32[]{:S(2)}, u32[]{:S(2)}) collective-permute-start(bf16[128,1024]{1,0:T(8,128)(2,1)S(1)} %collective-permute-done.15.refs_6_), channel_id=1, source_target_pairs={{0,4},{2,6},{4,0},{6,2},{8,12},{10,14},{12,8},{14,10},{16,20},{18,... | collective-permute-start | bytes 786440 | tf_op jit(solution)/shard_map/ppermute | solution.py:154
  54.2 9.2 %collective-permute-start.25 = (bf16[256,512]{1,0:T(8,128)(2,1)S(1)}, bf16[256,512]{1,0:T(8,128)(2,1)S(1)}, u32[]{:S(2)}, u32[]{:S(2)}) collective-permute-start(bf16[256,512]{1,0:T(8,128)(2,1)S(1)} %collective-permute-done.16.refs_8_), channel_id=1, source_target_pairs={{0,1},{1,0},{2,3},{3,2},{4,5},{5,4},{6,7},{7,6},{8,9},{9,8},{10,11... | collective-permute-start | bytes 786440 | tf_op jit(solution)/shard_map/ppermute | solution.py:163
  58.3 7.3 %collective-permute-start.24 = (bf16[256,1024]{1,0:T(8,128)(2,1)S(1)}, bf16[256,1024]{1,0:T(8,128)(2,1)S(1)}, u32[]{:S(2)}, u32[]{:S(2)}) collective-permute-start(bf16[256,1024]{1,0:T(8,128)(2,1)S(1)} %get-tuple-element.66.refs_16_), channel_id=1, source_target_pairs={{0,1},{1,0},{2,3},{3,2},{4,5},{5,4},{6,7},{7,6},{8,9},{9,8},{10,11... | collective-permute-start | bytes 1572872 | tf_op jit(solution)/shard_map/ppermute | solution.py:163
  62.4 11.6 %collective-permute-start.28 = (bf16[256,1024]{1,0:T(8,128)(2,1)S(1)}, bf16[256,1024]{1,0:T(8,128)(2,1)S(1)}, u32[]{:S(2)}, u32[]{:S(2)}) collective-permute-start(bf16[256,1024]{1,0:T(8,128)(2,1)S(1)} %shard_map.62), channel_id=1, source_target_pairs={{0,4},{2,6},{4,0},{6,2},{8,12},{10,14},{12,8},{14,10},{16,20},{18,... | collective-permute-start | bytes 1572872 | tf_op jit(solution)/shard_map/ppermute | solution.py:154
  64.7 11.3 %collective-permute-start.26 = (bf16[256,1024]{1,0:T(8,128)(2,1)S(1)}, bf16[256,1024]{1,0:T(8,128)(2,1)S(1)}, u32[]{:S(2)}, u32[]{:S(2)}) collective-permute-start(bf16[256,1024]{1,0:T(8,128)(2,1)S(1)} %shard_map.61), channel_id=1, source_target_pairs={{0,2},{2,0},{4,6},{6,4},{8,10},{10,8},{12,14},{14,12},{16,18},{18,... | collective-permute-start | bytes 1572872 | tf_op jit(solution)/shard_map/ppermute | solution.py:154
  (11 other events, 172.1 us)

commit v3 on v2

--- a/solution.py
+++ b/solution.py
@@ -131,10 +131,52 @@
     out[:, cut:] = sums(place, refs[8:16], own, other, ways[1], 1, False)
 
 
+def cut_kernel(block, first, second, sems):
+    width = first.shape[1]
+    copies = [
+        pltpu.make_async_copy(block.at[:, pl.ds(0, width)], first, sems.at[0]),
+        pltpu.make_async_copy(block.at[:, pl.ds(width, second.shape[1])], second, sems.at[1]),
+    ]
+    for copy in copies:
+        copy.start()
+    for copy in copies:
+        copy.wait()
+
+
+def finish_kernel(at, mine, part, *refs):
+    out, held, sems = refs[-3:]
+    rows, width = part.shape
+    step = rows // 4
+    copies = []
+    for i in range(4):
+        these = slice(i * step, (i + 1) * step)
+        held[these] = (mine[these, at:at + width] + part[these].astype(F32)).astype(BF16)
+        copies.append(
+            pltpu.make_async_copy(
+                held.at[pl.ds(i * step, step)], out.at[pl.ds(i * step, step), pl.ds(at, width)], sems.at[i]
+            )
+        )
+        copies[-1].start()
+    for copy in copies:
+        copy.wait()
+
+
+def finish(mine, part, at, result):
+    return pl.pallas_call(
+        functools.partial(finish_kernel, at),
+        out_shape=shape(mine.shape, BF16),
+        in_specs=[VMEM] * 2 + ([ANY] if result is not None else []),
+        out_specs=ANY,
+        scratch_shapes=[pltpu.VMEM(part.shape, BF16), pltpu.SemaphoreType.DMA((4,))],
+        input_output_aliases={2: 0} if result is not None else {},
+        compiler_params=pltpu.CompilerParams(vmem_limit_bytes=VMEM_LIMIT),
+    )(*([mine, part] + ([result] if result is not None else [])))
+
+
 CUT = 8
 ZD = 0
 BD = 0
-TIES = {'tot': '', 'z1': 'b1', 'z2': '', 'add': 'x0 y0', 'back': 'a2 y1', 'norm': 'b2', 'act': 'a3', 'act2': 'y2', 'act3': 'b3 x2'}
+TIES = {'tot': '', 'z1': 'y0', 'z2': '', 'add': 'x0', 'back': 'a2 x1 y1', 'norm': '', 'act': 'a3', 'act2': 'y3', 'act3': 'b3'}
 
 
 def tie(value, *others):
@@ -168,7 +210,16 @@
 
     def piece(n):
         if n not in held:
-            if n[0] in "ab":
+            if n == "r1":
+                held[n] = ring(w_out)
+            elif n in ("a1", "b1"):
+                held["a1"], held["b1"] = call(
+                    cut_kernel,
+                    [shape((HD, half), BF16), shape((HD, cols - half), BF16)],
+                    [ANY],
+                    [pltpu.SemaphoreType.DMA((2,))],
+                )(piece("r1"))
+            elif n[0] in "ab":
                 held[n] = ring(piece(n[0] + str(int(n[1]) - 1)), -1 if BD and n[0] == "b" else 1)
             else:
                 held[n] = partner(piece({"x": "b", "y": "a"}[n[0]] + n[1]), {"x": 1, "y": 2}[n[0]])
@@ -253,8 +304,10 @@
         [SMEM] + [VMEM] * 18,
         flops=rows * feats * cols * 2,
     )(place, *wa, *wb, normed, other)
-    theirs = jnp.concatenate(parts, axis=1)
-    return (mine_all + theirs.astype(F32)).astype(BF16)
+    result = None
+    for at, part in ((half, parts[1]), (0, parts[0])):
+        result = finish(mine_all, part, at, result)
+    return result
 
 
 def solution(mesh):

time: 78 us -> 73.2 us (0.938)
  waiting for transfers between devices: 29.3 us -> 25.6 us
  Pallas kernels: 8.67 us -> 10.4 us
  other arithmetic: 1.36 us -> 0.1 us
  starting transfers between devices: 34.6 us -> 33.5 us
    ppermute x18, waiting for transfers between devices: 25.8 us -> 21.2 us  [partner(): return lax.ppermute(value, 'seq', [(i, i ^ flip) for i in range(blocks)])]
    pallas_call x0 -> x3, Pallas kernels: none -> 1.76 us  [the longest x2 1.7 us: finish(): pl.pallas_call(functools.partial(finish_kernel, at), out_shape=shape(mine...]
    ppermute x2, starting transfers between devices: 7.14 us -> 5.82 us  [up(): lax.ppermute(value, 'seq', [(i, i + by * PLANE) for i in range(blocks - b...]
    convert_element_type x1 -> x0, other arithmetic: 1.26 us -> none  [per_device(): return (mine_all + theirs.astype(F32)).astype(BF16)]
    ppermute x18, starting transfers between devices: 18.9 us -> 19.9 us  [partner(): return lax.ppermute(value, 'seq', [(i, i ^ flip) for i in range(blocks)])]
    ppermute x6 -> x5, waiting for transfers between devices: 3.43 us -> 4.33 us  [ring(): lax.ppermute(value, 'seq', [(i, (i + way * PLANE) % blocks) for i in rang...]
    ppermute x6 -> x5, starting transfers between devices: 8.58 us -> 7.74 us  [ring(): lax.ppermute(value, 'seq', [(i, (i + way * PLANE) % blocks) for i in rang...]
  transfers between devices with their start and end apart: 29 -> 28, of which waited for: 15 -> 15; matrix products, arithmetic and copies ran while one was open for 0% -> 2% of each run, Pallas kernels for 11% -> 13%
where the time goes in v3:
time: 73.2 us; the launch traced here: 72.9 us
  starting transfers between devices  33.5 us (46%)
  waiting for transfers between devices  25.6 us (35%)
  Pallas kernels  10.4 us (14%)
  local copies, waits for them, and re-layouts  3.16 us (4%)
    ppermute x18, waiting for transfers between devices, partner(): return lax.ppermute(value, 'seq', [(i, i ^ flip) for i in range(blocks)])  21.2 us
    ppermute x18, starting transfers between devices, partner(): return lax.ppermute(value, 'seq', [(i, i ^ flip) for i in range(blocks)])  19.9 us
    ppermute x5, starting transfers between devices, ring(): lax.ppermute(value, 'seq', [(i, (i + way * PLANE) % blocks) for i in rang...  7.74 us
    ppermute x2, starting transfers between devices, up(): lax.ppermute(value, 'seq', [(i, i + by * PLANE) for i in range(blocks - b...  5.82 us
    ppermute x5, waiting for transfers between devices, ring(): lax.ppermute(value, 'seq', [(i, (i + way * PLANE) % blocks) for i in rang...  4.33 us
    pallas_call x2, Pallas kernels, per_device(): call(functools.partial(partner_kernel, way, flip), [shape((rows, width),...  2.57 us
    unnamed x12, local copies, waits for them, and re-layouts  2.1 us
    pallas_call x1, Pallas kernels, per_device(): call(functools.partial(own_kernel, ways), [shape((rows, cols), F32)], [SM...  1.95 us
  transfers between devices with their start and end apart: 28, of which 15 were waited for; matrix products, arithmetic and copies ran while one was open for 2% of the time, Pallas kernels for 13%

profile of v3, /device:TPU:0, one launch (start us, length us, event | category | flops | bytes accessed | tf_op | source)
XLA Modules:
  0.0 72.9 jit_solution(15194466214524735745)
XLA Ops:
  0.0 3.0 %collective-permute-start.4 = (bf16[128,2048]{1,0:T(8,128)(2,1)}, bf16[128,2048]{1,0:T(8,128)(2,1)S(1)}, u32[]{:S(2)}, u32[]{:S(2)}) collective-permute-start(bf16[128,2048]{1,0:T(8,128)(2,1)} %param.9), channel_id=1, source_target_pairs={{0,8},{2,10},{4,12},{6,14},{8,16},{10,18},{12,20},{14,22},{16,24},... | collective-permute-start | bytes 1572872 | tf_op jit(solution)/shard_map/ppermute | solution.py:199
  4.1 1.6 %collective-permute-start.3 = (bf16[128,1024]{1,0:T(8,128)(2,1)S(1)}, bf16[128,1024]{1,0:T(8,128)(2,1)S(1)}, u32[]{:S(2)}, u32[]{:S(2)}) collective-permute-start(bf16[128,1024]{1,0:T(8,128)(2,1)S(1)} %get-tuple-element.68.refs_0_), channel_id=1, source_target_pairs={{0,4},{2,6},{4,0},{6,2},{8,12},{10,14},{12,8},{14,10},{16,20},{18,... | collective-permute-start | bytes 786440 | tf_op jit(solution)/shard_map/ppermute | solution.py:196
  9.0 1.6 %collective-permute-start = (bf16[2,128,128]{2,1,0:T(8,128)(2,1)S(1)}, bf16[2,128,128]{2,1,0:T(8,128)(2,1)S(1)}, u32[]{:S(2)}, u32[]{:S(2)}) collective-permute-start(bf16[2,128,128]{2,1,0:T(8,128)(2,1)S(1)} %get-tuple-element.37), channel_id=1, source_target_pairs={{0,2},{2,0},{4,6},{6,4},{8,10},{10,8},{12,14},{14,12},{16,18},{18,... | collective-permute-start | bytes 196616 | tf_op jit(solution)/shard_map/ppermute | solution.py:196
  11.0 1.5 %collective-permute-start.2 = (bf16[2,128,128]{2,1,0:T(8,128)(2,1)S(1)}, bf16[2,128,128]{2,1,0:T(8,128)(2,1)S(1)}, u32[]{:S(2)}, u32[]{:S(2)}) collective-permute-start(bf16[2,128,128]{2,1,0:T(8,128)(2,1)S(1)} %get-tuple-element.39), channel_id=1, source_target_pairs={{0,6},{2,4},{4,2},{6,0},{8,14},{10,12},{12,10},{14,8},{16,22},{18,... | collective-permute-start | bytes 196616 | tf_op jit(solution)/shard_map/ppermute | solution.py:196
  13.4 1.4 %collective-permute-done.1.a2.refs_2_ = bf16[2,128,128]{2,1,0:T(8,128)(2,1)S(1)} collective-permute-done((bf16[2,128,128]{2,1,0:T(8,128)(2,1)S(1)}, bf16[2,128,128]{2,1,0:T(8,128)(2,1)S(1)}, u32[]{:S(2)}, u32[]{:S(2)}) %collective-permute-start.1) | collective-permute-done | bytes 65568 | tf_op jit(solution)/shard_map/ppermute | solution.py:196
  14.8 1.4 %collective-permute-done.2.a3.refs_3_ = bf16[2,128,128]{2,1,0:T(8,128)(2,1)S(1)} collective-permute-done((bf16[2,128,128]{2,1,0:T(8,128)(2,1)S(1)}, bf16[2,128,128]{2,1,0:T(8,128)(2,1)S(1)}, u32[]{:S(2)}, u32[]{:S(2)}) %collective-permute-start.2) | collective-permute-done | bytes 65568 | tf_op jit(solution)/shard_map/ppermute | solution.py:196
  16.3 3.5 %collective-permute-start.5 = (bf16[2,128,128]{2,1,0:T(8,128)(2,1)S(1)}, bf16[2,128,128]{2,1,0:T(8,128)(2,1)S(1)}, u32[]{:S(2)}, u32[]{:S(2)}) collective-permute-start(bf16[2,128,128]{2,1,0:T(8,128)(2,1)S(1)} %shard_map.56), channel_id=1, source_target_pairs={{0,8},{2,10},{4,12},{6,14},{8,16},{10,18},{12,20},{14,22},{16,24},... | collective-permute-start | bytes 196616 | tf_op jit(solution)/shard_map/ppermute | solution.py:202
  20.4 1.6 %collective-permute-start.8 = (bf16[128,1024]{1,0:T(8,128)(2,1)S(1)}, bf16[128,1024]{1,0:T(8,128)(2,1)S(1)}, u32[]{:S(2)}, u32[]{:S(2)}) collective-permute-start(bf16[128,1024]{1,0:T(8,128)(2,1)S(1)} %get-tuple-element.41.refs_2_), channel_id=1, source_target_pairs={{0,8},{2,10},{4,12},{6,14},{8,16},{10,18},{12,20},{14,22},{16,24},... | collective-permute-start | bytes 786440 | tf_op jit(solution)/shard_map/ppermute | solution.py:199
  22.1 1.5 %collective-permute-start.10 = (bf16[128,1024]{1,0:T(8,128)(2,1)S(1)}, bf16[128,1024]{1,0:T(8,128)(2,1)S(1)}, u32[]{:S(2)}, u32[]{:S(2)}) collective-permute-start(bf16[128,1024]{1,0:T(8,128)(2,1)S(1)} %get-tuple-element.41.refs_2_), channel_id=1, source_target_pairs={{0,4},{2,6},{4,0},{6,2},{8,12},{10,14},{12,8},{14,10},{16,20},{18,... | collective-permute-start | bytes 786440 | tf_op jit(solution)/shard_map/ppermute | solution.py:196
  23.6 1.5 %collective-permute-start.9 = (bf16[128,1024]{1,0:T(8,128)(2,1)S(1)}, bf16[128,1024]{1,0:T(8,128)(2,1)S(1)}, u32[]{:S(2)}, u32[]{:S(2)}) collective-permute-start(bf16[128,1024]{1,0:T(8,128)(2,1)S(1)} %get-tuple-element.45.refs_10_.refs_2_), channel_id=1, source_target_pairs={{0,2},{2,0},{4,6},{6,4},{8,10},{10,8},{12,14},{14,12},{16,18},{18,... | collective-permute-start | bytes 786440 | tf_op jit(solution)/shard_map/ppermute | solution.py:196
  25.1 2.3 %collective-permute-start.6 = (bf16[2,128,128]{2,1,0:T(8,128)(2,1)S(1)}, bf16[2,128,128]{2,1,0:T(8,128)(2,1)S(1)}, u32[]{:S(2)}, u32[]{:S(2)}) collective-permute-start(bf16[2,128,128]{2,1,0:T(8,128)(2,1)S(1)} %add_convert_fusion), channel_id=1, source_target_pairs={{0,16},{2,18},{4,20},{6,22},{8,24},{10,26},{12,28},{14,30},{1,17},... | collective-permute-start | bytes 196616 | tf_op jit(solution)/shard_map/ppermute | solution.py:202
  31.5 1.9 %collective-permute-start.15 = (bf16[128,1024]{1,0:T(8,128)(2,1)S(1)}, bf16[128,1024]{1,0:T(8,128)(2,1)S(1)}, u32[]{:S(2)}, u32[]{:S(2)}) collective-permute-start(bf16[128,1024]{1,0:T(8,128)(2,1)S(1)} %collective-permute-done.8.refs_4_), channel_id=1, source_target_pairs={{0,8},{2,10},{4,12},{6,14},{8,16},{10,18},{12,20},{14,22},{16,24},... | collective-permute-start | bytes 786440 | tf_op jit(solution)/shard_map/ppermute | solution.py:199
  35.6 1.3 %collective-permute-start.12 = (bf16[2,128,128]{2,1,0:T(8,128)(2,1)S(1)}, bf16[2,128,128]{2,1,0:T(8,128)(2,1)S(1)}, u32[]{:S(2)}, u32[]{:S(2)}) collective-permute-start(bf16[2,128,128]{2,1,0:T(8,128)(2,1)S(1)} %get-tuple-element.51), channel_id=1, source_target_pairs={{0,2},{2,0},{4,6},{6,4},{8,10},{10,8},{12,14},{14,12},{16,18},{18,... | collective-permute-start | bytes 196616 | tf_op jit(solution)/shard_map/ppermute | solution.py:196
  37.9 1.8 %collective-permute-done.18.refs_12_.refs_4_ = bf16[128,1024]{1,0:T(8,128)(2,1)S(1)} collective-permute-done((bf16[128,1024]{1,0:T(8,128)(2,1)S(1)}, bf16[128,1024]{1,0:T(8,128)(2,1)S(1)}, u32[]{:S(2)}, u32[]{:S(2)}) %collective-permute-start.18) | collective-permute-done | bytes 262176 | tf_op jit(solution)/shard_map/ppermute | solution.py:199
  41.1 1.6 %collective-permute-start.20 = (bf16[256,512]{1,0:T(8,128)(2,1)S(1)}, bf16[256,512]{1,0:T(8,128)(2,1)S(1)}, u32[]{:S(2)}, u32[]{:S(2)}) collective-permute-start(bf16[256,512]{1,0:T(8,128)(2,1)S(1)} %get-tuple-element.62), channel_id=1, source_target_pairs={{0,4},{2,6},{4,0},{6,2},{8,12},{10,14},{12,8},{14,10},{16,20},{18,... | collective-permute-start | bytes 786440 | tf_op jit(solution)/shard_map/ppermute | solution.py:196
  42.8 1.4 %collective-permute-done.15.refs_6_ = bf16[128,1024]{1,0:T(8,128)(2,1)S(1)} collective-permute-done((bf16[128,1024]{1,0:T(8,128)(2,1)S(1)}, bf16[128,1024]{1,0:T(8,128)(2,1)S(1)}, u32[]{:S(2)}, u32[]{:S(2)}) %collective-permute-start.15) | collective-permute-done | bytes 262176 | tf_op jit(solution)/shard_map/ppermute | solution.py:199
  44.2 1.4 %collective-permute-start.16 = (bf16[256,512]{1,0:T(8,128)(2,1)S(1)}, bf16[256,512]{1,0:T(8,128)(2,1)S(1)}, u32[]{:S(2)}, u32[]{:S(2)}) collective-permute-start(bf16[256,512]{1,0:T(8,128)(2,1)S(1)} %get-tuple-element.58), channel_id=1, source_target_pairs={{0,2},{2,0},{4,6},{6,4},{8,10},{10,8},{12,14},{14,12},{16,18},{18,... | collective-permute-start | bytes 786440 | tf_op jit(solution)/shard_map/ppermute | solution.py:196
  48.9 3.0 %collective-permute-done.16.refs_8_ = bf16[256,512]{1,0:T(8,128)(2,1)S(1)} collective-permute-done((bf16[256,512]{1,0:T(8,128)(2,1)S(1)}, bf16[256,512]{1,0:T(8,128)(2,1)S(1)}, u32[]{:S(2)}, u32[]{:S(2)}) %collective-permute-start.16) | collective-permute-done | bytes 262176 | tf_op jit(solution)/shard_map/ppermute | solution.py:196
  52.5 2.2 %collective-permute-done.19.refs_13_.refs_5_ = bf16[128,1024]{1,0:T(8,128)(2,1)S(1)} collective-permute-done((bf16[128,1024]{1,0:T(8,128)(2,1)S(1)}, bf16[128,1024]{1,0:T(8,128)(2,1)S(1)}, u32[]{:S(2)}, u32[]{:S(2)}) %collective-permute-start.19) | collective-permute-done | bytes 262176 | tf_op jit(solution)/shard_map/ppermute | solution.py:196
  54.7 2.8 %collective-permute-done.22.refs_15_.refs_7_ = bf16[128,1024]{1,0:T(8,128)(2,1)S(1)} collective-permute-done((bf16[128,1024]{1,0:T(8,128)(2,1)S(1)}, bf16[128,1024]{1,0:T(8,128)(2,1)S(1)}, u32[]{:S(2)}, u32[]{:S(2)}) %collective-permute-start.22) | collective-permute-done | bytes 262176 | tf_op jit(solution)/shard_map/ppermute | solution.py:196
  57.5 1.3 %shard_map.63 = bf16[256,1024]{1,0:T(8,128)(2,1)S(1)} custom-call(s32[3]{0:T(128)S(1)} %pad_add_fusion.place, bf16[128,1024]{1,0:T(8,128)(2,1)S(1)} %get-tuple-element.67.refs_8_.refs_0_, bf16[128,1024]{1,0:T(8,128)(2,1)S(1)} %collective-permute-done.7.refs_9_.refs_1_, bf16[128,1024]{1,0:T(8,128)(2,1)S(1)} %get-tuple-element.45.refs_10_.refs_2_, ...), custom_call_target="tpu_custom_call" | custom-call | flops 536870912 | tf_op jit(solution)/shard_map/pallas_call | solution.py:294
  59.5 1.3 %shard_map.62 = bf16[256,1024]{1,0:T(8,128)(2,1)S(1)} custom-call(s32[3]{0:T(128)S(1)} %pad_add_fusion.place, bf16[128,1024]{1,0:T(8,128)(2,1)S(1)} %get-tuple-element.68.refs_0_, bf16[128,1024]{1,0:T(8,128)(2,1)S(1)} %collective-permute-done.3.refs_1_, bf16[128,1024]{1,0:T(8,128)(2,1)S(1)} %get-tuple-element.41.refs_2_, ...), custom_call_target="tpu_custom_call" | custom-call | flops 536870912 | tf_op jit(solution)/shard_map/pallas_call | solution.py:294
  62.0 2.0 %shard_map.61.mine = f32[256,2048]{1,0:T(8,128)S(1)} custom-call(s32[3]{0:T(128)S(1)} %pad_add_fusion.place, bf16[128,1024]{1,0:T(8,128)(2,1)S(1)} %get-tuple-element.68.refs_0_, bf16[128,1024]{1,0:T(8,128)(2,1)S(1)} %collective-permute-done.3.refs_1_, bf16[128,1024]{1,0:T(8,128)(2,1)S(1)} %get-tuple-element.41.refs_2_, ...), custom_call_target="tpu_custom_call" | custom-call | flops 1073741824 | tf_op jit(solution)/shard_map/pallas_call | solution.py:301
  64.0 6.4 %collective-permute-done.27.part = bf16[256,1024]{1,0:T(8,128)(2,1)S(1)} collective-permute-done((bf16[256,1024]{1,0:T(8,128)(2,1)S(1)}, bf16[256,1024]{1,0:T(8,128)(2,1)S(1)}, u32[]{:S(2)}, u32[]{:S(2)}) %collective-permute-start.27) | collective-permute-done | bytes 524320 | tf_op jit(solution)/shard_map/ppermute | solution.py:196
  (58 shorter events, 23.4 us)
Async XLA Ops:
  0.0 20.4 %collective-permute-start.4 = (bf16[128,2048]{1,0:T(8,128)(2,1)}, bf16[128,2048]{1,0:T(8,128)(2,1)S(1)}, u32[]{:S(2)}, u32[]{:S(2)}) collective-permute-start(bf16[128,2048]{1,0:T(8,128)(2,1)} %param.9), channel_id=1, source_target_pairs={{0,8},{2,10},{4,12},{6,14},{8,16},{10,18},{12,20},{14,22},{16,24},... | collective-permute-start | bytes 1572872 | tf_op jit(solution)/shard_map/ppermute | solution.py:199
  4.1 12.1 %collective-permute-start.3 = (bf16[128,1024]{1,0:T(8,128)(2,1)S(1)}, bf16[128,1024]{1,0:T(8,128)(2,1)S(1)}, u32[]{:S(2)}, u32[]{:S(2)}) collective-permute-start(bf16[128,1024]{1,0:T(8,128)(2,1)S(1)} %get-tuple-element.68.refs_0_), channel_id=1, source_target_pairs={{0,4},{2,6},{4,0},{6,2},{8,12},{10,14},{12,8},{14,10},{16,20},{18,... | collective-permute-start | bytes 786440 | tf_op jit(solution)/shard_map/ppermute | solution.py:196
  11.0 5.2 %collective-permute-start.2 = (bf16[2,128,128]{2,1,0:T(8,128)(2,1)S(1)}, bf16[2,128,128]{2,1,0:T(8,128)(2,1)S(1)}, u32[]{:S(2)}, u32[]{:S(2)}) collective-permute-start(bf16[2,128,128]{2,1,0:T(8,128)(2,1)S(1)} %get-tuple-element.39), channel_id=1, source_target_pairs={{0,6},{2,4},{4,2},{6,0},{8,14},{10,12},{12,10},{14,8},{16,22},{18,... | collective-permute-start | bytes 196616 | tf_op jit(solution)/shard_map/ppermute | solution.py:196
  16.3 8.8 %collective-permute-start.5 = (bf16[2,128,128]{2,1,0:T(8,128)(2,1)S(1)}, bf16[2,128,128]{2,1,0:T(8,128)(2,1)S(1)}, u32[]{:S(2)}, u32[]{:S(2)}) collective-permute-start(bf16[2,128,128]{2,1,0:T(8,128)(2,1)S(1)} %shard_map.56), channel_id=1, source_target_pairs={{0,8},{2,10},{4,12},{6,14},{8,16},{10,18},{12,20},{14,22},{16,24},... | collective-permute-start | bytes 196616 | tf_op jit(solution)/shard_map/ppermute | solution.py:202
  19.8 9.0 %collective-permute-start.7 = (bf16[128,1024]{1,0:T(8,128)(2,1)S(1)}, bf16[128,1024]{1,0:T(8,128)(2,1)S(1)}, u32[]{:S(2)}, u32[]{:S(2)}) collective-permute-start(bf16[128,1024]{1,0:T(8,128)(2,1)S(1)} %get-tuple-element.67.refs_8_.refs_0_), channel_id=1, source_target_pairs={{0,2},{2,0},{4,6},{6,4},{8,10},{10,8},{12,14},{14,12},{16,18},{18,... | collective-permute-start | bytes 786440 | tf_op jit(solution)/shard_map/ppermute | solution.py:196
  20.4 10.3 %collective-permute-start.8 = (bf16[128,1024]{1,0:T(8,128)(2,1)S(1)}, bf16[128,1024]{1,0:T(8,128)(2,1)S(1)}, u32[]{:S(2)}, u32[]{:S(2)}) collective-permute-start(bf16[128,1024]{1,0:T(8,128)(2,1)S(1)} %get-tuple-element.41.refs_2_), channel_id=1, source_target_pairs={{0,8},{2,10},{4,12},{6,14},{8,16},{10,18},{12,20},{14,22},{16,24},... | collective-permute-start | bytes 786440 | tf_op jit(solution)/shard_map/ppermute | solution.py:199
  22.1 9.5 %collective-permute-start.10 = (bf16[128,1024]{1,0:T(8,128)(2,1)S(1)}, bf16[128,1024]{1,0:T(8,128)(2,1)S(1)}, u32[]{:S(2)}, u32[]{:S(2)}) collective-permute-start(bf16[128,1024]{1,0:T(8,128)(2,1)S(1)} %get-tuple-element.41.refs_2_), channel_id=1, source_target_pairs={{0,4},{2,6},{4,0},{6,2},{8,12},{10,14},{12,8},{14,10},{16,20},{18,... | collective-permute-start | bytes 786440 | tf_op jit(solution)/shard_map/ppermute | solution.py:196
  23.6 7.9 %collective-permute-start.9 = (bf16[128,1024]{1,0:T(8,128)(2,1)S(1)}, bf16[128,1024]{1,0:T(8,128)(2,1)S(1)}, u32[]{:S(2)}, u32[]{:S(2)}) collective-permute-start(bf16[128,1024]{1,0:T(8,128)(2,1)S(1)} %get-tuple-element.45.refs_10_.refs_2_), channel_id=1, source_target_pairs={{0,2},{2,0},{4,6},{6,4},{8,10},{10,8},{12,14},{14,12},{16,18},{18,... | collective-permute-start | bytes 786440 | tf_op jit(solution)/shard_map/ppermute | solution.py:196
  28.7 11.0 %collective-permute-start.18 = (bf16[128,1024]{1,0:T(8,128)(2,1)S(1)}, bf16[128,1024]{1,0:T(8,128)(2,1)S(1)}, u32[]{:S(2)}, u32[]{:S(2)}) collective-permute-start(bf16[128,1024]{1,0:T(8,128)(2,1)S(1)} %get-tuple-element.45.refs_10_.refs_2_), channel_id=1, source_target_pairs={{0,8},{2,10},{4,12},{6,14},{8,16},{10,18},{12,20},{14,22},{16,24},... | collective-permute-start | bytes 786440 | tf_op jit(solution)/shard_map/ppermute | solution.py:199
  31.5 12.6 %collective-permute-start.15 = (bf16[128,1024]{1,0:T(8,128)(2,1)S(1)}, bf16[128,1024]{1,0:T(8,128)(2,1)S(1)}, u32[]{:S(2)}, u32[]{:S(2)}) collective-permute-start(bf16[128,1024]{1,0:T(8,128)(2,1)S(1)} %collective-permute-done.8.refs_4_), channel_id=1, source_target_pairs={{0,8},{2,10},{4,12},{6,14},{8,16},{10,18},{12,20},{14,22},{16,24},... | collective-permute-start | bytes 786440 | tf_op jit(solution)/shard_map/ppermute | solution.py:199
  33.4 6.3 %collective-permute-start.13 = (bf16[2,128,128]{2,1,0:T(8,128)(2,1)S(1)}, bf16[2,128,128]{2,1,0:T(8,128)(2,1)S(1)}, u32[]{:S(2)}, u32[]{:S(2)}) collective-permute-start(bf16[2,128,128]{2,1,0:T(8,128)(2,1)S(1)} %get-tuple-element.52), channel_id=1, source_target_pairs={{0,4},{2,6},{4,0},{6,2},{8,12},{10,14},{12,8},{14,10},{16,20},{18,... | collective-permute-start | bytes 196616 | tf_op jit(solution)/shard_map/ppermute | solution.py:196
  34.4 5.3 %collective-permute-start.14 = (bf16[2,128,128]{2,1,0:T(8,128)(2,1)S(1)}, bf16[2,128,128]{2,1,0:T(8,128)(2,1)S(1)}, u32[]{:S(2)}, u32[]{:S(2)}) collective-permute-start(bf16[2,128,128]{2,1,0:T(8,128)(2,1)S(1)} %get-tuple-element.53), channel_id=1, source_target_pairs={{0,6},{2,4},{4,2},{6,0},{8,14},{10,12},{12,10},{14,8},{16,22},{18,... | collective-permute-start | bytes 196616 | tf_op jit(solution)/shard_map/ppermute | solution.py:196
  39.7 8.2 %collective-permute-start.21 = (bf16[128,1024]{1,0:T(8,128)(2,1)S(1)}, bf16[128,1024]{1,0:T(8,128)(2,1)S(1)}, u32[]{:S(2)}, u32[]{:S(2)}) collective-permute-start(bf16[128,1024]{1,0:T(8,128)(2,1)S(1)} %collective-permute-done.18.refs_12_.refs_4_), channel_id=1, source_target_pairs={{0,8},{2,10},{4,12},{6,14},{8,16},{10,18},{12,20},{14,22},{16,24},... | collective-permute-start | bytes 786440 | tf_op jit(solution)/shard_map/ppermute | solution.py:199
  41.1 6.7 %collective-permute-start.20 = (bf16[256,512]{1,0:T(8,128)(2,1)S(1)}, bf16[256,512]{1,0:T(8,128)(2,1)S(1)}, u32[]{:S(2)}, u32[]{:S(2)}) collective-permute-start(bf16[256,512]{1,0:T(8,128)(2,1)S(1)} %get-tuple-element.62), channel_id=1, source_target_pairs={{0,4},{2,6},{4,0},{6,2},{8,12},{10,14},{12,8},{14,10},{16,20},{18,... | collective-permute-start | bytes 786440 | tf_op jit(solution)/shard_map/ppermute | solution.py:196
  44.2 7.7 %collective-permute-start.16 = (bf16[256,512]{1,0:T(8,128)(2,1)S(1)}, bf16[256,512]{1,0:T(8,128)(2,1)S(1)}, u32[]{:S(2)}, u32[]{:S(2)}) collective-permute-start(bf16[256,512]{1,0:T(8,128)(2,1)S(1)} %get-tuple-element.58), channel_id=1, source_target_pairs={{0,2},{2,0},{4,6},{6,4},{8,10},{10,8},{12,14},{14,12},{16,18},{18,... | collective-permute-start | bytes 786440 | tf_op jit(solution)/shard_map/ppermute | solution.py:196
  45.6 6.9 %collective-permute-start.17 = (bf16[128,1024]{1,0:T(8,128)(2,1)S(1)}, bf16[128,1024]{1,0:T(8,128)(2,1)S(1)}, u32[]{:S(2)}, u32[]{:S(2)}) collective-permute-start(bf16[128,1024]{1,0:T(8,128)(2,1)S(1)} %collective-permute-done.15.refs_6_), channel_id=1, source_target_pairs={{0,4},{2,6},{4,0},{6,2},{8,12},{10,14},{12,8},{14,10},{16,20},{18,... | collective-permute-start | bytes 786440 | tf_op jit(solution)/shard_map/ppermute | solution.py:196
  45.9 8.8 %collective-permute-start.19 = (bf16[128,1024]{1,0:T(8,128)(2,1)S(1)}, bf16[128,1024]{1,0:T(8,128)(2,1)S(1)}, u32[]{:S(2)}, u32[]{:S(2)}) collective-permute-start(bf16[128,1024]{1,0:T(8,128)(2,1)S(1)} %collective-permute-done.18.refs_12_.refs_4_), channel_id=1, source_target_pairs={{0,2},{2,0},{4,6},{6,4},{8,10},{10,8},{12,14},{14,12},{16,18},{18,... | collective-permute-start | bytes 786440 | tf_op jit(solution)/shard_map/ppermute | solution.py:196
  47.9 9.6 %collective-permute-start.22 = (bf16[128,1024]{1,0:T(8,128)(2,1)S(1)}, bf16[128,1024]{1,0:T(8,128)(2,1)S(1)}, u32[]{:S(2)}, u32[]{:S(2)}) collective-permute-start(bf16[128,1024]{1,0:T(8,128)(2,1)S(1)} %collective-permute-done.21.refs_14_.refs_6_), channel_id=1, source_target_pairs={{0,2},{2,0},{4,6},{6,4},{8,10},{10,8},{12,14},{14,12},{16,18},{18,... | collective-permute-start | bytes 786440 | tf_op jit(solution)/shard_map/ppermute | solution.py:196
  48.9 8.6 %collective-permute-start.26 = (bf16[256,512]{1,0:T(8,128)(2,1)S(1)}, bf16[256,512]{1,0:T(8,128)(2,1)S(1)}, u32[]{:S(2)}, u32[]{:S(2)}) collective-permute-start(bf16[256,512]{1,0:T(8,128)(2,1)S(1)} %collective-permute-done.20.refs_8_), channel_id=1, source_target_pairs={{0,1},{1,0},{2,3},{3,2},{4,5},{5,4},{6,7},{7,6},{8,9},{9,8},{10,11... | collective-permute-start | bytes 786440 | tf_op jit(solution)/shard_map/ppermute | solution.py:205
  51.9 7.6 %collective-permute-start.11 = (bf16[128,1024]{1,0:T(8,128)(2,1)S(1)}, bf16[128,1024]{1,0:T(8,128)(2,1)S(1)}, u32[]{:S(2)}, u32[]{:S(2)}) collective-permute-start(bf16[128,1024]{1,0:T(8,128)(2,1)S(1)} %collective-permute-done.8.refs_4_), channel_id=1, source_target_pairs={{0,4},{2,6},{4,0},{6,2},{8,12},{10,14},{12,8},{14,10},{16,20},{18,... | collective-permute-start | bytes 786440 | tf_op jit(solution)/shard_map/ppermute | solution.py:196
  52.5 7.0 %collective-permute-start.24 = (bf16[256,512]{1,0:T(8,128)(2,1)S(1)}, bf16[256,512]{1,0:T(8,128)(2,1)S(1)}, u32[]{:S(2)}, u32[]{:S(2)}) collective-permute-start(bf16[256,512]{1,0:T(8,128)(2,1)S(1)} %collective-permute-done.16.refs_8_), channel_id=1, source_target_pairs={{0,1},{1,0},{2,3},{3,2},{4,5},{5,4},{6,7},{7,6},{8,9},{9,8},{10,11... | collective-permute-start | bytes 786440 | tf_op jit(solution)/shard_map/ppermute | solution.py:205
  54.7 7.3 %collective-permute-start.23 = (bf16[256,1024]{1,0:T(8,128)(2,1)S(1)}, bf16[256,1024]{1,0:T(8,128)(2,1)S(1)}, u32[]{:S(2)}, u32[]{:S(2)}) collective-permute-start(bf16[256,1024]{1,0:T(8,128)(2,1)S(1)} %get-tuple-element.64.refs_16_), channel_id=1, source_target_pairs={{0,1},{1,0},{2,3},{3,2},{4,5},{5,4},{6,7},{7,6},{8,9},{9,8},{10,11... | collective-permute-start | bytes 1572872 | tf_op jit(solution)/shard_map/ppermute | solution.py:205
  58.8 11.6 %collective-permute-start.27 = (bf16[256,1024]{1,0:T(8,128)(2,1)S(1)}, bf16[256,1024]{1,0:T(8,128)(2,1)S(1)}, u32[]{:S(2)}, u32[]{:S(2)}) collective-permute-start(bf16[256,1024]{1,0:T(8,128)(2,1)S(1)} %shard_map.63), channel_id=1, source_target_pairs={{0,4},{2,6},{4,0},{6,2},{8,12},{10,14},{12,8},{14,10},{16,20},{18,... | collective-permute-start | bytes 1572872 | tf_op jit(solution)/shard_map/ppermute | solution.py:196
  60.8 11.3 %collective-permute-start.25 = (bf16[256,1024]{1,0:T(8,128)(2,1)S(1)}, bf16[256,1024]{1,0:T(8,128)(2,1)S(1)}, u32[]{:S(2)}, u32[]{:S(2)}) collective-permute-start(bf16[256,1024]{1,0:T(8,128)(2,1)S(1)} %shard_map.62), channel_id=1, source_target_pairs={{0,2},{2,0},{4,6},{6,4},{8,10},{10,8},{12,14},{14,12},{16,18},{18,... | collective-permute-start | bytes 1572872 | tf_op jit(solution)/shard_map/ppermute | solution.py:196
  (10 other events, 158.6 us)

commit v4 on v3

--- a/solution.py
+++ b/solution.py
@@ -12,12 +12,14 @@
 F32, BF16 = jnp.float32, jnp.bfloat16
 VMEM_LIMIT = 40 * 1024 * 1024
 
+COST = 0
+PER_US = 1.15e9
+
 ANY = pl.BlockSpec(memory_space=pl.ANY)
 VMEM = pl.BlockSpec(memory_space=pltpu.VMEM)
-SMEM = pl.BlockSpec(memory_space=pltpu.SMEM)
-
-
-def call(body, outs, ins, scratch=(), flops=0, moved=0):
+
+
+def call(body, outs, ins, scratch=(), flops=0, moved=0, us=0.0):
     return pl.pallas_call(
         body,
         out_shape=outs,
@@ -25,12 +27,17 @@
         out_specs=[VMEM] * len(outs),
         scratch_shapes=list(scratch),
         compiler_params=pltpu.CompilerParams(vmem_limit_bytes=VMEM_LIMIT),
-        cost_estimate=pl.CostEstimate(flops=flops, bytes_accessed=moved, transcendentals=0),
+        cost_estimate=pl.CostEstimate(flops=int(us * PER_US) if us and (COST or not flops) else flops, bytes_accessed=moved, transcendentals=0),
     )
 
 
 def shape(dims, dtype):
     return jax.ShapeDtypeStruct(dims, dtype)
+
+
+def spot():
+    me = lax.axis_index("seq")
+    return me % PLANE, me // PLANE, lax.axis_index("mp")
 
 
 def silu(block):
@@ -42,7 +49,8 @@
     return pl.ds(pl.multiple_of(head * HD, HD), HD)
 
 
-def states_kernel(place, k_ref, v_ref, *outs):
+def states_kernel(k_ref, v_ref, *outs):
+    place = spot()
     per = outs[0].shape[0]
     for j, out in enumerate(outs):
         quarter = place[0] ^ j
@@ -71,7 +79,8 @@
     out[...] = ((a0[...].astype(F32) + a1[...].astype(F32)) + (a2[...].astype(F32) + a3[...].astype(F32))).astype(BF16)
 
 
-def prefixes_kernel(steps, place, *refs):
+def prefixes_kernel(steps, *refs):
+    place = spot()
     own, shifts, outs = refs[:PLANE], refs[PLANE:PLANE + steps], refs[PLANE + steps:]
     before = sum(ref[...].astype(F32) for ref in shifts)
     for j, out in enumerate(outs):
@@ -81,7 +90,8 @@
         out[...] = total.astype(BF16)
 
 
-def norm_kernel(place, intra, feat, c0, c1, c2, c3, gain, normed):
+def norm_kernel(intra, feat, c0, c1, c2, c3, gain, normed):
+    place = spot()
     for j, state in enumerate((c0, c1, c2, c3)):
         per = state.shape[0]
         for i in range(per):
@@ -91,8 +101,9 @@
             normed[:, cols] = (mixed * scale * gain[:, cols]).astype(BF16)
 
 
-def norm_send_kernel(place, intra, feat, c0, c1, c2, c3, gain, normed, to_x, to_y):
-    norm_kernel(place, intra, feat, c0, c1, c2, c3, gain, normed)
+def norm_send_kernel(intra, feat, c0, c1, c2, c3, gain, normed, to_x, to_y):
+    place = spot()
+    norm_kernel(intra, feat, c0, c1, c2, c3, gain, normed)
     x, y = place[0] & 1, place[0] >> 1
     for t in range(4):
         slot = slice(t * HD, (t + 1) * HD)
@@ -105,7 +116,7 @@
     return from_z >> 1, 4 * (from_z & 1) + (place[0] ^ (t * flip))
 
 
-def sums(place, pieces, own, other, way, flip, thin):
+def sums(place, pieces, got, way, flip, thin):
     left = []
     for r in range(4):
         for t in range(2):
@@ -113,22 +124,28 @@
             if thin:
                 head = (head >> 1) if flip == 2 else 2 * (head >> 2) + (head & 1)
             cols = head_cols(head)
-            left.append(jnp.where(core == place[2], own[:, cols], other[:, cols]))
+            left.append(got[core, :, cols])
     return jnp.dot(
         jnp.concatenate(left, axis=1), jnp.concatenate([p[...] for p in pieces], axis=0), preferred_element_type=F32
     )
 
 
-def partner_kernel(way, flip, place, *refs):
-    own, other, out = refs[8:]
-    out[...] = sums(place, refs[:8], own, other, way, flip, True).astype(BF16)
-
-
-def own_kernel(ways, place, *refs):
-    own, other, out = refs[16:]
+def partner_kernel(way, flip, *refs):
+    place = spot()
+    own, other, out, got = refs[8:]
+    got[place[2]] = own[...]
+    got[1 - place[2]] = other[...]
+    out[...] = sums(place, refs[:8], got, way, flip, True).astype(BF16)
+
+
+def own_kernel(ways, *refs):
+    place = spot()
+    own, other, out, got = refs[16:]
+    got[place[2]] = own[...]
+    got[1 - place[2]] = other[...]
     cut = refs[0].shape[1]
-    out[:, :cut] = sums(place, refs[:8], own, other, ways[0], 2, False)
-    out[:, cut:] = sums(place, refs[8:16], own, other, ways[1], 1, False)
+    out[:, :cut] = sums(place, refs[:8], got, ways[0], 2, False)
+    out[:, cut:] = sums(place, refs[8:16], got, ways[1], 1, False)
 
 
 def cut_kernel(block, first, second, sems):
@@ -175,8 +192,10 @@
 
 CUT = 8
 ZD = 0
-BD = 0
-TIES = {'tot': '', 'z1': 'y0', 'z2': '', 'add': 'x0', 'back': 'a2 x1 y1', 'norm': '', 'act': 'a3', 'act2': 'y3', 'act3': 'b3'}
+DN = 0
+CUT_US = 0
+ORD = 0
+TIES = {'tot': '', 'z1': 'y0', 'z2': '', 'add': 'a2 x0', 'back': 'x1', 'norm': 'y1', 'act': '', 'act2': 'a3 x2 y3', 'act3': 'b3'}
 
 
 def tie(value, *others):
@@ -187,9 +206,6 @@
     rows, feats = queries.shape
     heads = feats // HD
     blocks = lax.axis_size("seq")
-    me, core = lax.axis_index("seq"), lax.axis_index("mp")
-    position, level = me % PLANE, me // PLANE
-    place = jnp.stack([position, level, core]).astype(jnp.int32)
     split = w_out.shape[0] == HD and blocks == 4 * PLANE
 
     def partner(value, flip):
@@ -206,21 +222,33 @@
 
     cols = w_out.shape[1]
     half = cols * CUT // 16
-    held = {"a0": w_out[:, :half], "b0": w_out[:, half:]}
+    def cut(block, us=0.0):
+        return call(
+            cut_kernel,
+            [shape((HD, half), BF16), shape((HD, cols - half), BF16)],
+            [ANY],
+            [pltpu.SemaphoreType.DMA((2,))],
+            us=us,
+        )(block)
+
+    held = {}
+    early_keys = keys
+    if split:
+        held["a0"], held["b0"] = cut(w_out, CUT_US)
+        if CUT_US:
+            early_keys, held["a0"] = tie(keys, held["a0"])
 
     def piece(n):
         if n not in held:
             if n == "r1":
                 held[n] = ring(w_out)
             elif n in ("a1", "b1"):
-                held["a1"], held["b1"] = call(
-                    cut_kernel,
-                    [shape((HD, half), BF16), shape((HD, cols - half), BF16)],
-                    [ANY],
-                    [pltpu.SemaphoreType.DMA((2,))],
-                )(piece("r1"))
+                held["a1"], held["b1"] = cut(piece("r1"))
             elif n[0] in "ab":
-                held[n] = ring(piece(n[0] + str(int(n[1]) - 1)), -1 if BD and n[0] == "b" else 1)
+                if DN and n[1] == "3":
+                    held[n] = ring(piece(n[0] + "0"), -1)
+                else:
+                    held[n] = ring(piece(n[0] + str(int(n[1]) - 1)))
             else:
                 held[n] = partner(piece({"x": "b", "y": "a"}[n[0]] + n[1]), {"x": 1, "y": 2}[n[0]])
         return held[n]
@@ -235,9 +263,11 @@
 
     per = heads // PLANE
     quarter = shape((per, HD, HD), BF16)
-    own = call(states_kernel, [quarter] * PLANE, [SMEM, VMEM, VMEM], flops=2 * rows * feats * HD)(place, keys, values)
+    own = call(states_kernel, [quarter] * PLANE, [VMEM, VMEM], flops=2 * rows * feats * HD, us=1.1)(
+        early_keys, values
+    )
     intra, feat = call(
-        intra_kernel, [shape((rows, feats), F32), shape((rows, feats), BF16)], [VMEM] * 3, flops=4 * rows * rows * feats
+        intra_kernel, [shape((rows, feats), F32), shape((rows, feats), BF16)], [VMEM] * 3, flops=4 * rows * rows * feats, us=1.0
     )(queries, keys, values)
     mine = [own[0]] + [partner(own[j], j) for j in range(1, PLANE)]
     mine[3] = tied(mine[3], "tot")
@@ -255,17 +285,17 @@
             by *= 2
     shifts[-1] = tied(shifts[-1], "add")
     prefixes = call(
-        functools.partial(prefixes_kernel, len(shifts)), [quarter] * PLANE, [SMEM] + [VMEM] * (PLANE + len(shifts))
-    )(place, *mine, *shifts)
+        functools.partial(prefixes_kernel, len(shifts)), [quarter] * PLANE, [VMEM] * (PLANE + len(shifts)), flops=1
+    )(*mine, *shifts)
     prefixes = list(prefixes)
     prefixes[1] = tied(prefixes[1], "back")
     states = [prefixes[0]] + [partner(prefixes[j], j) for j in range(1, PLANE)]
     states[3] = tied(states[3], "norm")
     gain = norm_gain.reshape(1, feats)
-    normed_args = (place, intra, feat, *states, gain)
+    normed_args = (intra, feat, *states, gain)
 
     if not split:
-        (normed,) = call(norm_kernel, [shape((rows, feats), BF16)], [SMEM] + [VMEM] * 7)(*normed_args)
+        (normed,) = call(norm_kernel, [shape((rows, feats), BF16)], [VMEM] * 7)(*normed_args)
         all_heads = lax.all_gather(normed, "mp", axis=1, tiled=True)
         weight = lax.all_gather(w_out, "seq", axis=0, tiled=True)
         return jnp.dot(all_heads, weight, preferred_element_type=F32).astype(BF16)
@@ -273,8 +303,9 @@
     normed, to_x, to_y = call(
         norm_send_kernel,
         [shape((rows, feats), BF16)] + [shape((rows, feats // 2), BF16)] * 2,
-        [SMEM] + [VMEM] * 7,
+        [VMEM] * 7,
         flops=2 * rows * feats * HD,
+        us=1.2,
     )(*normed_args)
     if TIES["act"]:
         to_x, to_y = tie(to_x, to_y)
@@ -287,25 +318,33 @@
         wa += [piece("a%d" % r), piece("y%d" % r)]
         wb += [piece("b%d" % r), piece("x%d" % r)]
     other = swap(normed)
-    ways = (-1, 1 if BD else -1)
-    parts = []
-    for way, flip, pieces, got in ((ways[0], 2, wa, got_x), (ways[1], 1, wb, got_y)):
+    ways = (-1, -1)
+    swapped = [swap(got_x), swap(got_y)]
+    parts = [None, None]
+    turns = [(0, 2, wa, got_x), (1, 1, wb, got_y)]
+    for at, flip, pieces, got in turns[::-1] if ORD == 2 else turns:
         width = pieces[0].shape[1]
         (part,) = call(
-            functools.partial(partner_kernel, way, flip),
+            functools.partial(partner_kernel, ways[at], flip),
             [shape((rows, width), BF16)],
-            [SMEM] + [VMEM] * 10,
+            [VMEM] * 10,
+            [pltpu.VMEM((2, rows, feats // 2), BF16)],
             flops=rows * feats * width * 2,
-        )(place, *pieces, got, swap(got))
-        parts.append(partner(part, 3 - flip))
+            us=1.3,
+        )(*pieces, got, swapped[at])
+        if ORD and parts[1 - at] is None:
+            part, swapped[1 - at] = tie(part, swapped[1 - at])
+        parts[at] = partner(part, 3 - flip)
     (mine_all,) = call(
         functools.partial(own_kernel, ways),
         [shape((rows, cols), F32)],
-        [SMEM] + [VMEM] * 18,
+        [VMEM] * 18,
+        [pltpu.VMEM((2, rows, feats), BF16)],
         flops=rows * feats * cols * 2,
-    )(place, *wa, *wb, normed, other)
+        us=2.0,
+    )(*wa, *wb, normed, other)
     result = None
-    for at, part in ((half, parts[1]), (0, parts[0])):
+    for at, part in ((0, parts[0]), (half, parts[1]))[:: 1 if ORD == 1 else -1]:
         result = finish(mine_all, part, at, result)
     return result
 

time: 73.2 us -> 70.5 us (0.963)
  starting transfers between devices: 33.5 us -> 36.8 us
  Pallas kernels: 10.4 us -> 7.13 us
  waiting for transfers between devices: 25.6 us -> 22.8 us
    pallas_call x5 -> x6, Pallas kernels: 5.71 us -> 3.51 us  [the longest x2 1.48 us: per_device(): call(functools.partial(partner_kernel, ways[at], flip), [shape((rows, wid...]
    ppermute x5, waiting for transfers between devices: 4.33 us -> 2.29 us  [ring(): lax.ppermute(value, 'seq', [(i, (i + way * PLANE) % blocks) for i in rang...]
    ppermute x5, starting transfers between devices: 7.74 us -> 9.29 us  [ring(): lax.ppermute(value, 'seq', [(i, (i + way * PLANE) % blocks) for i in rang...]
    ppermute x18, starting transfers between devices: 19.9 us -> 21.2 us  [partner(): return lax.ppermute(value, 'seq', [(i, i ^ flip) for i in range(blocks)])]
    unnamed x12 -> x14, local copies, waits for them, and re-layouts: 2.1 us -> 3.17 us
    slice x1 -> x0, local copies, waits for them, and re-layouts: 1.06 us -> none  [per_device(): held = {'a0': w_out[:, :half], 'b0': w_out[:, half:]}]
  transfers between devices with their start and end apart: 28 -> 28, of which waited for: 15 -> 15; matrix products, arithmetic and copies ran while one was open for 2% -> 0% of each run, Pallas kernels for 13% -> 9%
where the time goes in v4:
time: 70.5 us; the launch traced here: 70.1 us
  starting transfers between devices  36.8 us (52%)
  waiting for transfers between devices  22.8 us (32%)
  Pallas kernels  7.13 us (10%)
  local copies, waits for them, and re-layouts  3.17 us (4%)
    ppermute x18, starting transfers between devices, partner(): return lax.ppermute(value, 'seq', [(i, i ^ flip) for i in range(blocks)])  21.2 us
    ppermute x18, waiting for transfers between devices, partner(): return lax.ppermute(value, 'seq', [(i, i ^ flip) for i in range(blocks)])  20.5 us
    ppermute x5, starting transfers between devices, ring(): lax.ppermute(value, 'seq', [(i, (i + way * PLANE) % blocks) for i in rang...  9.29 us
    ppermute x2, starting transfers between devices, up(): lax.ppermute(value, 'seq', [(i, i + by * PLANE) for i in range(blocks - b...  5.8 us
    unnamed x14, local copies, waits for them, and re-layouts  3.17 us
    ppermute x5, waiting for transfers between devices, ring(): lax.ppermute(value, 'seq', [(i, (i + way * PLANE) % blocks) for i in rang...  2.29 us
    pallas_call x2, Pallas kernels, finish(): pl.pallas_call(functools.partial(finish_kernel, at), out_shape=shape(mine...  1.68 us
    pallas_call x2, Pallas kernels, per_device(): call(functools.partial(partner_kernel, ways[at], flip), [shape((rows, wid...  1.48 us
  transfers between devices with their start and end apart: 28, of which 15 were waited for; matrix products, arithmetic and copies ran while one was open for 0% of the time, Pallas kernels for 9%

profile of v4, /device:TPU:0, one launch (start us, length us, event | category | flops | bytes accessed | tf_op | source)
XLA Modules:
  0.0 70.1 jit_solution(14993005839283415271)
XLA Ops:
  0.0 3.0 %collective-permute-start.4 = (bf16[128,2048]{1,0:T(8,128)(2,1)}, bf16[128,2048]{1,0:T(8,128)(2,1)S(1)}, u32[]{:S(2)}, u32[]{:S(2)}) collective-permute-start(bf16[128,2048]{1,0:T(8,128)(2,1)} %block.1), channel_id=1, source_target_pairs={{0,8},{2,10},{4,12},{6,14},{8,16},{10,18},{12,20},{14,22},{16,24},... | collective-permute-start | bytes 1572872 | tf_op jit(solution)/shard_map/ppermute | solution.py:215
  4.2 1.6 %collective-permute-start.3 = (bf16[128,1024]{1,0:T(8,128)(2,1)S(1)}, bf16[128,1024]{1,0:T(8,128)(2,1)S(1)}, u32[]{:S(2)}, u32[]{:S(2)}) collective-permute-start(bf16[128,1024]{1,0:T(8,128)(2,1)S(1)} %get-tuple-element.37.refs_0_), channel_id=1, source_target_pairs={{0,4},{2,6},{4,0},{6,2},{8,12},{10,14},{12,8},{14,10},{16,20},{18,... | collective-permute-start | bytes 786440 | tf_op jit(solution)/shard_map/ppermute | solution.py:212
  8.4 1.5 %collective-permute-start = (bf16[2,128,128]{2,1,0:T(8,128)(2,1)S(1)}, bf16[2,128,128]{2,1,0:T(8,128)(2,1)S(1)}, u32[]{:S(2)}, u32[]{:S(2)}) collective-permute-start(bf16[2,128,128]{2,1,0:T(8,128)(2,1)S(1)} %get-tuple-element.39), channel_id=1, source_target_pairs={{0,2},{2,0},{4,6},{6,4},{8,10},{10,8},{12,14},{14,12},{16,18},{18,... | collective-permute-start | bytes 196616 | tf_op jit(solution)/shard_map/ppermute | solution.py:212
  10.5 1.5 %collective-permute-start.2 = (bf16[2,128,128]{2,1,0:T(8,128)(2,1)S(1)}, bf16[2,128,128]{2,1,0:T(8,128)(2,1)S(1)}, u32[]{:S(2)}, u32[]{:S(2)}) collective-permute-start(bf16[2,128,128]{2,1,0:T(8,128)(2,1)S(1)} %get-tuple-element.41), channel_id=1, source_target_pairs={{0,6},{2,4},{4,2},{6,0},{8,14},{10,12},{12,10},{14,8},{16,22},{18,... | collective-permute-start | bytes 196616 | tf_op jit(solution)/shard_map/ppermute | solution.py:212
  12.8 1.4 %collective-permute-done.1.a2.refs_2_ = bf16[2,128,128]{2,1,0:T(8,128)(2,1)S(1)} collective-permute-done((bf16[2,128,128]{2,1,0:T(8,128)(2,1)S(1)}, bf16[2,128,128]{2,1,0:T(8,128)(2,1)S(1)}, u32[]{:S(2)}, u32[]{:S(2)}) %collective-permute-start.1) | collective-permute-done | bytes 65568 | tf_op jit(solution)/shard_map/ppermute | solution.py:212
  14.2 1.4 %collective-permute-done.2.a3.refs_3_ = bf16[2,128,128]{2,1,0:T(8,128)(2,1)S(1)} collective-permute-done((bf16[2,128,128]{2,1,0:T(8,128)(2,1)S(1)}, bf16[2,128,128]{2,1,0:T(8,128)(2,1)S(1)}, u32[]{:S(2)}, u32[]{:S(2)}) %collective-permute-start.2) | collective-permute-done | bytes 65568 | tf_op jit(solution)/shard_map/ppermute | solution.py:212
  15.7 3.5 %collective-permute-start.5 = (bf16[2,128,128]{2,1,0:T(8,128)(2,1)S(1)}, bf16[2,128,128]{2,1,0:T(8,128)(2,1)S(1)}, u32[]{:S(2)}, u32[]{:S(2)}) collective-permute-start(bf16[2,128,128]{2,1,0:T(8,128)(2,1)S(1)} %shard_map.57), channel_id=1, source_target_pairs={{0,8},{2,10},{4,12},{6,14},{8,16},{10,18},{12,20},{14,22},{16,24},... | collective-permute-start | bytes 196616 | tf_op jit(solution)/shard_map/ppermute | solution.py:218
  20.0 1.6 %collective-permute-start.7 = (bf16[128,1024]{1,0:T(8,128)(2,1)S(1)}, bf16[128,1024]{1,0:T(8,128)(2,1)S(1)}, u32[]{:S(2)}, u32[]{:S(2)}) collective-permute-start(bf16[128,1024]{1,0:T(8,128)(2,1)S(1)} %get-tuple-element.43.refs_2_), channel_id=1, source_target_pairs={{0,8},{2,10},{4,12},{6,14},{8,16},{10,18},{12,20},{14,22},{16,24},... | collective-permute-start | bytes 786440 | tf_op jit(solution)/shard_map/ppermute | solution.py:215
  21.6 1.5 %collective-permute-start.10 = (bf16[128,1024]{1,0:T(8,128)(2,1)S(1)}, bf16[128,1024]{1,0:T(8,128)(2,1)S(1)}, u32[]{:S(2)}, u32[]{:S(2)}) collective-permute-start(bf16[128,1024]{1,0:T(8,128)(2,1)S(1)} %get-tuple-element.43.refs_2_), channel_id=1, source_target_pairs={{0,4},{2,6},{4,0},{6,2},{8,12},{10,14},{12,8},{14,10},{16,20},{18,... | collective-permute-start | bytes 786440 | tf_op jit(solution)/shard_map/ppermute | solution.py:212
  23.1 1.4 %collective-permute-start.12 = (bf16[128,1024]{1,0:T(8,128)(2,1)S(1)}, bf16[128,1024]{1,0:T(8,128)(2,1)S(1)}, u32[]{:S(2)}, u32[]{:S(2)}) collective-permute-start(bf16[128,1024]{1,0:T(8,128)(2,1)S(1)} %get-tuple-element.54.refs_10_.refs_2_), channel_id=1, source_target_pairs={{0,2},{2,0},{4,6},{6,4},{8,10},{10,8},{12,14},{14,12},{16,18},{18,... | collective-permute-start | bytes 786440 | tf_op jit(solution)/shard_map/ppermute | solution.py:212
  24.5 2.3 %collective-permute-start.6 = (bf16[2,128,128]{2,1,0:T(8,128)(2,1)S(1)}, bf16[2,128,128]{2,1,0:T(8,128)(2,1)S(1)}, u32[]{:S(2)}, u32[]{:S(2)}) collective-permute-start(bf16[2,128,128]{2,1,0:T(8,128)(2,1)S(1)} %add_convert_fusion), channel_id=1, source_target_pairs={{0,16},{2,18},{4,20},{6,22},{8,24},{10,26},{12,28},{14,30},{1,17},... | collective-permute-start | bytes 196616 | tf_op jit(solution)/shard_map/ppermute | solution.py:218
  26.9 1.3 %collective-permute-done.8.refs_9_.refs_1_ = bf16[128,1024]{1,0:T(8,128)(2,1)S(1)} collective-permute-done((bf16[128,1024]{1,0:T(8,128)(2,1)S(1)}, bf16[128,1024]{1,0:T(8,128)(2,1)S(1)}, u32[]{:S(2)}, u32[]{:S(2)}) %collective-permute-start.8) | collective-permute-done | bytes 262176 | tf_op jit(solution)/shard_map/ppermute | solution.py:212
  29.4 2.7 %collective-permute-start.16 = (bf16[128,1024]{1,0:T(8,128)(2,1)S(1)}, bf16[128,1024]{1,0:T(8,128)(2,1)S(1)}, u32[]{:S(2)}, u32[]{:S(2)}) collective-permute-start(bf16[128,1024]{1,0:T(8,128)(2,1)S(1)} %collective-permute-done.7.refs_4_), channel_id=1, source_target_pairs={{0,8},{2,10},{4,12},{6,14},{8,16},{10,18},{12,20},{14,22},{16,24},... | collective-permute-start | bytes 786440 | tf_op jit(solution)/shard_map/ppermute | solution.py:215
  33.1 1.6 %collective-permute-start.13 = (bf16[2,128,128]{2,1,0:T(8,128)(2,1)S(1)}, bf16[2,128,128]{2,1,0:T(8,128)(2,1)S(1)}, u32[]{:S(2)}, u32[]{:S(2)}) collective-permute-start(bf16[2,128,128]{2,1,0:T(8,128)(2,1)S(1)} %get-tuple-element.55), channel_id=1, source_target_pairs={{0,2},{2,0},{4,6},{6,4},{8,10},{10,8},{12,14},{14,12},{16,18},{18,... | collective-permute-start | bytes 196616 | tf_op jit(solution)/shard_map/ppermute | solution.py:212
  42.4 1.2 %collective-permute-start.15 = (bf16[256,512]{1,0:T(8,128)(2,1)S(1)}, bf16[256,512]{1,0:T(8,128)(2,1)S(1)}, u32[]{:S(2)}, u32[]{:S(2)}) collective-permute-start(bf16[256,512]{1,0:T(8,128)(2,1)S(1)} %get-tuple-element.58), channel_id=1, source_target_pairs={{0,2},{2,0},{4,6},{6,4},{8,10},{10,8},{12,14},{14,12},{16,18},{18,... | collective-permute-start | bytes 786440 | tf_op jit(solution)/shard_map/ppermute | solution.py:212
  44.6 1.3 %collective-permute-done.21.refs_14_.refs_6_ = bf16[128,1024]{1,0:T(8,128)(2,1)S(1)} collective-permute-done((bf16[128,1024]{1,0:T(8,128)(2,1)S(1)}, bf16[128,1024]{1,0:T(8,128)(2,1)S(1)}, u32[]{:S(2)}, u32[]{:S(2)}) %collective-permute-start.21) | collective-permute-done | bytes 262176 | tf_op jit(solution)/shard_map/ppermute | solution.py:215
  47.5 1.9 %collective-permute-done.18.refs_13_.refs_5_ = bf16[128,1024]{1,0:T(8,128)(2,1)S(1)} collective-permute-done((bf16[128,1024]{1,0:T(8,128)(2,1)S(1)}, bf16[128,1024]{1,0:T(8,128)(2,1)S(1)}, u32[]{:S(2)}, u32[]{:S(2)}) %collective-permute-start.18) | collective-permute-done | bytes 262176 | tf_op jit(solution)/shard_map/ppermute | solution.py:212
  49.4 1.3 %collective-permute-start.11 = (bf16[128,1024]{1,0:T(8,128)(2,1)S(1)}, bf16[128,1024]{1,0:T(8,128)(2,1)S(1)}, u32[]{:S(2)}, u32[]{:S(2)}) collective-permute-start(bf16[128,1024]{1,0:T(8,128)(2,1)S(1)} %collective-permute-done.7.refs_4_), channel_id=1, source_target_pairs={{0,4},{2,6},{4,0},{6,2},{8,12},{10,14},{12,8},{14,10},{16,20},{18,... | collective-permute-start | bytes 786440 | tf_op jit(solution)/shard_map/ppermute | solution.py:212
  50.7 1.5 %collective-permute-done.15.refs_8_ = bf16[256,512]{1,0:T(8,128)(2,1)S(1)} collective-permute-done((bf16[256,512]{1,0:T(8,128)(2,1)S(1)}, bf16[256,512]{1,0:T(8,128)(2,1)S(1)}, u32[]{:S(2)}, u32[]{:S(2)}) %collective-permute-start.15) | collective-permute-done | bytes 262176 | tf_op jit(solution)/shard_map/ppermute | solution.py:212
  52.7 2.3 %collective-permute-done.22.refs_15_.refs_7_ = bf16[128,1024]{1,0:T(8,128)(2,1)S(1)} collective-permute-done((bf16[128,1024]{1,0:T(8,128)(2,1)S(1)}, bf16[128,1024]{1,0:T(8,128)(2,1)S(1)}, u32[]{:S(2)}, u32[]{:S(2)}) %collective-permute-start.22) | collective-permute-done | bytes 262176 | tf_op jit(solution)/shard_map/ppermute | solution.py:212
  55.8 1.4 %collective-permute-start.27 = (bf16[256,1024]{1,0:T(8,128)(2,1)S(1)}, bf16[256,1024]{1,0:T(8,128)(2,1)S(1)}, u32[]{:S(2)}, u32[]{:S(2)}) collective-permute-start(bf16[256,1024]{1,0:T(8,128)(2,1)S(1)} %shard_map.64), channel_id=1, source_target_pairs={{0,4},{2,6},{4,0},{6,2},{8,12},{10,14},{12,8},{14,10},{16,20},{18,... | collective-permute-start | bytes 1572872 | tf_op jit(solution)/shard_map/ppermute | solution.py:212
  57.9 1.4 %collective-permute-start.25 = (bf16[256,1024]{1,0:T(8,128)(2,1)S(1)}, bf16[256,1024]{1,0:T(8,128)(2,1)S(1)}, u32[]{:S(2)}, u32[]{:S(2)}) collective-permute-start(bf16[256,1024]{1,0:T(8,128)(2,1)S(1)} %shard_map.63), channel_id=1, source_target_pairs={{0,2},{2,0},{4,6},{6,4},{8,10},{10,8},{12,14},{14,12},{16,18},{18,... | collective-permute-start | bytes 1572872 | tf_op jit(solution)/shard_map/ppermute | solution.py:212
  59.4 1.3 %shard_map.62.mine = f32[256,2048]{1,0:T(8,128)S(1)} custom-call(bf16[128,1024]{1,0:T(8,128)(2,1)S(1)} %get-tuple-element.37.refs_0_, bf16[128,1024]{1,0:T(8,128)(2,1)S(1)} %collective-permute-done.3.refs_1_, bf16[128,1024]{1,0:T(8,128)(2,1)S(1)} %get-tuple-element.43.refs_2_, bf16[128,1024]{1,0:T(8,128)(2,1)S(1)} %collective-permute-done.10.refs_3_, ...), custom_call_target="tpu_custom_call" | custom-call | flops 1073741824 | tf_op jit(solution)/shard_map/pallas_call | solution.py:338
  60.7 6.8 %collective-permute-done.27.part = bf16[256,1024]{1,0:T(8,128)(2,1)S(1)} collective-permute-done((bf16[256,1024]{1,0:T(8,128)(2,1)S(1)}, bf16[256,1024]{1,0:T(8,128)(2,1)S(1)}, u32[]{:S(2)}, u32[]{:S(2)}) %collective-permute-start.27) | collective-permute-done | bytes 524320 | tf_op jit(solution)/shard_map/ppermute | solution.py:212
  (59 shorter events, 23.0 us)
Async XLA Ops:
  0.0 19.9 %collective-permute-start.4 = (bf16[128,2048]{1,0:T(8,128)(2,1)}, bf16[128,2048]{1,0:T(8,128)(2,1)S(1)}, u32[]{:S(2)}, u32[]{:S(2)}) collective-permute-start(bf16[128,2048]{1,0:T(8,128)(2,1)} %block.1), channel_id=1, source_target_pairs={{0,8},{2,10},{4,12},{6,14},{8,16},{10,18},{12,20},{14,22},{16,24},... | collective-permute-start | bytes 1572872 | tf_op jit(solution)/shard_map/ppermute | solution.py:215
  4.2 11.5 %collective-permute-start.3 = (bf16[128,1024]{1,0:T(8,128)(2,1)S(1)}, bf16[128,1024]{1,0:T(8,128)(2,1)S(1)}, u32[]{:S(2)}, u32[]{:S(2)}) collective-permute-start(bf16[128,1024]{1,0:T(8,128)(2,1)S(1)} %get-tuple-element.37.refs_0_), channel_id=1, source_target_pairs={{0,4},{2,6},{4,0},{6,2},{8,12},{10,14},{12,8},{14,10},{16,20},{18,... | collective-permute-start | bytes 786440 | tf_op jit(solution)/shard_map/ppermute | solution.py:212
  10.5 5.2 %collective-permute-start.2 = (bf16[2,128,128]{2,1,0:T(8,128)(2,1)S(1)}, bf16[2,128,128]{2,1,0:T(8,128)(2,1)S(1)}, u32[]{:S(2)}, u32[]{:S(2)}) collective-permute-start(bf16[2,128,128]{2,1,0:T(8,128)(2,1)S(1)} %get-tuple-element.41), channel_id=1, source_target_pairs={{0,6},{2,4},{4,2},{6,0},{8,14},{10,12},{12,10},{14,8},{16,22},{18,... | collective-permute-start | bytes 196616 | tf_op jit(solution)/shard_map/ppermute | solution.py:212
  15.7 8.8 %collective-permute-start.5 = (bf16[2,128,128]{2,1,0:T(8,128)(2,1)S(1)}, bf16[2,128,128]{2,1,0:T(8,128)(2,1)S(1)}, u32[]{:S(2)}, u32[]{:S(2)}) collective-permute-start(bf16[2,128,128]{2,1,0:T(8,128)(2,1)S(1)} %shard_map.57), channel_id=1, source_target_pairs={{0,8},{2,10},{4,12},{6,14},{8,16},{10,18},{12,20},{14,22},{16,24},... | collective-permute-start | bytes 196616 | tf_op jit(solution)/shard_map/ppermute | solution.py:218
  19.2 9.0 %collective-permute-start.8 = (bf16[128,1024]{1,0:T(8,128)(2,1)S(1)}, bf16[128,1024]{1,0:T(8,128)(2,1)S(1)}, u32[]{:S(2)}, u32[]{:S(2)}) collective-permute-start(bf16[128,1024]{1,0:T(8,128)(2,1)S(1)} %get-tuple-element.45.refs_8_.refs_0_), channel_id=1, source_target_pairs={{0,2},{2,0},{4,6},{6,4},{8,10},{10,8},{12,14},{14,12},{16,18},{18,... | collective-permute-start | bytes 786440 | tf_op jit(solution)/shard_map/ppermute | solution.py:212
  20.0 9.4 %collective-permute-start.7 = (bf16[128,1024]{1,0:T(8,128)(2,1)S(1)}, bf16[128,1024]{1,0:T(8,128)(2,1)S(1)}, u32[]{:S(2)}, u32[]{:S(2)}) collective-permute-start(bf16[128,1024]{1,0:T(8,128)(2,1)S(1)} %get-tuple-element.43.refs_2_), channel_id=1, source_target_pairs={{0,8},{2,10},{4,12},{6,14},{8,16},{10,18},{12,20},{14,22},{16,24},... | collective-permute-start | bytes 786440 | tf_op jit(solution)/shard_map/ppermute | solution.py:215
  21.6 13.1 %collective-permute-start.10 = (bf16[128,1024]{1,0:T(8,128)(2,1)S(1)}, bf16[128,1024]{1,0:T(8,128)(2,1)S(1)}, u32[]{:S(2)}, u32[]{:S(2)}) collective-permute-start(bf16[128,1024]{1,0:T(8,128)(2,1)S(1)} %get-tuple-element.43.refs_2_), channel_id=1, source_target_pairs={{0,4},{2,6},{4,0},{6,2},{8,12},{10,14},{12,8},{14,10},{16,20},{18,... | collective-permute-start | bytes 786440 | tf_op jit(solution)/shard_map/ppermute | solution.py:212
  23.1 10.0 %collective-permute-start.12 = (bf16[128,1024]{1,0:T(8,128)(2,1)S(1)}, bf16[128,1024]{1,0:T(8,128)(2,1)S(1)}, u32[]{:S(2)}, u32[]{:S(2)}) collective-permute-start(bf16[128,1024]{1,0:T(8,128)(2,1)S(1)} %get-tuple-element.54.refs_10_.refs_2_), channel_id=1, source_target_pairs={{0,2},{2,0},{4,6},{6,4},{8,10},{10,8},{12,14},{14,12},{16,18},{18,... | collective-permute-start | bytes 786440 | tf_op jit(solution)/shard_map/ppermute | solution.py:212
  28.2 9.6 %collective-permute-start.17 = (bf16[128,1024]{1,0:T(8,128)(2,1)S(1)}, bf16[128,1024]{1,0:T(8,128)(2,1)S(1)}, u32[]{:S(2)}, u32[]{:S(2)}) collective-permute-start(bf16[128,1024]{1,0:T(8,128)(2,1)S(1)} %get-tuple-element.54.refs_10_.refs_2_), channel_id=1, source_target_pairs={{0,8},{2,10},{4,12},{6,14},{8,16},{10,18},{12,20},{14,22},{16,24},... | collective-permute-start | bytes 786440 | tf_op jit(solution)/shard_map/ppermute | solution.py:215
  29.4 14.3 %collective-permute-start.16 = (bf16[128,1024]{1,0:T(8,128)(2,1)S(1)}, bf16[128,1024]{1,0:T(8,128)(2,1)S(1)}, u32[]{:S(2)}, u32[]{:S(2)}) collective-permute-start(bf16[128,1024]{1,0:T(8,128)(2,1)S(1)} %collective-permute-done.7.refs_4_), channel_id=1, source_target_pairs={{0,8},{2,10},{4,12},{6,14},{8,16},{10,18},{12,20},{14,22},{16,24},... | collective-permute-start | bytes 786440 | tf_op jit(solution)/shard_map/ppermute | solution.py:215
  32.3 6.3 %collective-permute-start.9 = (bf16[2,128,128]{2,1,0:T(8,128)(2,1)S(1)}, bf16[2,128,128]{2,1,0:T(8,128)(2,1)S(1)}, u32[]{:S(2)}, u32[]{:S(2)}) collective-permute-start(bf16[2,128,128]{2,1,0:T(8,128)(2,1)S(1)} %get-tuple-element.47), channel_id=1, source_target_pairs={{0,6},{2,4},{4,2},{6,0},{8,14},{10,12},{12,10},{14,8},{16,22},{18,... | collective-permute-start | bytes 196616 | tf_op jit(solution)/shard_map/ppermute | solution.py:212
  33.1 5.6 %collective-permute-start.13 = (bf16[2,128,128]{2,1,0:T(8,128)(2,1)S(1)}, bf16[2,128,128]{2,1,0:T(8,128)(2,1)S(1)}, u32[]{:S(2)}, u32[]{:S(2)}) collective-permute-start(bf16[2,128,128]{2,1,0:T(8,128)(2,1)S(1)} %get-tuple-element.55), channel_id=1, source_target_pairs={{0,2},{2,0},{4,6},{6,4},{8,10},{10,8},{12,14},{14,12},{16,18},{18,... | collective-permute-start | bytes 196616 | tf_op jit(solution)/shard_map/ppermute | solution.py:212
  34.7 5.0 %collective-permute-start.14 = (bf16[2,128,128]{2,1,0:T(8,128)(2,1)S(1)}, bf16[2,128,128]{2,1,0:T(8,128)(2,1)S(1)}, u32[]{:S(2)}, u32[]{:S(2)}) collective-permute-start(bf16[2,128,128]{2,1,0:T(8,128)(2,1)S(1)} %get-tuple-element.56), channel_id=1, source_target_pairs={{0,4},{2,6},{4,0},{6,2},{8,12},{10,14},{12,8},{14,10},{16,20},{18,... | collective-permute-start | bytes 196616 | tf_op jit(solution)/shard_map/ppermute | solution.py:212
  37.8 8.2 %collective-permute-start.21 = (bf16[128,1024]{1,0:T(8,128)(2,1)S(1)}, bf16[128,1024]{1,0:T(8,128)(2,1)S(1)}, u32[]{:S(2)}, u32[]{:S(2)}) collective-permute-start(bf16[128,1024]{1,0:T(8,128)(2,1)S(1)} %collective-permute-done.17.refs_12_.refs_4_), channel_id=1, source_target_pairs={{0,8},{2,10},{4,12},{6,14},{8,16},{10,18},{12,20},{14,22},{16,24},... | collective-permute-start | bytes 786440 | tf_op jit(solution)/shard_map/ppermute | solution.py:215
  40.5 6.4 %collective-permute-start.20 = (bf16[256,512]{1,0:T(8,128)(2,1)S(1)}, bf16[256,512]{1,0:T(8,128)(2,1)S(1)}, u32[]{:S(2)}, u32[]{:S(2)}) collective-permute-start(bf16[256,512]{1,0:T(8,128)(2,1)S(1)} %get-tuple-element.64), channel_id=1, source_target_pairs={{0,4},{2,6},{4,0},{6,2},{8,12},{10,14},{12,8},{14,10},{16,20},{18,... | collective-permute-start | bytes 786440 | tf_op jit(solution)/shard_map/ppermute | solution.py:212
  41.6 7.8 %collective-permute-start.18 = (bf16[128,1024]{1,0:T(8,128)(2,1)S(1)}, bf16[128,1024]{1,0:T(8,128)(2,1)S(1)}, u32[]{:S(2)}, u32[]{:S(2)}) collective-permute-start(bf16[128,1024]{1,0:T(8,128)(2,1)S(1)} %collective-permute-done.17.refs_12_.refs_4_), channel_id=1, source_target_pairs={{0,2},{2,0},{4,6},{6,4},{8,10},{10,8},{12,14},{14,12},{16,18},{18,... | collective-permute-start | bytes 786440 | tf_op jit(solution)/shard_map/ppermute | solution.py:212
  42.4 9.8 %collective-permute-start.15 = (bf16[256,512]{1,0:T(8,128)(2,1)S(1)}, bf16[256,512]{1,0:T(8,128)(2,1)S(1)}, u32[]{:S(2)}, u32[]{:S(2)}) collective-permute-start(bf16[256,512]{1,0:T(8,128)(2,1)S(1)} %get-tuple-element.58), channel_id=1, source_target_pairs={{0,2},{2,0},{4,6},{6,4},{8,10},{10,8},{12,14},{14,12},{16,18},{18,... | collective-permute-start | bytes 786440 | tf_op jit(solution)/shard_map/ppermute | solution.py:212
  43.7 8.6 %collective-permute-start.19 = (bf16[128,1024]{1,0:T(8,128)(2,1)S(1)}, bf16[128,1024]{1,0:T(8,128)(2,1)S(1)}, u32[]{:S(2)}, u32[]{:S(2)}) collective-permute-start(bf16[128,1024]{1,0:T(8,128)(2,1)S(1)} %collective-permute-done.16.refs_6_), channel_id=1, source_target_pairs={{0,4},{2,6},{4,0},{6,2},{8,12},{10,14},{12,8},{14,10},{16,20},{18,... | collective-permute-start | bytes 786440 | tf_op jit(solution)/shard_map/ppermute | solution.py:212
  46.9 8.1 %collective-permute-start.22 = (bf16[128,1024]{1,0:T(8,128)(2,1)S(1)}, bf16[128,1024]{1,0:T(8,128)(2,1)S(1)}, u32[]{:S(2)}, u32[]{:S(2)}) collective-permute-start(bf16[128,1024]{1,0:T(8,128)(2,1)S(1)} %collective-permute-done.21.refs_14_.refs_6_), channel_id=1, source_target_pairs={{0,2},{2,0},{4,6},{6,4},{8,10},{10,8},{12,14},{14,12},{16,18},{18,... | collective-permute-start | bytes 786440 | tf_op jit(solution)/shard_map/ppermute | solution.py:212
  47.5 7.5 %collective-permute-start.26 = (bf16[256,512]{1,0:T(8,128)(2,1)S(1)}, bf16[256,512]{1,0:T(8,128)(2,1)S(1)}, u32[]{:S(2)}, u32[]{:S(2)}) collective-permute-start(bf16[256,512]{1,0:T(8,128)(2,1)S(1)} %collective-permute-done.20.refs_8_), channel_id=1, source_target_pairs={{0,1},{1,0},{2,3},{3,2},{4,5},{5,4},{6,7},{7,6},{8,9},{9,8},{10,11... | collective-permute-start | bytes 786440 | tf_op jit(solution)/shard_map/ppermute | solution.py:221
  49.4 7.8 %collective-permute-start.11 = (bf16[128,1024]{1,0:T(8,128)(2,1)S(1)}, bf16[128,1024]{1,0:T(8,128)(2,1)S(1)}, u32[]{:S(2)}, u32[]{:S(2)}) collective-permute-start(bf16[128,1024]{1,0:T(8,128)(2,1)S(1)} %collective-permute-done.7.refs_4_), channel_id=1, source_target_pairs={{0,4},{2,6},{4,0},{6,2},{8,12},{10,14},{12,8},{14,10},{16,20},{18,... | collective-permute-start | bytes 786440 | tf_op jit(solution)/shard_map/ppermute | solution.py:212
  52.2 7.2 %collective-permute-start.23 = (bf16[256,1024]{1,0:T(8,128)(2,1)S(1)}, bf16[256,1024]{1,0:T(8,128)(2,1)S(1)}, u32[]{:S(2)}, u32[]{:S(2)}) collective-permute-start(bf16[256,1024]{1,0:T(8,128)(2,1)S(1)} %get-tuple-element.66.refs_16_), channel_id=1, source_target_pairs={{0,1},{1,0},{2,3},{3,2},{4,5},{5,4},{6,7},{7,6},{8,9},{9,8},{10,11... | collective-permute-start | bytes 1572872 | tf_op jit(solution)/shard_map/ppermute | solution.py:221
  55.8 11.7 %collective-permute-start.27 = (bf16[256,1024]{1,0:T(8,128)(2,1)S(1)}, bf16[256,1024]{1,0:T(8,128)(2,1)S(1)}, u32[]{:S(2)}, u32[]{:S(2)}) collective-permute-start(bf16[256,1024]{1,0:T(8,128)(2,1)S(1)} %shard_map.64), channel_id=1, source_target_pairs={{0,4},{2,6},{4,0},{6,2},{8,12},{10,14},{12,8},{14,10},{16,20},{18,... | collective-permute-start | bytes 1572872 | tf_op jit(solution)/shard_map/ppermute | solution.py:212
  57.9 11.3 %collective-permute-start.25 = (bf16[256,1024]{1,0:T(8,128)(2,1)S(1)}, bf16[256,1024]{1,0:T(8,128)(2,1)S(1)}, u32[]{:S(2)}, u32[]{:S(2)}) collective-permute-start(bf16[256,1024]{1,0:T(8,128)(2,1)S(1)} %shard_map.63), channel_id=1, source_target_pairs={{0,2},{2,0},{4,6},{6,4},{8,10},{10,8},{12,14},{14,12},{16,18},{18,... | collective-permute-start | bytes 1572872 | tf_op jit(solution)/shard_map/ppermute | solution.py:212
  (11 other events, 145.3 us)

commit v5 on v4

--- a/solution.py
+++ b/solution.py
@@ -12,14 +12,11 @@
 F32, BF16 = jnp.float32, jnp.bfloat16
 VMEM_LIMIT = 40 * 1024 * 1024
 
-COST = 0
-PER_US = 1.15e9
-
 ANY = pl.BlockSpec(memory_space=pl.ANY)
 VMEM = pl.BlockSpec(memory_space=pltpu.VMEM)
 
 
-def call(body, outs, ins, scratch=(), flops=0, moved=0, us=0.0):
+def call(body, outs, ins, scratch=(), flops=0):
     return pl.pallas_call(
         body,
         out_shape=outs,
@@ -27,7 +24,7 @@
         out_specs=[VMEM] * len(outs),
         scratch_shapes=list(scratch),
         compiler_params=pltpu.CompilerParams(vmem_limit_bytes=VMEM_LIMIT),
-        cost_estimate=pl.CostEstimate(flops=int(us * PER_US) if us and (COST or not flops) else flops, bytes_accessed=moved, transcendentals=0),
+        cost_estimate=pl.CostEstimate(flops=flops, bytes_accessed=0, transcendentals=0),
     )
 
 
@@ -111,16 +108,16 @@
         to_y[:, slot] = normed[:, head_cols(4 * (t // 2) + 2 * (1 - y) + t % 2)]
 
 
-def head_at(place, r, t, way, flip):
-    from_z = (place[1] + way * r) & 3
+def head_at(place, r, t, flip):
+    from_z = (place[1] - r) & 3
     return from_z >> 1, 4 * (from_z & 1) + (place[0] ^ (t * flip))
 
 
-def sums(place, pieces, got, way, flip, thin):
+def sums(place, pieces, got, flip, thin):
     left = []
     for r in range(4):
         for t in range(2):
-            core, head = head_at(place, r, t, way, flip)
+            core, head = head_at(place, r, t, flip)
             if thin:
                 head = (head >> 1) if flip == 2 else 2 * (head >> 2) + (head & 1)
             cols = head_cols(head)
@@ -130,22 +127,22 @@
     )
 
 
-def partner_kernel(way, flip, *refs):
+def partner_kernel(flip, *refs):
     place = spot()
     own, other, out, got = refs[8:]
     got[place[2]] = own[...]
     got[1 - place[2]] = other[...]
-    out[...] = sums(place, refs[:8], got, way, flip, True).astype(BF16)
-
-
-def own_kernel(ways, *refs):
+    out[...] = sums(place, refs[:8], got, flip, True).astype(BF16)
+
+
+def own_kernel(*refs):
     place = spot()
     own, other, out, got = refs[16:]
     got[place[2]] = own[...]
     got[1 - place[2]] = other[...]
     cut = refs[0].shape[1]
-    out[:, :cut] = sums(place, refs[:8], got, ways[0], 2, False)
-    out[:, cut:] = sums(place, refs[8:16], got, ways[1], 1, False)
+    out[:, :cut] = sums(place, refs[:8], got, 2, False)
+    out[:, cut:] = sums(place, refs[8:16], got, 1, False)
 
 
 def cut_kernel(block, first, second, sems):
@@ -190,12 +187,7 @@
     )(*([mine, part] + ([result] if result is not None else [])))
 
 
-CUT = 8
-ZD = 0
-DN = 0
-CUT_US = 0
-ORD = 0
-TIES = {'tot': '', 'z1': 'y0', 'z2': '', 'add': 'a2 x0', 'back': 'x1', 'norm': 'y1', 'act': '', 'act2': 'a3 x2 y3', 'act3': 'b3'}
+DEADLINES = {'shift1': 'y0', 'shifted': 'a2 x0', 'back': 'x1', 'states': 'y1', 'got_x': 'a3 x2 y3', 'got_y': 'b3'}
 
 
 def tie(value, *others):
@@ -211,8 +203,8 @@
     def partner(value, flip):
         return lax.ppermute(value, "seq", [(i, i ^ flip) for i in range(blocks)])
 
-    def ring(value, way=1):
-        return lax.ppermute(value, "seq", [(i, (i + way * PLANE) % blocks) for i in range(blocks)])
+    def ring(value):
+        return lax.ppermute(value, "seq", [(i, (i + PLANE) % blocks) for i in range(blocks)])
 
     def up(value, by):
         return lax.ppermute(value, "seq", [(i, i + by * PLANE) for i in range(blocks - by * PLANE)])
@@ -221,22 +213,19 @@
         return lax.ppermute(value, "mp", [(0, 1), (1, 0)])
 
     cols = w_out.shape[1]
-    half = cols * CUT // 16
-    def cut(block, us=0.0):
+    half = cols // 2
+
+    def cut(block):
         return call(
             cut_kernel,
             [shape((HD, half), BF16), shape((HD, cols - half), BF16)],
             [ANY],
             [pltpu.SemaphoreType.DMA((2,))],
-            us=us,
         )(block)
 
     held = {}
-    early_keys = keys
     if split:
-        held["a0"], held["b0"] = cut(w_out, CUT_US)
-        if CUT_US:
-            early_keys, held["a0"] = tie(keys, held["a0"])
+        held["a0"], held["b0"] = cut(w_out)
 
     def piece(n):
         if n not in held:
@@ -245,16 +234,13 @@
             elif n in ("a1", "b1"):
                 held["a1"], held["b1"] = cut(piece("r1"))
             elif n[0] in "ab":
-                if DN and n[1] == "3":
-                    held[n] = ring(piece(n[0] + "0"), -1)
-                else:
-                    held[n] = ring(piece(n[0] + str(int(n[1]) - 1)))
+                held[n] = ring(piece(n[0] + str(int(n[1]) - 1)))
             else:
                 held[n] = partner(piece({"x": "b", "y": "a"}[n[0]] + n[1]), {"x": 1, "y": 2}[n[0]])
         return held[n]
 
     def tied(value, name):
-        names = TIES[name].split() if split else []
+        names = DEADLINES.get(name, "").split() if split else []
         if not names:
             return value
         value, *rest = tie(value, *[piece(n) for n in names])
@@ -263,34 +249,29 @@
 
     per = heads // PLANE
     quarter = shape((per, HD, HD), BF16)
-    own = call(states_kernel, [quarter] * PLANE, [VMEM, VMEM], flops=2 * rows * feats * HD, us=1.1)(
-        early_keys, values
-    )
+    own = call(states_kernel, [quarter] * PLANE, [VMEM, VMEM], flops=2 * rows * feats * HD)(keys, values)
     intra, feat = call(
-        intra_kernel, [shape((rows, feats), F32), shape((rows, feats), BF16)], [VMEM] * 3, flops=4 * rows * rows * feats, us=1.0
+        intra_kernel, [shape((rows, feats), F32), shape((rows, feats), BF16)], [VMEM] * 3, flops=4 * rows * rows * feats
     )(queries, keys, values)
     mine = [own[0]] + [partner(own[j], j) for j in range(1, PLANE)]
-    mine[3] = tied(mine[3], "tot")
+    mine[3] = tied(mine[3], "plane")
     (running,) = call(total_kernel, [quarter], [VMEM] * PLANE)(*mine)
-    running = tied(running, "z1")
-    if split and ZD:
-        shifts = [up(running, by) for by in range(1, blocks // PLANE)]
-    else:
-        shifts, by = [], 1
-        while by * PLANE < blocks:
-            if by == 2:
-                running = tied(running, "z2")
-            shifts.append(up(running, by))
-            running = (running.astype(F32) + shifts[-1].astype(F32)).astype(BF16)
-            by *= 2
-    shifts[-1] = tied(shifts[-1], "add")
+    running = tied(running, "shift1")
+    shifts, by = [], 1
+    while by * PLANE < blocks:
+        if by == 2:
+            running = tied(running, "shift2")
+        shifts.append(up(running, by))
+        running = (running.astype(F32) + shifts[-1].astype(F32)).astype(BF16)
+        by *= 2
+    shifts[-1] = tied(shifts[-1], "shifted")
     prefixes = call(
-        functools.partial(prefixes_kernel, len(shifts)), [quarter] * PLANE, [VMEM] * (PLANE + len(shifts)), flops=1
+        functools.partial(prefixes_kernel, len(shifts)), [quarter] * PLANE, [VMEM] * (PLANE + len(shifts))
     )(*mine, *shifts)
     prefixes = list(prefixes)
     prefixes[1] = tied(prefixes[1], "back")
     states = [prefixes[0]] + [partner(prefixes[j], j) for j in range(1, PLANE)]
-    states[3] = tied(states[3], "norm")
+    states[3] = tied(states[3], "states")
     gain = norm_gain.reshape(1, feats)
     normed_args = (intra, feat, *states, gain)
 
@@ -305,46 +286,35 @@
         [shape((rows, feats), BF16)] + [shape((rows, feats // 2), BF16)] * 2,
         [VMEM] * 7,
         flops=2 * rows * feats * HD,
-        us=1.2,
     )(*normed_args)
-    if TIES["act"]:
-        to_x, to_y = tie(to_x, to_y)
-    to_x = tied(to_x, "act")
+    to_x = tied(to_x, "send")
     got_x, got_y = partner(to_x, 1), partner(to_y, 2)
-    got_x = tied(got_x, "act2")
-    got_y = tied(got_y, "act3")
+    got_x = tied(got_x, "got_x")
+    got_y = tied(got_y, "got_y")
     wa, wb = [], []
     for r in range(4):
         wa += [piece("a%d" % r), piece("y%d" % r)]
         wb += [piece("b%d" % r), piece("x%d" % r)]
     other = swap(normed)
-    ways = (-1, -1)
-    swapped = [swap(got_x), swap(got_y)]
-    parts = [None, None]
-    turns = [(0, 2, wa, got_x), (1, 1, wb, got_y)]
-    for at, flip, pieces, got in turns[::-1] if ORD == 2 else turns:
-        width = pieces[0].shape[1]
+    parts = []
+    for flip, pieces, got in ((2, wa, got_x), (1, wb, got_y)):
         (part,) = call(
-            functools.partial(partner_kernel, ways[at], flip),
-            [shape((rows, width), BF16)],
+            functools.partial(partner_kernel, flip),
+            [shape((rows, half), BF16)],
             [VMEM] * 10,
             [pltpu.VMEM((2, rows, feats // 2), BF16)],
-            flops=rows * feats * width * 2,
-            us=1.3,
-        )(*pieces, got, swapped[at])
-        if ORD and parts[1 - at] is None:
-            part, swapped[1 - at] = tie(part, swapped[1 - at])
-        parts[at] = partner(part, 3 - flip)
+            flops=rows * feats * half * 2,
+        )(*pieces, got, swap(got))
+        parts.append(partner(part, 3 - flip))
     (mine_all,) = call(
-        functools.partial(own_kernel, ways),
+        own_kernel,
         [shape((rows, cols), F32)],
         [VMEM] * 18,
         [pltpu.VMEM((2, rows, feats), BF16)],
         flops=rows * feats * cols * 2,
-        us=2.0,
     )(*wa, *wb, normed, other)
     result = None
-    for at, part in ((0, parts[0]), (half, parts[1]))[:: 1 if ORD == 1 else -1]:
+    for at, part in ((half, parts[1]), (0, parts[0])):
         result = finish(mine_all, part, at, result)
     return result
 

time: 70.5 us -> 70.5 us (level)
  no operation moved by 1% of the time
where the time goes in v5:
time: 70.5 us; the launch traced here: 70.1 us
  starting transfers between devices  36.8 us (52%)
  waiting for transfers between devices  22.8 us (32%)
  Pallas kernels  7.13 us (10%)
  local copies, waits for them, and re-layouts  3.17 us (4%)
    ppermute x18, starting transfers between devices, partner(): return lax.ppermute(value, 'seq', [(i, i ^ flip) for i in range(blocks)])  21.2 us
    ppermute x18, waiting for transfers between devices, partner(): return lax.ppermute(value, 'seq', [(i, i ^ flip) for i in range(blocks)])  20.5 us
    ppermute x5, starting transfers between devices, ring(): lax.ppermute(value, 'seq', [(i, (i + PLANE) % blocks) for i in range(bloc...  9.29 us
    ppermute x2, starting transfers between devices, up(): lax.ppermute(value, 'seq', [(i, i + by * PLANE) for i in range(blocks - b...  5.8 us
    unnamed x14, local copies, waits for them, and re-layouts  3.17 us
    ppermute x5, waiting for transfers between devices, ring(): lax.ppermute(value, 'seq', [(i, (i + PLANE) % blocks) for i in range(bloc...  2.29 us
    pallas_call x2, Pallas kernels, finish(): pl.pallas_call(functools.partial(finish_kernel, at), out_shape=shape(mine...  1.68 us
    pallas_call x2, Pallas kernels, per_device(): call(functools.partial(partner_kernel, flip), [shape((rows, half), BF16)]...  1.48 us
  transfers between devices with their start and end apart: 28, of which 15 were waited for; matrix products, arithmetic and copies ran while one was open for 0% of the time, Pallas kernels for 9%

profile of v5, /device:TPU:0, one launch (start us, length us, event | category | flops | bytes accessed | tf_op | source)
XLA Modules:
  0.0 70.1 jit_solution(14993005839283415271)
XLA Ops:
  0.0 3.0 %collective-permute-start.4 = (bf16[128,2048]{1,0:T(8,128)(2,1)}, bf16[128,2048]{1,0:T(8,128)(2,1)S(1)}, u32[]{:S(2)}, u32[]{:S(2)}) collective-permute-start(bf16[128,2048]{1,0:T(8,128)(2,1)} %block.1), channel_id=1, source_target_pairs={{0,8},{2,10},{4,12},{6,14},{8,16},{10,18},{12,20},{14,22},{16,24},... | collective-permute-start | bytes 1572872 | tf_op jit(solution)/shard_map/ppermute | solution.py:207
  4.2 1.6 %collective-permute-start.3 = (bf16[128,1024]{1,0:T(8,128)(2,1)S(1)}, bf16[128,1024]{1,0:T(8,128)(2,1)S(1)}, u32[]{:S(2)}, u32[]{:S(2)}) collective-permute-start(bf16[128,1024]{1,0:T(8,128)(2,1)S(1)} %get-tuple-element.37.refs_0_), channel_id=1, source_target_pairs={{0,4},{2,6},{4,0},{6,2},{8,12},{10,14},{12,8},{14,10},{16,20},{18,... | collective-permute-start | bytes 786440 | tf_op jit(solution)/shard_map/ppermute | solution.py:204
  8.4 1.5 %collective-permute-start = (bf16[2,128,128]{2,1,0:T(8,128)(2,1)S(1)}, bf16[2,128,128]{2,1,0:T(8,128)(2,1)S(1)}, u32[]{:S(2)}, u32[]{:S(2)}) collective-permute-start(bf16[2,128,128]{2,1,0:T(8,128)(2,1)S(1)} %get-tuple-element.39), channel_id=1, source_target_pairs={{0,2},{2,0},{4,6},{6,4},{8,10},{10,8},{12,14},{14,12},{16,18},{18,... | collective-permute-start | bytes 196616 | tf_op jit(solution)/shard_map/ppermute | solution.py:204
  10.5 1.5 %collective-permute-start.2 = (bf16[2,128,128]{2,1,0:T(8,128)(2,1)S(1)}, bf16[2,128,128]{2,1,0:T(8,128)(2,1)S(1)}, u32[]{:S(2)}, u32[]{:S(2)}) collective-permute-start(bf16[2,128,128]{2,1,0:T(8,128)(2,1)S(1)} %get-tuple-element.41), channel_id=1, source_target_pairs={{0,6},{2,4},{4,2},{6,0},{8,14},{10,12},{12,10},{14,8},{16,22},{18,... | collective-permute-start | bytes 196616 | tf_op jit(solution)/shard_map/ppermute | solution.py:204
  12.8 1.4 %collective-permute-done.1.a2.refs_2_ = bf16[2,128,128]{2,1,0:T(8,128)(2,1)S(1)} collective-permute-done((bf16[2,128,128]{2,1,0:T(8,128)(2,1)S(1)}, bf16[2,128,128]{2,1,0:T(8,128)(2,1)S(1)}, u32[]{:S(2)}, u32[]{:S(2)}) %collective-permute-start.1) | collective-permute-done | bytes 65568 | tf_op jit(solution)/shard_map/ppermute | solution.py:204
  14.2 1.4 %collective-permute-done.2.a3.refs_3_ = bf16[2,128,128]{2,1,0:T(8,128)(2,1)S(1)} collective-permute-done((bf16[2,128,128]{2,1,0:T(8,128)(2,1)S(1)}, bf16[2,128,128]{2,1,0:T(8,128)(2,1)S(1)}, u32[]{:S(2)}, u32[]{:S(2)}) %collective-permute-start.2) | collective-permute-done | bytes 65568 | tf_op jit(solution)/shard_map/ppermute | solution.py:204
  15.7 3.5 %collective-permute-start.5 = (bf16[2,128,128]{2,1,0:T(8,128)(2,1)S(1)}, bf16[2,128,128]{2,1,0:T(8,128)(2,1)S(1)}, u32[]{:S(2)}, u32[]{:S(2)}) collective-permute-start(bf16[2,128,128]{2,1,0:T(8,128)(2,1)S(1)} %shard_map.57), channel_id=1, source_target_pairs={{0,8},{2,10},{4,12},{6,14},{8,16},{10,18},{12,20},{14,22},{16,24},... | collective-permute-start | bytes 196616 | tf_op jit(solution)/shard_map/ppermute | solution.py:210
  20.0 1.6 %collective-permute-start.7 = (bf16[128,1024]{1,0:T(8,128)(2,1)S(1)}, bf16[128,1024]{1,0:T(8,128)(2,1)S(1)}, u32[]{:S(2)}, u32[]{:S(2)}) collective-permute-start(bf16[128,1024]{1,0:T(8,128)(2,1)S(1)} %get-tuple-element.43.refs_2_), channel_id=1, source_target_pairs={{0,8},{2,10},{4,12},{6,14},{8,16},{10,18},{12,20},{14,22},{16,24},... | collective-permute-start | bytes 786440 | tf_op jit(solution)/shard_map/ppermute | solution.py:207
  21.6 1.5 %collective-permute-start.10 = (bf16[128,1024]{1,0:T(8,128)(2,1)S(1)}, bf16[128,1024]{1,0:T(8,128)(2,1)S(1)}, u32[]{:S(2)}, u32[]{:S(2)}) collective-permute-start(bf16[128,1024]{1,0:T(8,128)(2,1)S(1)} %get-tuple-element.43.refs_2_), channel_id=1, source_target_pairs={{0,4},{2,6},{4,0},{6,2},{8,12},{10,14},{12,8},{14,10},{16,20},{18,... | collective-permute-start | bytes 786440 | tf_op jit(solution)/shard_map/ppermute | solution.py:204
  23.1 1.4 %collective-permute-start.12 = (bf16[128,1024]{1,0:T(8,128)(2,1)S(1)}, bf16[128,1024]{1,0:T(8,128)(2,1)S(1)}, u32[]{:S(2)}, u32[]{:S(2)}) collective-permute-start(bf16[128,1024]{1,0:T(8,128)(2,1)S(1)} %get-tuple-element.54.refs_10_.refs_2_), channel_id=1, source_target_pairs={{0,2},{2,0},{4,6},{6,4},{8,10},{10,8},{12,14},{14,12},{16,18},{18,... | collective-permute-start | bytes 786440 | tf_op jit(solution)/shard_map/ppermute | solution.py:204
  24.5 2.3 %collective-permute-start.6 = (bf16[2,128,128]{2,1,0:T(8,128)(2,1)S(1)}, bf16[2,128,128]{2,1,0:T(8,128)(2,1)S(1)}, u32[]{:S(2)}, u32[]{:S(2)}) collective-permute-start(bf16[2,128,128]{2,1,0:T(8,128)(2,1)S(1)} %add_convert_fusion), channel_id=1, source_target_pairs={{0,16},{2,18},{4,20},{6,22},{8,24},{10,26},{12,28},{14,30},{1,17},... | collective-permute-start | bytes 196616 | tf_op jit(solution)/shard_map/ppermute | solution.py:210
  26.9 1.3 %collective-permute-done.8.refs_9_.refs_1_ = bf16[128,1024]{1,0:T(8,128)(2,1)S(1)} collective-permute-done((bf16[128,1024]{1,0:T(8,128)(2,1)S(1)}, bf16[128,1024]{1,0:T(8,128)(2,1)S(1)}, u32[]{:S(2)}, u32[]{:S(2)}) %collective-permute-start.8) | collective-permute-done | bytes 262176 | tf_op jit(solution)/shard_map/ppermute | solution.py:204
  29.4 2.7 %collective-permute-start.16 = (bf16[128,1024]{1,0:T(8,128)(2,1)S(1)}, bf16[128,1024]{1,0:T(8,128)(2,1)S(1)}, u32[]{:S(2)}, u32[]{:S(2)}) collective-permute-start(bf16[128,1024]{1,0:T(8,128)(2,1)S(1)} %collective-permute-done.7.refs_4_), channel_id=1, source_target_pairs={{0,8},{2,10},{4,12},{6,14},{8,16},{10,18},{12,20},{14,22},{16,24},... | collective-permute-start | bytes 786440 | tf_op jit(solution)/shard_map/ppermute | solution.py:207
  33.1 1.6 %collective-permute-start.13 = (bf16[2,128,128]{2,1,0:T(8,128)(2,1)S(1)}, bf16[2,128,128]{2,1,0:T(8,128)(2,1)S(1)}, u32[]{:S(2)}, u32[]{:S(2)}) collective-permute-start(bf16[2,128,128]{2,1,0:T(8,128)(2,1)S(1)} %get-tuple-element.55), channel_id=1, source_target_pairs={{0,2},{2,0},{4,6},{6,4},{8,10},{10,8},{12,14},{14,12},{16,18},{18,... | collective-permute-start | bytes 196616 | tf_op jit(solution)/shard_map/ppermute | solution.py:204
  42.4 1.2 %collective-permute-start.15 = (bf16[256,512]{1,0:T(8,128)(2,1)S(1)}, bf16[256,512]{1,0:T(8,128)(2,1)S(1)}, u32[]{:S(2)}, u32[]{:S(2)}) collective-permute-start(bf16[256,512]{1,0:T(8,128)(2,1)S(1)} %get-tuple-element.58), channel_id=1, source_target_pairs={{0,2},{2,0},{4,6},{6,4},{8,10},{10,8},{12,14},{14,12},{16,18},{18,... | collective-permute-start | bytes 786440 | tf_op jit(solution)/shard_map/ppermute | solution.py:204
  44.6 1.3 %collective-permute-done.21.refs_14_.refs_6_ = bf16[128,1024]{1,0:T(8,128)(2,1)S(1)} collective-permute-done((bf16[128,1024]{1,0:T(8,128)(2,1)S(1)}, bf16[128,1024]{1,0:T(8,128)(2,1)S(1)}, u32[]{:S(2)}, u32[]{:S(2)}) %collective-permute-start.21) | collective-permute-done | bytes 262176 | tf_op jit(solution)/shard_map/ppermute | solution.py:207
  47.5 1.9 %collective-permute-done.18.refs_13_.refs_5_ = bf16[128,1024]{1,0:T(8,128)(2,1)S(1)} collective-permute-done((bf16[128,1024]{1,0:T(8,128)(2,1)S(1)}, bf16[128,1024]{1,0:T(8,128)(2,1)S(1)}, u32[]{:S(2)}, u32[]{:S(2)}) %collective-permute-start.18) | collective-permute-done | bytes 262176 | tf_op jit(solution)/shard_map/ppermute | solution.py:204
  49.4 1.3 %collective-permute-start.11 = (bf16[128,1024]{1,0:T(8,128)(2,1)S(1)}, bf16[128,1024]{1,0:T(8,128)(2,1)S(1)}, u32[]{:S(2)}, u32[]{:S(2)}) collective-permute-start(bf16[128,1024]{1,0:T(8,128)(2,1)S(1)} %collective-permute-done.7.refs_4_), channel_id=1, source_target_pairs={{0,4},{2,6},{4,0},{6,2},{8,12},{10,14},{12,8},{14,10},{16,20},{18,... | collective-permute-start | bytes 786440 | tf_op jit(solution)/shard_map/ppermute | solution.py:204
  50.7 1.5 %collective-permute-done.15.refs_8_ = bf16[256,512]{1,0:T(8,128)(2,1)S(1)} collective-permute-done((bf16[256,512]{1,0:T(8,128)(2,1)S(1)}, bf16[256,512]{1,0:T(8,128)(2,1)S(1)}, u32[]{:S(2)}, u32[]{:S(2)}) %collective-permute-start.15) | collective-permute-done | bytes 262176 | tf_op jit(solution)/shard_map/ppermute | solution.py:204
  52.7 2.3 %collective-permute-done.22.refs_15_.refs_7_ = bf16[128,1024]{1,0:T(8,128)(2,1)S(1)} collective-permute-done((bf16[128,1024]{1,0:T(8,128)(2,1)S(1)}, bf16[128,1024]{1,0:T(8,128)(2,1)S(1)}, u32[]{:S(2)}, u32[]{:S(2)}) %collective-permute-start.22) | collective-permute-done | bytes 262176 | tf_op jit(solution)/shard_map/ppermute | solution.py:204
  55.8 1.4 %collective-permute-start.27 = (bf16[256,1024]{1,0:T(8,128)(2,1)S(1)}, bf16[256,1024]{1,0:T(8,128)(2,1)S(1)}, u32[]{:S(2)}, u32[]{:S(2)}) collective-permute-start(bf16[256,1024]{1,0:T(8,128)(2,1)S(1)} %shard_map.64), channel_id=1, source_target_pairs={{0,4},{2,6},{4,0},{6,2},{8,12},{10,14},{12,8},{14,10},{16,20},{18,... | collective-permute-start | bytes 1572872 | tf_op jit(solution)/shard_map/ppermute | solution.py:204
  57.9 1.4 %collective-permute-start.25 = (bf16[256,1024]{1,0:T(8,128)(2,1)S(1)}, bf16[256,1024]{1,0:T(8,128)(2,1)S(1)}, u32[]{:S(2)}, u32[]{:S(2)}) collective-permute-start(bf16[256,1024]{1,0:T(8,128)(2,1)S(1)} %shard_map.63), channel_id=1, source_target_pairs={{0,2},{2,0},{4,6},{6,4},{8,10},{10,8},{12,14},{14,12},{16,18},{18,... | collective-permute-start | bytes 1572872 | tf_op jit(solution)/shard_map/ppermute | solution.py:204
  59.4 1.3 %shard_map.62.mine = f32[256,2048]{1,0:T(8,128)S(1)} custom-call(bf16[128,1024]{1,0:T(8,128)(2,1)S(1)} %get-tuple-element.37.refs_0_, bf16[128,1024]{1,0:T(8,128)(2,1)S(1)} %collective-permute-done.3.refs_1_, bf16[128,1024]{1,0:T(8,128)(2,1)S(1)} %get-tuple-element.43.refs_2_, bf16[128,1024]{1,0:T(8,128)(2,1)S(1)} %collective-permute-done.10.refs_3_, ...), custom_call_target="tpu_custom_call" | custom-call | flops 1073741824 | tf_op jit(solution)/shard_map/pallas_call | solution.py:309
  60.7 6.8 %collective-permute-done.27.part = bf16[256,1024]{1,0:T(8,128)(2,1)S(1)} collective-permute-done((bf16[256,1024]{1,0:T(8,128)(2,1)S(1)}, bf16[256,1024]{1,0:T(8,128)(2,1)S(1)}, u32[]{:S(2)}, u32[]{:S(2)}) %collective-permute-start.27) | collective-permute-done | bytes 524320 | tf_op jit(solution)/shard_map/ppermute | solution.py:204
  (59 shorter events, 23.0 us)
Async XLA Ops:
  0.0 19.9 %collective-permute-start.4 = (bf16[128,2048]{1,0:T(8,128)(2,1)}, bf16[128,2048]{1,0:T(8,128)(2,1)S(1)}, u32[]{:S(2)}, u32[]{:S(2)}) collective-permute-start(bf16[128,2048]{1,0:T(8,128)(2,1)} %block.1), channel_id=1, source_target_pairs={{0,8},{2,10},{4,12},{6,14},{8,16},{10,18},{12,20},{14,22},{16,24},... | collective-permute-start | bytes 1572872 | tf_op jit(solution)/shard_map/ppermute | solution.py:207
  4.2 11.5 %collective-permute-start.3 = (bf16[128,1024]{1,0:T(8,128)(2,1)S(1)}, bf16[128,1024]{1,0:T(8,128)(2,1)S(1)}, u32[]{:S(2)}, u32[]{:S(2)}) collective-permute-start(bf16[128,1024]{1,0:T(8,128)(2,1)S(1)} %get-tuple-element.37.refs_0_), channel_id=1, source_target_pairs={{0,4},{2,6},{4,0},{6,2},{8,12},{10,14},{12,8},{14,10},{16,20},{18,... | collective-permute-start | bytes 786440 | tf_op jit(solution)/shard_map/ppermute | solution.py:204
  10.5 5.2 %collective-permute-start.2 = (bf16[2,128,128]{2,1,0:T(8,128)(2,1)S(1)}, bf16[2,128,128]{2,1,0:T(8,128)(2,1)S(1)}, u32[]{:S(2)}, u32[]{:S(2)}) collective-permute-start(bf16[2,128,128]{2,1,0:T(8,128)(2,1)S(1)} %get-tuple-element.41), channel_id=1, source_target_pairs={{0,6},{2,4},{4,2},{6,0},{8,14},{10,12},{12,10},{14,8},{16,22},{18,... | collective-permute-start | bytes 196616 | tf_op jit(solution)/shard_map/ppermute | solution.py:204
  15.7 8.8 %collective-permute-start.5 = (bf16[2,128,128]{2,1,0:T(8,128)(2,1)S(1)}, bf16[2,128,128]{2,1,0:T(8,128)(2,1)S(1)}, u32[]{:S(2)}, u32[]{:S(2)}) collective-permute-start(bf16[2,128,128]{2,1,0:T(8,128)(2,1)S(1)} %shard_map.57), channel_id=1, source_target_pairs={{0,8},{2,10},{4,12},{6,14},{8,16},{10,18},{12,20},{14,22},{16,24},... | collective-permute-start | bytes 196616 | tf_op jit(solution)/shard_map/ppermute | solution.py:210
  19.2 9.0 %collective-permute-start.8 = (bf16[128,1024]{1,0:T(8,128)(2,1)S(1)}, bf16[128,1024]{1,0:T(8,128)(2,1)S(1)}, u32[]{:S(2)}, u32[]{:S(2)}) collective-permute-start(bf16[128,1024]{1,0:T(8,128)(2,1)S(1)} %get-tuple-element.45.refs_8_.refs_0_), channel_id=1, source_target_pairs={{0,2},{2,0},{4,6},{6,4},{8,10},{10,8},{12,14},{14,12},{16,18},{18,... | collective-permute-start | bytes 786440 | tf_op jit(solution)/shard_map/ppermute | solution.py:204
  20.0 9.4 %collective-permute-start.7 = (bf16[128,1024]{1,0:T(8,128)(2,1)S(1)}, bf16[128,1024]{1,0:T(8,128)(2,1)S(1)}, u32[]{:S(2)}, u32[]{:S(2)}) collective-permute-start(bf16[128,1024]{1,0:T(8,128)(2,1)S(1)} %get-tuple-element.43.refs_2_), channel_id=1, source_target_pairs={{0,8},{2,10},{4,12},{6,14},{8,16},{10,18},{12,20},{14,22},{16,24},... | collective-permute-start | bytes 786440 | tf_op jit(solution)/shard_map/ppermute | solution.py:207
  21.6 13.1 %collective-permute-start.10 = (bf16[128,1024]{1,0:T(8,128)(2,1)S(1)}, bf16[128,1024]{1,0:T(8,128)(2,1)S(1)}, u32[]{:S(2)}, u32[]{:S(2)}) collective-permute-start(bf16[128,1024]{1,0:T(8,128)(2,1)S(1)} %get-tuple-element.43.refs_2_), channel_id=1, source_target_pairs={{0,4},{2,6},{4,0},{6,2},{8,12},{10,14},{12,8},{14,10},{16,20},{18,... | collective-permute-start | bytes 786440 | tf_op jit(solution)/shard_map/ppermute | solution.py:204
  23.1 10.0 %collective-permute-start.12 = (bf16[128,1024]{1,0:T(8,128)(2,1)S(1)}, bf16[128,1024]{1,0:T(8,128)(2,1)S(1)}, u32[]{:S(2)}, u32[]{:S(2)}) collective-permute-start(bf16[128,1024]{1,0:T(8,128)(2,1)S(1)} %get-tuple-element.54.refs_10_.refs_2_), channel_id=1, source_target_pairs={{0,2},{2,0},{4,6},{6,4},{8,10},{10,8},{12,14},{14,12},{16,18},{18,... | collective-permute-start | bytes 786440 | tf_op jit(solution)/shard_map/ppermute | solution.py:204
  28.2 9.6 %collective-permute-start.17 = (bf16[128,1024]{1,0:T(8,128)(2,1)S(1)}, bf16[128,1024]{1,0:T(8,128)(2,1)S(1)}, u32[]{:S(2)}, u32[]{:S(2)}) collective-permute-start(bf16[128,1024]{1,0:T(8,128)(2,1)S(1)} %get-tuple-element.54.refs_10_.refs_2_), channel_id=1, source_target_pairs={{0,8},{2,10},{4,12},{6,14},{8,16},{10,18},{12,20},{14,22},{16,24},... | collective-permute-start | bytes 786440 | tf_op jit(solution)/shard_map/ppermute | solution.py:207
  29.4 14.3 %collective-permute-start.16 = (bf16[128,1024]{1,0:T(8,128)(2,1)S(1)}, bf16[128,1024]{1,0:T(8,128)(2,1)S(1)}, u32[]{:S(2)}, u32[]{:S(2)}) collective-permute-start(bf16[128,1024]{1,0:T(8,128)(2,1)S(1)} %collective-permute-done.7.refs_4_), channel_id=1, source_target_pairs={{0,8},{2,10},{4,12},{6,14},{8,16},{10,18},{12,20},{14,22},{16,24},... | collective-permute-start | bytes 786440 | tf_op jit(solution)/shard_map/ppermute | solution.py:207
  32.3 6.3 %collective-permute-start.9 = (bf16[2,128,128]{2,1,0:T(8,128)(2,1)S(1)}, bf16[2,128,128]{2,1,0:T(8,128)(2,1)S(1)}, u32[]{:S(2)}, u32[]{:S(2)}) collective-permute-start(bf16[2,128,128]{2,1,0:T(8,128)(2,1)S(1)} %get-tuple-element.47), channel_id=1, source_target_pairs={{0,6},{2,4},{4,2},{6,0},{8,14},{10,12},{12,10},{14,8},{16,22},{18,... | collective-permute-start | bytes 196616 | tf_op jit(solution)/shard_map/ppermute | solution.py:204
  33.1 5.6 %collective-permute-start.13 = (bf16[2,128,128]{2,1,0:T(8,128)(2,1)S(1)}, bf16[2,128,128]{2,1,0:T(8,128)(2,1)S(1)}, u32[]{:S(2)}, u32[]{:S(2)}) collective-permute-start(bf16[2,128,128]{2,1,0:T(8,128)(2,1)S(1)} %get-tuple-element.55), channel_id=1, source_target_pairs={{0,2},{2,0},{4,6},{6,4},{8,10},{10,8},{12,14},{14,12},{16,18},{18,... | collective-permute-start | bytes 196616 | tf_op jit(solution)/shard_map/ppermute | solution.py:204
  34.7 5.0 %collective-permute-start.14 = (bf16[2,128,128]{2,1,0:T(8,128)(2,1)S(1)}, bf16[2,128,128]{2,1,0:T(8,128)(2,1)S(1)}, u32[]{:S(2)}, u32[]{:S(2)}) collective-permute-start(bf16[2,128,128]{2,1,0:T(8,128)(2,1)S(1)} %get-tuple-element.56), channel_id=1, source_target_pairs={{0,4},{2,6},{4,0},{6,2},{8,12},{10,14},{12,8},{14,10},{16,20},{18,... | collective-permute-start | bytes 196616 | tf_op jit(solution)/shard_map/ppermute | solution.py:204
  37.8 8.2 %collective-permute-start.21 = (bf16[128,1024]{1,0:T(8,128)(2,1)S(1)}, bf16[128,1024]{1,0:T(8,128)(2,1)S(1)}, u32[]{:S(2)}, u32[]{:S(2)}) collective-permute-start(bf16[128,1024]{1,0:T(8,128)(2,1)S(1)} %collective-permute-done.17.refs_12_.refs_4_), channel_id=1, source_target_pairs={{0,8},{2,10},{4,12},{6,14},{8,16},{10,18},{12,20},{14,22},{16,24},... | collective-permute-start | bytes 786440 | tf_op jit(solution)/shard_map/ppermute | solution.py:207
  40.5 6.4 %collective-permute-start.20 = (bf16[256,512]{1,0:T(8,128)(2,1)S(1)}, bf16[256,512]{1,0:T(8,128)(2,1)S(1)}, u32[]{:S(2)}, u32[]{:S(2)}) collective-permute-start(bf16[256,512]{1,0:T(8,128)(2,1)S(1)} %get-tuple-element.64), channel_id=1, source_target_pairs={{0,4},{2,6},{4,0},{6,2},{8,12},{10,14},{12,8},{14,10},{16,20},{18,... | collective-permute-start | bytes 786440 | tf_op jit(solution)/shard_map/ppermute | solution.py:204
  41.6 7.8 %collective-permute-start.18 = (bf16[128,1024]{1,0:T(8,128)(2,1)S(1)}, bf16[128,1024]{1,0:T(8,128)(2,1)S(1)}, u32[]{:S(2)}, u32[]{:S(2)}) collective-permute-start(bf16[128,1024]{1,0:T(8,128)(2,1)S(1)} %collective-permute-done.17.refs_12_.refs_4_), channel_id=1, source_target_pairs={{0,2},{2,0},{4,6},{6,4},{8,10},{10,8},{12,14},{14,12},{16,18},{18,... | collective-permute-start | bytes 786440 | tf_op jit(solution)/shard_map/ppermute | solution.py:204
  42.4 9.8 %collective-permute-start.15 = (bf16[256,512]{1,0:T(8,128)(2,1)S(1)}, bf16[256,512]{1,0:T(8,128)(2,1)S(1)}, u32[]{:S(2)}, u32[]{:S(2)}) collective-permute-start(bf16[256,512]{1,0:T(8,128)(2,1)S(1)} %get-tuple-element.58), channel_id=1, source_target_pairs={{0,2},{2,0},{4,6},{6,4},{8,10},{10,8},{12,14},{14,12},{16,18},{18,... | collective-permute-start | bytes 786440 | tf_op jit(solution)/shard_map/ppermute | solution.py:204
  43.7 8.6 %collective-permute-start.19 = (bf16[128,1024]{1,0:T(8,128)(2,1)S(1)}, bf16[128,1024]{1,0:T(8,128)(2,1)S(1)}, u32[]{:S(2)}, u32[]{:S(2)}) collective-permute-start(bf16[128,1024]{1,0:T(8,128)(2,1)S(1)} %collective-permute-done.16.refs_6_), channel_id=1, source_target_pairs={{0,4},{2,6},{4,0},{6,2},{8,12},{10,14},{12,8},{14,10},{16,20},{18,... | collective-permute-start | bytes 786440 | tf_op jit(solution)/shard_map/ppermute | solution.py:204
  46.9 8.1 %collective-permute-start.22 = (bf16[128,1024]{1,0:T(8,128)(2,1)S(1)}, bf16[128,1024]{1,0:T(8,128)(2,1)S(1)}, u32[]{:S(2)}, u32[]{:S(2)}) collective-permute-start(bf16[128,1024]{1,0:T(8,128)(2,1)S(1)} %collective-permute-done.21.refs_14_.refs_6_), channel_id=1, source_target_pairs={{0,2},{2,0},{4,6},{6,4},{8,10},{10,8},{12,14},{14,12},{16,18},{18,... | collective-permute-start | bytes 786440 | tf_op jit(solution)/shard_map/ppermute | solution.py:204
  47.5 7.5 %collective-permute-start.26 = (bf16[256,512]{1,0:T(8,128)(2,1)S(1)}, bf16[256,512]{1,0:T(8,128)(2,1)S(1)}, u32[]{:S(2)}, u32[]{:S(2)}) collective-permute-start(bf16[256,512]{1,0:T(8,128)(2,1)S(1)} %collective-permute-done.20.refs_8_), channel_id=1, source_target_pairs={{0,1},{1,0},{2,3},{3,2},{4,5},{5,4},{6,7},{7,6},{8,9},{9,8},{10,11... | collective-permute-start | bytes 786440 | tf_op jit(solution)/shard_map/ppermute | solution.py:213
  49.4 7.8 %collective-permute-start.11 = (bf16[128,1024]{1,0:T(8,128)(2,1)S(1)}, bf16[128,1024]{1,0:T(8,128)(2,1)S(1)}, u32[]{:S(2)}, u32[]{:S(2)}) collective-permute-start(bf16[128,1024]{1,0:T(8,128)(2,1)S(1)} %collective-permute-done.7.refs_4_), channel_id=1, source_target_pairs={{0,4},{2,6},{4,0},{6,2},{8,12},{10,14},{12,8},{14,10},{16,20},{18,... | collective-permute-start | bytes 786440 | tf_op jit(solution)/shard_map/ppermute | solution.py:204
  52.2 7.2 %collective-permute-start.23 = (bf16[256,1024]{1,0:T(8,128)(2,1)S(1)}, bf16[256,1024]{1,0:T(8,128)(2,1)S(1)}, u32[]{:S(2)}, u32[]{:S(2)}) collective-permute-start(bf16[256,1024]{1,0:T(8,128)(2,1)S(1)} %get-tuple-element.66.refs_16_), channel_id=1, source_target_pairs={{0,1},{1,0},{2,3},{3,2},{4,5},{5,4},{6,7},{7,6},{8,9},{9,8},{10,11... | collective-permute-start | bytes 1572872 | tf_op jit(solution)/shard_map/ppermute | solution.py:213
  55.8 11.7 %collective-permute-start.27 = (bf16[256,1024]{1,0:T(8,128)(2,1)S(1)}, bf16[256,1024]{1,0:T(8,128)(2,1)S(1)}, u32[]{:S(2)}, u32[]{:S(2)}) collective-permute-start(bf16[256,1024]{1,0:T(8,128)(2,1)S(1)} %shard_map.64), channel_id=1, source_target_pairs={{0,4},{2,6},{4,0},{6,2},{8,12},{10,14},{12,8},{14,10},{16,20},{18,... | collective-permute-start | bytes 1572872 | tf_op jit(solution)/shard_map/ppermute | solution.py:204
  57.9 11.3 %collective-permute-start.25 = (bf16[256,1024]{1,0:T(8,128)(2,1)S(1)}, bf16[256,1024]{1,0:T(8,128)(2,1)S(1)}, u32[]{:S(2)}, u32[]{:S(2)}) collective-permute-start(bf16[256,1024]{1,0:T(8,128)(2,1)S(1)} %shard_map.63), channel_id=1, source_target_pairs={{0,2},{2,0},{4,6},{6,4},{8,10},{10,8},{12,14},{14,12},{16,18},{18,... | collective-permute-start | bytes 1572872 | tf_op jit(solution)/shard_map/ppermute | solution.py:204
  (11 other events, 145.3 us)

commit v6 on v5

--- a/solution.py
+++ b/solution.py
@@ -288,14 +288,14 @@
         flops=2 * rows * feats * HD,
     )(*normed_args)
     to_x = tied(to_x, "send")
-    got_x, got_y = partner(to_x, 1), partner(to_y, 2)
+    other = swap(normed)
+    got_y, got_x = partner(to_y, 2), partner(to_x, 1)
     got_x = tied(got_x, "got_x")
     got_y = tied(got_y, "got_y")
     wa, wb = [], []
     for r in range(4):
         wa += [piece("a%d" % r), piece("y%d" % r)]
         wb += [piece("b%d" % r), piece("x%d" % r)]
-    other = swap(normed)
     parts = []
     for flip, pieces, got in ((2, wa, got_x), (1, wb, got_y)):
         (part,) = call(

time: 70.5 us -> 70.5 us (level)
  no operation moved by 1% of the time
where the time goes in v6:
time: 70.5 us; the launch traced here: 70.1 us
  starting transfers between devices  36.8 us (52%)
  waiting for transfers between devices  22.8 us (32%)
  Pallas kernels  7.13 us (10%)
  local copies, waits for them, and re-layouts  3.17 us (4%)
    ppermute x18, starting transfers between devices, partner(): return lax.ppermute(value, 'seq', [(i, i ^ flip) for i in range(blocks)])  21.2 us
    ppermute x18, waiting for transfers between devices, partner(): return lax.ppermute(value, 'seq', [(i, i ^ flip) for i in range(blocks)])  20.5 us
    ppermute x5, starting transfers between devices, ring(): lax.ppermute(value, 'seq', [(i, (i + PLANE) % blocks) for i in range(bloc...  9.29 us
    ppermute x2, starting transfers between devices, up(): lax.ppermute(value, 'seq', [(i, i + by * PLANE) for i in range(blocks - b...  5.8 us
    unnamed x14, local copies, waits for them, and re-layouts  3.17 us
    ppermute x5, waiting for transfers between devices, ring(): lax.ppermute(value, 'seq', [(i, (i + PLANE) % blocks) for i in range(bloc...  2.29 us
    pallas_call x2, Pallas kernels, finish(): pl.pallas_call(functools.partial(finish_kernel, at), out_shape=shape(mine...  1.68 us
    pallas_call x2, Pallas kernels, per_device(): call(functools.partial(partner_kernel, flip), [shape((rows, half), BF16)]...  1.48 us
  transfers between devices with their start and end apart: 28, of which 15 were waited for; matrix products, arithmetic and copies ran while one was open for 0% of the time, Pallas kernels for 9%

profile of v6, /device:TPU:0, one launch (start us, length us, event | category | flops | bytes accessed | tf_op | source)
XLA Modules:
  0.0 70.1 jit_solution(14993005839283415271)
XLA Ops:
  0.0 3.0 %collective-permute-start.4 = (bf16[128,2048]{1,0:T(8,128)(2,1)}, bf16[128,2048]{1,0:T(8,128)(2,1)S(1)}, u32[]{:S(2)}, u32[]{:S(2)}) collective-permute-start(bf16[128,2048]{1,0:T(8,128)(2,1)} %block.1), channel_id=1, source_target_pairs={{0,8},{2,10},{4,12},{6,14},{8,16},{10,18},{12,20},{14,22},{16,24},... | collective-permute-start | bytes 1572872 | tf_op jit(solution)/shard_map/ppermute | solution.py:207
  4.2 1.6 %collective-permute-start.3 = (bf16[128,1024]{1,0:T(8,128)(2,1)S(1)}, bf16[128,1024]{1,0:T(8,128)(2,1)S(1)}, u32[]{:S(2)}, u32[]{:S(2)}) collective-permute-start(bf16[128,1024]{1,0:T(8,128)(2,1)S(1)} %get-tuple-element.37.refs_0_), channel_id=1, source_target_pairs={{0,4},{2,6},{4,0},{6,2},{8,12},{10,14},{12,8},{14,10},{16,20},{18,... | collective-permute-start | bytes 786440 | tf_op jit(solution)/shard_map/ppermute | solution.py:204
  8.4 1.5 %collective-permute-start = (bf16[2,128,128]{2,1,0:T(8,128)(2,1)S(1)}, bf16[2,128,128]{2,1,0:T(8,128)(2,1)S(1)}, u32[]{:S(2)}, u32[]{:S(2)}) collective-permute-start(bf16[2,128,128]{2,1,0:T(8,128)(2,1)S(1)} %get-tuple-element.39), channel_id=1, source_target_pairs={{0,2},{2,0},{4,6},{6,4},{8,10},{10,8},{12,14},{14,12},{16,18},{18,... | collective-permute-start | bytes 196616 | tf_op jit(solution)/shard_map/ppermute | solution.py:204
  10.5 1.5 %collective-permute-start.2 = (bf16[2,128,128]{2,1,0:T(8,128)(2,1)S(1)}, bf16[2,128,128]{2,1,0:T(8,128)(2,1)S(1)}, u32[]{:S(2)}, u32[]{:S(2)}) collective-permute-start(bf16[2,128,128]{2,1,0:T(8,128)(2,1)S(1)} %get-tuple-element.41), channel_id=1, source_target_pairs={{0,6},{2,4},{4,2},{6,0},{8,14},{10,12},{12,10},{14,8},{16,22},{18,... | collective-permute-start | bytes 196616 | tf_op jit(solution)/shard_map/ppermute | solution.py:204
  12.8 1.4 %collective-permute-done.1.a2.refs_2_ = bf16[2,128,128]{2,1,0:T(8,128)(2,1)S(1)} collective-permute-done((bf16[2,128,128]{2,1,0:T(8,128)(2,1)S(1)}, bf16[2,128,128]{2,1,0:T(8,128)(2,1)S(1)}, u32[]{:S(2)}, u32[]{:S(2)}) %collective-permute-start.1) | collective-permute-done | bytes 65568 | tf_op jit(solution)/shard_map/ppermute | solution.py:204
  14.2 1.4 %collective-permute-done.2.a3.refs_3_ = bf16[2,128,128]{2,1,0:T(8,128)(2,1)S(1)} collective-permute-done((bf16[2,128,128]{2,1,0:T(8,128)(2,1)S(1)}, bf16[2,128,128]{2,1,0:T(8,128)(2,1)S(1)}, u32[]{:S(2)}, u32[]{:S(2)}) %collective-permute-start.2) | collective-permute-done | bytes 65568 | tf_op jit(solution)/shard_map/ppermute | solution.py:204
  15.7 3.5 %collective-permute-start.5 = (bf16[2,128,128]{2,1,0:T(8,128)(2,1)S(1)}, bf16[2,128,128]{2,1,0:T(8,128)(2,1)S(1)}, u32[]{:S(2)}, u32[]{:S(2)}) collective-permute-start(bf16[2,128,128]{2,1,0:T(8,128)(2,1)S(1)} %shard_map.57), channel_id=1, source_target_pairs={{0,8},{2,10},{4,12},{6,14},{8,16},{10,18},{12,20},{14,22},{16,24},... | collective-permute-start | bytes 196616 | tf_op jit(solution)/shard_map/ppermute | solution.py:210
  20.0 1.6 %collective-permute-start.7 = (bf16[128,1024]{1,0:T(8,128)(2,1)S(1)}, bf16[128,1024]{1,0:T(8,128)(2,1)S(1)}, u32[]{:S(2)}, u32[]{:S(2)}) collective-permute-start(bf16[128,1024]{1,0:T(8,128)(2,1)S(1)} %get-tuple-element.43.refs_2_), channel_id=1, source_target_pairs={{0,8},{2,10},{4,12},{6,14},{8,16},{10,18},{12,20},{14,22},{16,24},... | collective-permute-start | bytes 786440 | tf_op jit(solution)/shard_map/ppermute | solution.py:207
  21.6 1.5 %collective-permute-start.10 = (bf16[128,1024]{1,0:T(8,128)(2,1)S(1)}, bf16[128,1024]{1,0:T(8,128)(2,1)S(1)}, u32[]{:S(2)}, u32[]{:S(2)}) collective-permute-start(bf16[128,1024]{1,0:T(8,128)(2,1)S(1)} %get-tuple-element.43.refs_2_), channel_id=1, source_target_pairs={{0,4},{2,6},{4,0},{6,2},{8,12},{10,14},{12,8},{14,10},{16,20},{18,... | collective-permute-start | bytes 786440 | tf_op jit(solution)/shard_map/ppermute | solution.py:204
  23.1 1.4 %collective-permute-start.12 = (bf16[128,1024]{1,0:T(8,128)(2,1)S(1)}, bf16[128,1024]{1,0:T(8,128)(2,1)S(1)}, u32[]{:S(2)}, u32[]{:S(2)}) collective-permute-start(bf16[128,1024]{1,0:T(8,128)(2,1)S(1)} %get-tuple-element.54.refs_10_.refs_2_), channel_id=1, source_target_pairs={{0,2},{2,0},{4,6},{6,4},{8,10},{10,8},{12,14},{14,12},{16,18},{18,... | collective-permute-start | bytes 786440 | tf_op jit(solution)/shard_map/ppermute | solution.py:204
  24.5 2.3 %collective-permute-start.6 = (bf16[2,128,128]{2,1,0:T(8,128)(2,1)S(1)}, bf16[2,128,128]{2,1,0:T(8,128)(2,1)S(1)}, u32[]{:S(2)}, u32[]{:S(2)}) collective-permute-start(bf16[2,128,128]{2,1,0:T(8,128)(2,1)S(1)} %add_convert_fusion), channel_id=1, source_target_pairs={{0,16},{2,18},{4,20},{6,22},{8,24},{10,26},{12,28},{14,30},{1,17},... | collective-permute-start | bytes 196616 | tf_op jit(solution)/shard_map/ppermute | solution.py:210
  26.9 1.3 %collective-permute-done.8.refs_9_.refs_1_ = bf16[128,1024]{1,0:T(8,128)(2,1)S(1)} collective-permute-done((bf16[128,1024]{1,0:T(8,128)(2,1)S(1)}, bf16[128,1024]{1,0:T(8,128)(2,1)S(1)}, u32[]{:S(2)}, u32[]{:S(2)}) %collective-permute-start.8) | collective-permute-done | bytes 262176 | tf_op jit(solution)/shard_map/ppermute | solution.py:204
  29.4 2.7 %collective-permute-start.16 = (bf16[128,1024]{1,0:T(8,128)(2,1)S(1)}, bf16[128,1024]{1,0:T(8,128)(2,1)S(1)}, u32[]{:S(2)}, u32[]{:S(2)}) collective-permute-start(bf16[128,1024]{1,0:T(8,128)(2,1)S(1)} %collective-permute-done.7.refs_4_), channel_id=1, source_target_pairs={{0,8},{2,10},{4,12},{6,14},{8,16},{10,18},{12,20},{14,22},{16,24},... | collective-permute-start | bytes 786440 | tf_op jit(solution)/shard_map/ppermute | solution.py:207
  33.1 1.6 %collective-permute-start.13 = (bf16[2,128,128]{2,1,0:T(8,128)(2,1)S(1)}, bf16[2,128,128]{2,1,0:T(8,128)(2,1)S(1)}, u32[]{:S(2)}, u32[]{:S(2)}) collective-permute-start(bf16[2,128,128]{2,1,0:T(8,128)(2,1)S(1)} %get-tuple-element.55), channel_id=1, source_target_pairs={{0,2},{2,0},{4,6},{6,4},{8,10},{10,8},{12,14},{14,12},{16,18},{18,... | collective-permute-start | bytes 196616 | tf_op jit(solution)/shard_map/ppermute | solution.py:204
  42.4 1.2 %collective-permute-start.15 = (bf16[256,512]{1,0:T(8,128)(2,1)S(1)}, bf16[256,512]{1,0:T(8,128)(2,1)S(1)}, u32[]{:S(2)}, u32[]{:S(2)}) collective-permute-start(bf16[256,512]{1,0:T(8,128)(2,1)S(1)} %get-tuple-element.58), channel_id=1, source_target_pairs={{0,2},{2,0},{4,6},{6,4},{8,10},{10,8},{12,14},{14,12},{16,18},{18,... | collective-permute-start | bytes 786440 | tf_op jit(solution)/shard_map/ppermute | solution.py:204
  44.6 1.3 %collective-permute-done.21.refs_14_.refs_6_ = bf16[128,1024]{1,0:T(8,128)(2,1)S(1)} collective-permute-done((bf16[128,1024]{1,0:T(8,128)(2,1)S(1)}, bf16[128,1024]{1,0:T(8,128)(2,1)S(1)}, u32[]{:S(2)}, u32[]{:S(2)}) %collective-permute-start.21) | collective-permute-done | bytes 262176 | tf_op jit(solution)/shard_map/ppermute | solution.py:207
  47.5 1.9 %collective-permute-done.18.refs_13_.refs_5_ = bf16[128,1024]{1,0:T(8,128)(2,1)S(1)} collective-permute-done((bf16[128,1024]{1,0:T(8,128)(2,1)S(1)}, bf16[128,1024]{1,0:T(8,128)(2,1)S(1)}, u32[]{:S(2)}, u32[]{:S(2)}) %collective-permute-start.18) | collective-permute-done | bytes 262176 | tf_op jit(solution)/shard_map/ppermute | solution.py:204
  49.4 1.3 %collective-permute-start.11 = (bf16[128,1024]{1,0:T(8,128)(2,1)S(1)}, bf16[128,1024]{1,0:T(8,128)(2,1)S(1)}, u32[]{:S(2)}, u32[]{:S(2)}) collective-permute-start(bf16[128,1024]{1,0:T(8,128)(2,1)S(1)} %collective-permute-done.7.refs_4_), channel_id=1, source_target_pairs={{0,4},{2,6},{4,0},{6,2},{8,12},{10,14},{12,8},{14,10},{16,20},{18,... | collective-permute-start | bytes 786440 | tf_op jit(solution)/shard_map/ppermute | solution.py:204
  50.7 1.5 %collective-permute-done.15.refs_8_ = bf16[256,512]{1,0:T(8,128)(2,1)S(1)} collective-permute-done((bf16[256,512]{1,0:T(8,128)(2,1)S(1)}, bf16[256,512]{1,0:T(8,128)(2,1)S(1)}, u32[]{:S(2)}, u32[]{:S(2)}) %collective-permute-start.15) | collective-permute-done | bytes 262176 | tf_op jit(solution)/shard_map/ppermute | solution.py:204
  52.7 2.3 %collective-permute-done.22.refs_15_.refs_7_ = bf16[128,1024]{1,0:T(8,128)(2,1)S(1)} collective-permute-done((bf16[128,1024]{1,0:T(8,128)(2,1)S(1)}, bf16[128,1024]{1,0:T(8,128)(2,1)S(1)}, u32[]{:S(2)}, u32[]{:S(2)}) %collective-permute-start.22) | collective-permute-done | bytes 262176 | tf_op jit(solution)/shard_map/ppermute | solution.py:204
  55.8 1.4 %collective-permute-start.27 = (bf16[256,1024]{1,0:T(8,128)(2,1)S(1)}, bf16[256,1024]{1,0:T(8,128)(2,1)S(1)}, u32[]{:S(2)}, u32[]{:S(2)}) collective-permute-start(bf16[256,1024]{1,0:T(8,128)(2,1)S(1)} %shard_map.64), channel_id=1, source_target_pairs={{0,4},{2,6},{4,0},{6,2},{8,12},{10,14},{12,8},{14,10},{16,20},{18,... | collective-permute-start | bytes 1572872 | tf_op jit(solution)/shard_map/ppermute | solution.py:204
  57.9 1.4 %collective-permute-start.25 = (bf16[256,1024]{1,0:T(8,128)(2,1)S(1)}, bf16[256,1024]{1,0:T(8,128)(2,1)S(1)}, u32[]{:S(2)}, u32[]{:S(2)}) collective-permute-start(bf16[256,1024]{1,0:T(8,128)(2,1)S(1)} %shard_map.63), channel_id=1, source_target_pairs={{0,2},{2,0},{4,6},{6,4},{8,10},{10,8},{12,14},{14,12},{16,18},{18,... | collective-permute-start | bytes 1572872 | tf_op jit(solution)/shard_map/ppermute | solution.py:204
  59.4 1.3 %shard_map.62.mine = f32[256,2048]{1,0:T(8,128)S(1)} custom-call(bf16[128,1024]{1,0:T(8,128)(2,1)S(1)} %get-tuple-element.37.refs_0_, bf16[128,1024]{1,0:T(8,128)(2,1)S(1)} %collective-permute-done.3.refs_1_, bf16[128,1024]{1,0:T(8,128)(2,1)S(1)} %get-tuple-element.43.refs_2_, bf16[128,1024]{1,0:T(8,128)(2,1)S(1)} %collective-permute-done.10.refs_3_, ...), custom_call_target="tpu_custom_call" | custom-call | flops 1073741824 | tf_op jit(solution)/shard_map/pallas_call | solution.py:309
  60.7 6.8 %collective-permute-done.27.part = bf16[256,1024]{1,0:T(8,128)(2,1)S(1)} collective-permute-done((bf16[256,1024]{1,0:T(8,128)(2,1)S(1)}, bf16[256,1024]{1,0:T(8,128)(2,1)S(1)}, u32[]{:S(2)}, u32[]{:S(2)}) %collective-permute-start.27) | collective-permute-done | bytes 524320 | tf_op jit(solution)/shard_map/ppermute | solution.py:204
  (59 shorter events, 23.0 us)
Async XLA Ops:
  0.0 19.9 %collective-permute-start.4 = (bf16[128,2048]{1,0:T(8,128)(2,1)}, bf16[128,2048]{1,0:T(8,128)(2,1)S(1)}, u32[]{:S(2)}, u32[]{:S(2)}) collective-permute-start(bf16[128,2048]{1,0:T(8,128)(2,1)} %block.1), channel_id=1, source_target_pairs={{0,8},{2,10},{4,12},{6,14},{8,16},{10,18},{12,20},{14,22},{16,24},... | collective-permute-start | bytes 1572872 | tf_op jit(solution)/shard_map/ppermute | solution.py:207
  4.2 11.5 %collective-permute-start.3 = (bf16[128,1024]{1,0:T(8,128)(2,1)S(1)}, bf16[128,1024]{1,0:T(8,128)(2,1)S(1)}, u32[]{:S(2)}, u32[]{:S(2)}) collective-permute-start(bf16[128,1024]{1,0:T(8,128)(2,1)S(1)} %get-tuple-element.37.refs_0_), channel_id=1, source_target_pairs={{0,4},{2,6},{4,0},{6,2},{8,12},{10,14},{12,8},{14,10},{16,20},{18,... | collective-permute-start | bytes 786440 | tf_op jit(solution)/shard_map/ppermute | solution.py:204
  10.5 5.2 %collective-permute-start.2 = (bf16[2,128,128]{2,1,0:T(8,128)(2,1)S(1)}, bf16[2,128,128]{2,1,0:T(8,128)(2,1)S(1)}, u32[]{:S(2)}, u32[]{:S(2)}) collective-permute-start(bf16[2,128,128]{2,1,0:T(8,128)(2,1)S(1)} %get-tuple-element.41), channel_id=1, source_target_pairs={{0,6},{2,4},{4,2},{6,0},{8,14},{10,12},{12,10},{14,8},{16,22},{18,... | collective-permute-start | bytes 196616 | tf_op jit(solution)/shard_map/ppermute | solution.py:204
  15.7 8.8 %collective-permute-start.5 = (bf16[2,128,128]{2,1,0:T(8,128)(2,1)S(1)}, bf16[2,128,128]{2,1,0:T(8,128)(2,1)S(1)}, u32[]{:S(2)}, u32[]{:S(2)}) collective-permute-start(bf16[2,128,128]{2,1,0:T(8,128)(2,1)S(1)} %shard_map.57), channel_id=1, source_target_pairs={{0,8},{2,10},{4,12},{6,14},{8,16},{10,18},{12,20},{14,22},{16,24},... | collective-permute-start | bytes 196616 | tf_op jit(solution)/shard_map/ppermute | solution.py:210
  19.2 9.0 %collective-permute-start.8 = (bf16[128,1024]{1,0:T(8,128)(2,1)S(1)}, bf16[128,1024]{1,0:T(8,128)(2,1)S(1)}, u32[]{:S(2)}, u32[]{:S(2)}) collective-permute-start(bf16[128,1024]{1,0:T(8,128)(2,1)S(1)} %get-tuple-element.45.refs_8_.refs_0_), channel_id=1, source_target_pairs={{0,2},{2,0},{4,6},{6,4},{8,10},{10,8},{12,14},{14,12},{16,18},{18,... | collective-permute-start | bytes 786440 | tf_op jit(solution)/shard_map/ppermute | solution.py:204
  20.0 9.4 %collective-permute-start.7 = (bf16[128,1024]{1,0:T(8,128)(2,1)S(1)}, bf16[128,1024]{1,0:T(8,128)(2,1)S(1)}, u32[]{:S(2)}, u32[]{:S(2)}) collective-permute-start(bf16[128,1024]{1,0:T(8,128)(2,1)S(1)} %get-tuple-element.43.refs_2_), channel_id=1, source_target_pairs={{0,8},{2,10},{4,12},{6,14},{8,16},{10,18},{12,20},{14,22},{16,24},... | collective-permute-start | bytes 786440 | tf_op jit(solution)/shard_map/ppermute | solution.py:207
  21.6 13.1 %collective-permute-start.10 = (bf16[128,1024]{1,0:T(8,128)(2,1)S(1)}, bf16[128,1024]{1,0:T(8,128)(2,1)S(1)}, u32[]{:S(2)}, u32[]{:S(2)}) collective-permute-start(bf16[128,1024]{1,0:T(8,128)(2,1)S(1)} %get-tuple-element.43.refs_2_), channel_id=1, source_target_pairs={{0,4},{2,6},{4,0},{6,2},{8,12},{10,14},{12,8},{14,10},{16,20},{18,... | collective-permute-start | bytes 786440 | tf_op jit(solution)/shard_map/ppermute | solution.py:204
  23.1 10.0 %collective-permute-start.12 = (bf16[128,1024]{1,0:T(8,128)(2,1)S(1)}, bf16[128,1024]{1,0:T(8,128)(2,1)S(1)}, u32[]{:S(2)}, u32[]{:S(2)}) collective-permute-start(bf16[128,1024]{1,0:T(8,128)(2,1)S(1)} %get-tuple-element.54.refs_10_.refs_2_), channel_id=1, source_target_pairs={{0,2},{2,0},{4,6},{6,4},{8,10},{10,8},{12,14},{14,12},{16,18},{18,... | collective-permute-start | bytes 786440 | tf_op jit(solution)/shard_map/ppermute | solution.py:204
  28.2 9.6 %collective-permute-start.17 = (bf16[128,1024]{1,0:T(8,128)(2,1)S(1)}, bf16[128,1024]{1,0:T(8,128)(2,1)S(1)}, u32[]{:S(2)}, u32[]{:S(2)}) collective-permute-start(bf16[128,1024]{1,0:T(8,128)(2,1)S(1)} %get-tuple-element.54.refs_10_.refs_2_), channel_id=1, source_target_pairs={{0,8},{2,10},{4,12},{6,14},{8,16},{10,18},{12,20},{14,22},{16,24},... | collective-permute-start | bytes 786440 | tf_op jit(solution)/shard_map/ppermute | solution.py:207
  29.4 14.3 %collective-permute-start.16 = (bf16[128,1024]{1,0:T(8,128)(2,1)S(1)}, bf16[128,1024]{1,0:T(8,128)(2,1)S(1)}, u32[]{:S(2)}, u32[]{:S(2)}) collective-permute-start(bf16[128,1024]{1,0:T(8,128)(2,1)S(1)} %collective-permute-done.7.refs_4_), channel_id=1, source_target_pairs={{0,8},{2,10},{4,12},{6,14},{8,16},{10,18},{12,20},{14,22},{16,24},... | collective-permute-start | bytes 786440 | tf_op jit(solution)/shard_map/ppermute | solution.py:207
  32.3 6.3 %collective-permute-start.9 = (bf16[2,128,128]{2,1,0:T(8,128)(2,1)S(1)}, bf16[2,128,128]{2,1,0:T(8,128)(2,1)S(1)}, u32[]{:S(2)}, u32[]{:S(2)}) collective-permute-start(bf16[2,128,128]{2,1,0:T(8,128)(2,1)S(1)} %get-tuple-element.47), channel_id=1, source_target_pairs={{0,6},{2,4},{4,2},{6,0},{8,14},{10,12},{12,10},{14,8},{16,22},{18,... | collective-permute-start | bytes 196616 | tf_op jit(solution)/shard_map/ppermute | solution.py:204
  33.1 5.6 %collective-permute-start.13 = (bf16[2,128,128]{2,1,0:T(8,128)(2,1)S(1)}, bf16[2,128,128]{2,1,0:T(8,128)(2,1)S(1)}, u32[]{:S(2)}, u32[]{:S(2)}) collective-permute-start(bf16[2,128,128]{2,1,0:T(8,128)(2,1)S(1)} %get-tuple-element.55), channel_id=1, source_target_pairs={{0,2},{2,0},{4,6},{6,4},{8,10},{10,8},{12,14},{14,12},{16,18},{18,... | collective-permute-start | bytes 196616 | tf_op jit(solution)/shard_map/ppermute | solution.py:204
  34.7 5.0 %collective-permute-start.14 = (bf16[2,128,128]{2,1,0:T(8,128)(2,1)S(1)}, bf16[2,128,128]{2,1,0:T(8,128)(2,1)S(1)}, u32[]{:S(2)}, u32[]{:S(2)}) collective-permute-start(bf16[2,128,128]{2,1,0:T(8,128)(2,1)S(1)} %get-tuple-element.56), channel_id=1, source_target_pairs={{0,4},{2,6},{4,0},{6,2},{8,12},{10,14},{12,8},{14,10},{16,20},{18,... | collective-permute-start | bytes 196616 | tf_op jit(solution)/shard_map/ppermute | solution.py:204
  37.8 8.2 %collective-permute-start.21 = (bf16[128,1024]{1,0:T(8,128)(2,1)S(1)}, bf16[128,1024]{1,0:T(8,128)(2,1)S(1)}, u32[]{:S(2)}, u32[]{:S(2)}) collective-permute-start(bf16[128,1024]{1,0:T(8,128)(2,1)S(1)} %collective-permute-done.17.refs_12_.refs_4_), channel_id=1, source_target_pairs={{0,8},{2,10},{4,12},{6,14},{8,16},{10,18},{12,20},{14,22},{16,24},... | collective-permute-start | bytes 786440 | tf_op jit(solution)/shard_map/ppermute | solution.py:207
  40.5 6.4 %collective-permute-start.20 = (bf16[256,512]{1,0:T(8,128)(2,1)S(1)}, bf16[256,512]{1,0:T(8,128)(2,1)S(1)}, u32[]{:S(2)}, u32[]{:S(2)}) collective-permute-start(bf16[256,512]{1,0:T(8,128)(2,1)S(1)} %get-tuple-element.64), channel_id=1, source_target_pairs={{0,4},{2,6},{4,0},{6,2},{8,12},{10,14},{12,8},{14,10},{16,20},{18,... | collective-permute-start | bytes 786440 | tf_op jit(solution)/shard_map/ppermute | solution.py:204
  41.6 7.8 %collective-permute-start.18 = (bf16[128,1024]{1,0:T(8,128)(2,1)S(1)}, bf16[128,1024]{1,0:T(8,128)(2,1)S(1)}, u32[]{:S(2)}, u32[]{:S(2)}) collective-permute-start(bf16[128,1024]{1,0:T(8,128)(2,1)S(1)} %collective-permute-done.17.refs_12_.refs_4_), channel_id=1, source_target_pairs={{0,2},{2,0},{4,6},{6,4},{8,10},{10,8},{12,14},{14,12},{16,18},{18,... | collective-permute-start | bytes 786440 | tf_op jit(solution)/shard_map/ppermute | solution.py:204
  42.4 9.8 %collective-permute-start.15 = (bf16[256,512]{1,0:T(8,128)(2,1)S(1)}, bf16[256,512]{1,0:T(8,128)(2,1)S(1)}, u32[]{:S(2)}, u32[]{:S(2)}) collective-permute-start(bf16[256,512]{1,0:T(8,128)(2,1)S(1)} %get-tuple-element.58), channel_id=1, source_target_pairs={{0,2},{2,0},{4,6},{6,4},{8,10},{10,8},{12,14},{14,12},{16,18},{18,... | collective-permute-start | bytes 786440 | tf_op jit(solution)/shard_map/ppermute | solution.py:204
  43.7 8.6 %collective-permute-start.19 = (bf16[128,1024]{1,0:T(8,128)(2,1)S(1)}, bf16[128,1024]{1,0:T(8,128)(2,1)S(1)}, u32[]{:S(2)}, u32[]{:S(2)}) collective-permute-start(bf16[128,1024]{1,0:T(8,128)(2,1)S(1)} %collective-permute-done.16.refs_6_), channel_id=1, source_target_pairs={{0,4},{2,6},{4,0},{6,2},{8,12},{10,14},{12,8},{14,10},{16,20},{18,... | collective-permute-start | bytes 786440 | tf_op jit(solution)/shard_map/ppermute | solution.py:204
  46.9 8.1 %collective-permute-start.22 = (bf16[128,1024]{1,0:T(8,128)(2,1)S(1)}, bf16[128,1024]{1,0:T(8,128)(2,1)S(1)}, u32[]{:S(2)}, u32[]{:S(2)}) collective-permute-start(bf16[128,1024]{1,0:T(8,128)(2,1)S(1)} %collective-permute-done.21.refs_14_.refs_6_), channel_id=1, source_target_pairs={{0,2},{2,0},{4,6},{6,4},{8,10},{10,8},{12,14},{14,12},{16,18},{18,... | collective-permute-start | bytes 786440 | tf_op jit(solution)/shard_map/ppermute | solution.py:204
  47.5 7.5 %collective-permute-start.26 = (bf16[256,512]{1,0:T(8,128)(2,1)S(1)}, bf16[256,512]{1,0:T(8,128)(2,1)S(1)}, u32[]{:S(2)}, u32[]{:S(2)}) collective-permute-start(bf16[256,512]{1,0:T(8,128)(2,1)S(1)} %collective-permute-done.20.refs_8_), channel_id=1, source_target_pairs={{0,1},{1,0},{2,3},{3,2},{4,5},{5,4},{6,7},{7,6},{8,9},{9,8},{10,11... | collective-permute-start | bytes 786440 | tf_op jit(solution)/shard_map/ppermute | solution.py:213
  49.4 7.8 %collective-permute-start.11 = (bf16[128,1024]{1,0:T(8,128)(2,1)S(1)}, bf16[128,1024]{1,0:T(8,128)(2,1)S(1)}, u32[]{:S(2)}, u32[]{:S(2)}) collective-permute-start(bf16[128,1024]{1,0:T(8,128)(2,1)S(1)} %collective-permute-done.7.refs_4_), channel_id=1, source_target_pairs={{0,4},{2,6},{4,0},{6,2},{8,12},{10,14},{12,8},{14,10},{16,20},{18,... | collective-permute-start | bytes 786440 | tf_op jit(solution)/shard_map/ppermute | solution.py:204
  52.2 7.2 %collective-permute-start.23 = (bf16[256,1024]{1,0:T(8,128)(2,1)S(1)}, bf16[256,1024]{1,0:T(8,128)(2,1)S(1)}, u32[]{:S(2)}, u32[]{:S(2)}) collective-permute-start(bf16[256,1024]{1,0:T(8,128)(2,1)S(1)} %get-tuple-element.66.refs_16_), channel_id=1, source_target_pairs={{0,1},{1,0},{2,3},{3,2},{4,5},{5,4},{6,7},{7,6},{8,9},{9,8},{10,11... | collective-permute-start | bytes 1572872 | tf_op jit(solution)/shard_map/ppermute | solution.py:213
  55.8 11.7 %collective-permute-start.27 = (bf16[256,1024]{1,0:T(8,128)(2,1)S(1)}, bf16[256,1024]{1,0:T(8,128)(2,1)S(1)}, u32[]{:S(2)}, u32[]{:S(2)}) collective-permute-start(bf16[256,1024]{1,0:T(8,128)(2,1)S(1)} %shard_map.64), channel_id=1, source_target_pairs={{0,4},{2,6},{4,0},{6,2},{8,12},{10,14},{12,8},{14,10},{16,20},{18,... | collective-permute-start | bytes 1572872 | tf_op jit(solution)/shard_map/ppermute | solution.py:204
  57.9 11.3 %collective-permute-start.25 = (bf16[256,1024]{1,0:T(8,128)(2,1)S(1)}, bf16[256,1024]{1,0:T(8,128)(2,1)S(1)}, u32[]{:S(2)}, u32[]{:S(2)}) collective-permute-start(bf16[256,1024]{1,0:T(8,128)(2,1)S(1)} %shard_map.63), channel_id=1, source_target_pairs={{0,2},{2,0},{4,6},{6,4},{8,10},{10,8},{12,14},{14,12},{16,18},{18,... | collective-permute-start | bytes 1572872 | tf_op jit(solution)/shard_map/ppermute | solution.py:204
  (11 other events, 145.3 us)
